TPU v7x, 32 devices: a whole 2x2x4 slice. The times are simulated.
32 devices in a mesh: grp: 2 (over y), ex: 4 (over z), lyr: 4 (over x, core).
Axes of the slice: x: 2, y: 2, z: 4, core: 2. Of those that a mesh axis runs over, the one named last changes fastest.
Arguments:
- train_grads: bfloat16 [4, 4096, 4096], P('lyr', ('grp', 'ex')), parts along dimension 1, may hold values from -6 to 6
- query_grads: bfloat16 [4, 128, 4096], P('lyr', 'ex'), may hold values from -6 to 6
- basis_out: float32 [4, 64, 64], P('lyr'), may hold values from -0.75 to 0.75
- basis_in: float32 [4, 64, 64], P('lyr'), may hold values from -0.75 to 0.75
- eigenvalues: float32 [4, 4096], P('lyr'), may hold values from 0.05 to 5
Outputs:
- scores: float32 [4096, 128], P(('grp', 'ex'), 'lyr'), parts along dimension 0
There are 2 independent parts, one for each index of `grp`. A program takes and returns all parts, laid end to end along the dimension named above; an argument that names none is the same for every part. Nothing has to cross between parts.
All inputs are finite; a program needn't handle non-finite values.
Results may differ from a plain program's by a relative error of at most 0.0029.
Values may be sent and summed in bfloat16 or wider, within the bound.
No kernel may reach another device: no remote copies, remote signals or barrier semaphores. Data moves between devices by JAX's collectives and lax.ppermute only.
A program may use at most 64 MiB of HBM per device.

v0:
```python
import math

import jax
import jax.numpy as jnp
from jax import lax
from jax.sharding import PartitionSpec as P

GR = 64
GC = 64


damping = 0.1


def prepare(grads, basis_out, basis_in, eigenvalues):
    layers, count, width = grads.shape
    rows_out = basis_out.shape[1]
    cols_in = basis_in.shape[1]
    matrix = grads.astype(jnp.float32).reshape(layers, count, rows_out, cols_in)
    rotated = jnp.einsum("lba,lqbc->lqac", basis_out, matrix, precision=lax.Precision.HIGHEST)
    rotated = jnp.einsum("lqac,lcd->lqad", rotated, basis_in, precision=lax.Precision.HIGHEST)
    scaled = rotated / (eigenvalues.reshape(layers, 1, rows_out, cols_in) + damping)
    back = jnp.einsum("lab,lqbc->lqac", basis_out, scaled, precision=lax.Precision.HIGHEST)
    back = jnp.einsum("lqac,ldc->lqad", back, basis_in, precision=lax.Precision.HIGHEST)
    return back.reshape(layers, count, width).astype(jnp.bfloat16)


def local(train_grads, query_grads, basis_out, basis_in, eigenvalues):
    own_ready = prepare(query_grads, basis_out, basis_in, eigenvalues)
    partial_scores = jnp.einsum(
        "lnf,lqf->nq",
        train_grads,
        lax.all_gather(own_ready, "ex", axis=1, tiled=True),
        preferred_element_type=jnp.float32,
    )
    summed = lax.psum_scatter(partial_scores, "lyr", scatter_dimension=1, tiled=True)
    return summed / math.sqrt(GR * GC)


def solution(mesh):
    return jax.shard_map(
        local,
        mesh=mesh,
        in_specs=(
            P("lyr", ("grp", "ex"), None),
            P("lyr", "ex", None),
            P("lyr", None, None),
            P("lyr", None, None),
            P("lyr", None),
        ),
        out_specs=P(("grp", "ex"), "lyr"),
        check_vma=False,
    )
```

profile of v0, /device:TPU:0, one launch (start us, length us, event | category | flops | bytes accessed | tf_op | source)
XLA Modules:
  0.0 79.0 jit_solution(3265886439719348564)
XLA Ops:
  6.5 0.0 copy-start
  6.5 0.0 copy-start.1
  6.5 0.0 all-gather.2.cloned.1.call-start
  6.5 0.8 add_reduce_fusion
  7.3 0.1 add.18
  7.4 0.1 copy.7
  7.5 1.5 %reshape.59 = bf16[32,64,64]{2,1,0:T(8,128)(2,1)S(1)} reshape(bf16[1,32,4096]{2,1,0:T(8,128)(2,1)} %param.6) | data formatting | bytes 524288 | tf_op jit(solution)/shard_map/reshape
  8.9 0.0 copy-done
  9.0 0.7 convolution_bitcast_fusion
  9.6 1.8 %convolution_divide_fusion = f32[32,64,64]{1,2,0:T(8,128)S(1)} fusion(f32[32,64,64]{1,2,0:T(8,128)S(1)} %convolution_bitcast_fusion, f32[64,64]{0,1:T(8,128)S(1)} %copy.7, f32[1,64,64]{2,1,0:T(8,128)} %param.8), kind=kOutput, calls=%fused_computation.4 | convolution fusion | flops 100794368 | bytes 1081344 | tf_op jit(solution)/shard_map/lqac,lcd->lqad/dot_general | solution.py:21
  11.4 1.0 %convolution_bitcast_fusion.1 = f32[32,64,64]{1,2,0:T(8,128)S(1)} fusion(f32[32,64,64]{1,2,0:T(8,128)S(1)} %convolution_divide_fusion, f32[1,64,64]{2,1,0:T(8,128)S(1)} %copy-done), kind=kOutput, calls=%fused_computation.3 | convolution fusion | flops 100663296 | bytes 1064960 | tf_op jit(solution)/shard_map/lab,lqbc->lqac/dot_general | solution.py:23
  12.4 0.0 copy-done.1
  12.4 1.8 %convolution_convert_fusion = bf16[32,64,64]{2,1,0:T(8,128)(2,1)S(1)} fusion(f32[32,64,64]{1,2,0:T(8,128)S(1)} %convolution_bitcast_fusion.1, f32[1,64,64]{2,1,0:T(8,128)S(1)} %copy-done.1), kind=kOutput, calls=%fused_computation.5 | convolution fusion | flops 100794368 | bytes 802816 | tf_op jit(solution)/shard_map/lqac,ldc->lqad/dot_general | solution.py:24
  14.2 1.2 %convert_element_type.16 = bf16[1,32,4096]{2,1,0:T(8,128)(2,1)} reshape(bf16[32,64,64]{2,1,0:T(8,128)(2,1)S(1)} %convolution_convert_fusion) | data formatting | bytes 524288 | tf_op jit(solution)/shard_map/convert_element_type | solution.py:25
  15.4 0.0 all-gather.2.cloned.1.call-update
  15.4 0.0 reduce-scatter.2.cloned.1.call-start
  15.5 30.7 %all-gather.2.cloned.1.call-done = bf16[1,128,4096]{2,1,0:T(8,128)(2,1)} async-done(((bf16[1,32,4096]{2,1,0:T(8,128)(2,1)}), bf16[1,128,4096]{2,1,0:T(8,128)(2,1)}) %all-gather.2.cloned.1.call-update) | async-done | bytes 1048592 | tf_op jit(solution)/shard_map/all_gather | solution.py:33
  46.2 4.7 %fusion.2 = f32[512,128]{0,1:T(8,128)} fusion(bf16[1,512,4096]{2,1,0:T(8,128)(2,1)} %param.5, bf16[1,128,4096]{2,1,0:T(8,128)(2,1)} %all-gather.2.cloned.1.call-done), kind=kOutput, calls=%fused_computation.6 | convolution fusion | flops 536870912 | bytes 5505024 | tf_op jit(solution)/shard_map/lnf,lqf->nq/dot_general | solution.py:30
  51.0 0.0 reduce-scatter.2.cloned.1.call-update
  51.0 19.7 %reduce-scatter.2.cloned.1.call-done = f32[512,32]{0,1:T(8,128)} async-done(((f32[512,128]{0,1:T(8,128)}), f32[512,32]{0,1:T(8,128)}) %reduce-scatter.2.cloned.1.call-update) | async-done | bytes 65552 | tf_op jit(solution)/shard_map/reduce_scatter | solution.py:36
  70.7 1.5 %broadcast_multiply_fusion = f32[512,32]{0,1:T(8,128)} fusion(f32[512,32]{0,1:T(8,128)} %reduce-scatter.2.cloned.1.call-done), kind=kLoop, calls=%fused_computation.12 | loop fusion | flops 16384 | bytes 131072 | tf_op jit(solution)/shard_map/div | solution.py:37
Async XLA Ops:
  6.5 2.4 %copy-start = (f32[1,64,64]{2,1,0:T(8,128)S(1)}, f32[1,64,64]{2,1,0:T(8,128)}, u32[]{:S(2)}) copy-start(f32[1,64,64]{2,1,0:T(8,128)} %param.7) | copy-start | bytes 49156
  6.5 5.9 %copy-start.1 = (f32[1,64,64]{2,1,0:T(8,128)S(1)}, f32[1,64,64]{2,1,0:T(8,128)}, u32[]{:S(2)}) copy-start(f32[1,64,64]{2,1,0:T(8,128)} %param.8) | copy-start | bytes 49156
  6.5 39.7 %all-gather.2.cloned.1.call-start = ((), (), s32[]{:S(2)}) async-start(), calls=%async_computation.1 | async-start | bytes 1310720 | tf_op jit(solution)/shard_map/all_gather | solution.py:33
  15.4 55.3 %reduce-scatter.2.cloned.1.call-start = ((), (), s32[]{:S(2)}) async-start(), calls=%async_computation.2 | async-start | bytes 327680 | tf_op jit(solution)/shard_map/reduce_scatter | solution.py:36
Sparse Core Ops, SparseCore 0:
  15.6 30.6 all-gather.1
  51.1 19.5 reduce-scatter.1
where the time goes:
time: 79.3 us; the launch traced here: 79 us
  waiting for transfers between devices  50.5 us (64%)
  between operations  13.5 us (17%)
  matrix products  10 us (13%)
  local copies, waits for them, and re-layouts  2.81 us (4%)
  other arithmetic  2.25 us (3%)
    all_gather x1, waiting for transfers between devices, local(): lax.all_gather(own_ready, 'ex', axis=1, tiled=True)  30.7 us
    reduce_scatter x1, waiting for transfers between devices, local(): lax.psum_scatter(partial_scores, 'lyr', scatter_dimension=1, tiled=True)  19.7 us
    dot_general x1, matrix products, local(): jnp.einsum('lnf,lqf->nq', train_grads, lax.all_gather(own_ready, 'ex', ax...  4.75 us
    dot_general x1, matrix products, prepare(): jnp.einsum('lqac,lcd->lqad', rotated, basis_in, precision=lax.Precision.H...  1.81 us
    dot_general x1, matrix products, prepare(): jnp.einsum('lqac,ldc->lqad', back, basis_in, precision=lax.Precision.HIGH...  1.8 us
  transfers between devices with their start and end apart: 2, of which 2 were waited for; matrix products, arithmetic and copies ran while one was open for 0% of the time, Pallas kernels for 0%

commit v1 on v0

v1 whole, which is shorter than its diff:
```python
import functools
import math

import jax, jax.numpy as jnp
from jax import lax
from jax.experimental import pallas as pl
from jax.experimental.pallas import tpu as pltpu
from jax.sharding import PartitionSpec as P

GR = 64
GC = 64
damping = 0.1
F32, BF16 = jnp.float32, jnp.bfloat16


def dot(a, b, ca=1, cb=0):
    return lax.dot_general(a, b, (((ca,), (cb,)), ((), ())), preferred_element_type=F32)
def split(x):
    h = x.astype(BF16)
    return h, (x - h.astype(F32)).astype(BF16)
def selector(rows, which, swap):
    k = lax.broadcasted_iota(jnp.int32, (rows, 64), 0)
    b = lax.broadcasted_iota(jnp.int32, (rows, 64), 1)
    kk = k % 64
    par = kk // 32
    if swap: par = 1 - par
    hit = b == 2 * (kk % 32) + par
    if which == 1: hit = hit & (k < 128)
    if which == 2: hit = hit & (k >= 128)
    return jnp.where(hit, 1.0, 0.0).astype(BF16)
def row_maps(bo):
    h, l = split(bo)
    sel = selector(64, 0, False)
    outs = []
    for cb in (1, 0):
        th, tl = dot(sel, h, 1, cb).astype(BF16), dot(sel, l, 1, cb).astype(BF16)
        parts = []
        for swap in (False, True):
            full = dot(th, selector(192, 1, swap), 1, 1) + dot(tl, selector(192, 2, swap), 1, 1)
            parts.append(full[32 * swap:32 * swap + 32])
        outs.append(jnp.concatenate(parts, 0).astype(BF16))
    return outs
def col_maps(bi):
    h, l = split(bi)
    r = lax.broadcasted_iota(jnp.int32, (128, 64), 0) % 64
    c = lax.broadcasted_iota(jnp.int32, (128, 64), 1)
    e = jnp.where(r == c, 1.0, 0.0).astype(BF16)
    i = lax.broadcasted_iota(jnp.int32, (128, 128), 0) // 64
    j = lax.broadcasted_iota(jnp.int32, (128, 128), 1) // 64
    same = i == j
    def tile(x, cb):
        t = dot(e, x, 1, cb).astype(BF16)
        return dot(t, e, 1, 1)
    def pick(t, m): return jnp.where(m, t, 0.0).astype(BF16)
    th, tl = tile(h, 0), tile(l, 0)
    diff = jnp.logical_not(same)
    first = jnp.concatenate([jnp.concatenate([pick(th, same), pick(th, diff)], 1), jnp.concatenate([pick(tl, same), pick(tl, diff)], 1)], 0)
    uh, ul = tile(h, 1), tile(l, 1)
    last = jnp.concatenate([pick(uh, same), pick(uh, same), pick(ul, same)], 0)
    return first, last
def prep_body(nq, get, put, left_in, left_out, first, last, rec, xa, xb, os, group=8):
    g = jnp.concatenate([get(t) for t in range(32)], 0)
    x = dot(jnp.concatenate([g, g], 1), first)
    xa[...] = x[:, :128]
    xb[...] = x[:, 128:]
    lane = lax.broadcasted_iota(jnp.int32, (32, 128), 1) < 64
    for q0 in range(0, nq, group):
        qs = range(q0, q0 + group)
        ww = jnp.concatenate([jnp.concatenate([r[pl.ds(q, 32, stride=nq), :] for q in qs], 1) for r in (xa, xb)], 0)
        h, l = split(ww)
        r = dot(left_in, jnp.concatenate([h, l, h], 0))
        ys, yr = [], []
        for i in range(group):
            s = slice(i * 128, i * 128 + 128)
            y = jnp.where(lane, r[:32, s], r[32:, s]) * rec
            ys.append(y); yr.append(pltpu.roll(y, 64, 1))
        yy = jnp.concatenate([jnp.concatenate(ys, 1), jnp.concatenate(yr, 1)], 0)
        h, l = split(yy)
        r = dot(left_out, jnp.concatenate([h, l, h], 0))
        z = jnp.concatenate([jnp.where(lane, r[:32, i * 128:i * 128 + 128], r[32:, i * 128:i * 128 + 128]) for i in range(group)], 0)
        h, l = split(z)
        os[pl.ds(q0 * 32, group * 32), :] = dot(jnp.concatenate([h, l, h], 1), last)
    for t in range(32):
        put(t, os[pl.ds(t, nq, stride=32), :])

def prep_kernel(nq, group, q_hbm, bo_hbm, bi_hbm, ev_hbm, o_ref, qv, bov, biv, evv, xa, xb, os, rc, sem):
    copies = [
        pltpu.make_async_copy(a, b, sem.at[i])
        for i, (a, b) in enumerate(((bo_hbm, bov), (bi_hbm, biv), (ev_hbm, evv), (q_hbm, qv)))
    ]
    for c in copies:
        c.start()
    for c in copies:
        c.wait()
    for t in range(32):
        rc[t:t + 1, :] = evv[0:1, t * 128:t * 128 + 128]
    rec = 1.0 / (rc[...] + damping)
    left_in, left_out = row_maps(bov[0])
    first, last = col_maps(biv[0])

    def get(t):
        return qv[0, :, t * 128:t * 128 + 128]

    def put(t, v):
        o_ref[:, t * 128:t * 128 + 128] = v.astype(BF16)

    prep_body(nq, get, put, left_in, left_out, first, last, rec, xa, xb, os, group)


def prep(q, bo, bi, ev):
    nq = q.shape[1]
    group = 16 if nq % 16 == 0 else nq
    return pl.pallas_call(
        functools.partial(prep_kernel, nq, group),
        out_shape=jax.ShapeDtypeStruct(q.shape[1:], BF16),
        in_specs=[pl.BlockSpec(memory_space=pltpu.HBM)] * 4,
        out_specs=pl.BlockSpec(memory_space=pltpu.VMEM),
        scratch_shapes=[
            pltpu.VMEM(q.shape, BF16),
            pltpu.VMEM(bo.shape, F32),
            pltpu.VMEM(bi.shape, F32),
            pltpu.VMEM(ev.shape, F32),
            pltpu.VMEM((32 * nq, 128), F32),
            pltpu.VMEM((32 * nq, 128), F32),
            pltpu.VMEM((32 * nq, 128), F32),
            pltpu.VMEM((32, 128), F32),
            pltpu.SemaphoreType.DMA((4,)),
        ],
        compiler_params=pltpu.CompilerParams(vmem_limit_bytes=24 << 20),
    )(q, bo, bi, ev)


PIECES = 4


def score_kernel(train_hbm, own, near, mid, mid2, far, far2, mine, core, across, both, tv, qv, pv, sem):
    n = tv.shape[0]
    step = n // PIECES
    copies = [
        pltpu.make_async_copy(train_hbm.at[0, pl.ds(i * step, step)], tv.at[pl.ds(i * step, step)], sem.at[i])
        for i in range(PIECES)
    ]
    for c in copies:
        c.start()
    half = 16 * lax.axis_index("grp")
    rest = 16 - half
    rows = own.shape[0]
    slot = lax.axis_index("ex") ^ lax.axis_index("lyr")

    def at(m, extra):
        return pl.ds(pl.multiple_of((slot ^ m) * rows + extra, 16), 16)

    whole = lambda m: pl.ds(pl.multiple_of((slot ^ m) * rows, 16), rows)
    qv[whole(0), :] = own[...]
    qv[whole(1), :] = near[...]
    qv[at(2, half), :] = mid[...]
    qv[at(2, rest), :] = mid2[...]
    qv[at(3, half), :] = far[...]
    qv[at(3, rest), :] = far2[...]
    for i, c in enumerate(copies):
        c.wait()
        part = dot(tv[i * step:i * step + step, :], qv[...], 1, 1)
        pv[:, i * step:i * step + step] = part.T * (1.0 / math.sqrt(GR * GC))
    for m, o in enumerate((mine, core, across, both)):
        o[...] = pv[m * rows:m * rows + rows, :]


def score(train, *chunks):
    n, f = train.shape[1:]
    rows = chunks[0].shape[0]
    return pl.pallas_call(
        score_kernel,
        out_shape=[jax.ShapeDtypeStruct((rows, n), F32)] * 4,
        in_specs=[pl.BlockSpec(memory_space=pltpu.HBM)] + [pl.BlockSpec(memory_space=pltpu.VMEM)] * 6,
        out_specs=[pl.BlockSpec(memory_space=pltpu.VMEM)] * 4,
        scratch_shapes=[
            pltpu.VMEM((n, f), BF16),
            pltpu.VMEM((4 * rows, f), BF16),
            pltpu.VMEM((4 * rows, n), F32),
            pltpu.SemaphoreType.DMA((PIECES,)),
        ],
        compiler_params=pltpu.CompilerParams(vmem_limit_bytes=32 << 20),
    )(train, *chunks)


def flip(x, axis, mask, size):
    return lax.ppermute(x, axis, [(i, i ^ mask) for i in range(size)])


def local(sizes, train, query, bo, bi, ev):
    ready = prep(query, bo, bi, ev)
    ex, lyr, grp = sizes
    if (ex, lyr, grp) != (4, 4, 2) or ready.shape[0] != 32:
        everyone = lax.all_gather(ready, "ex", axis=0, tiled=True)
        part = dot(train[0], everyone, 1, 1)
        return lax.psum_scatter(part, "lyr", scatter_dimension=1, tiled=True) / math.sqrt(GR * GC)
    start = 16 * lax.axis_index("grp")
    half = lax.dynamic_slice_in_dim(ready, start, 16, 0)
    mid = flip(half, "ex", 2, 4)
    far = flip(half, "ex", 3, 4)
    near = flip(ready, "ex", 1, 4)
    mid2 = flip(mid, "grp", 1, 2)
    far2 = flip(far, "grp", 1, 2)
    mine, core, across, both = score(train, ready, near, mid, mid2, far, far2)
    total = mine + flip(core, "lyr", 1, 4) + flip(across, "lyr", 2, 4) + flip(both, "lyr", 3, 4)
    return total.T


def solution(mesh):
    sizes = tuple(mesh.shape[a] for a in ("ex", "lyr", "grp"))
    return jax.shard_map(
        functools.partial(local, sizes),
        mesh=mesh,
        in_specs=(
            P("lyr", ("grp", "ex"), None),
            P("lyr", "ex", None),
            P("lyr", None, None),
            P("lyr", None, None),
            P("lyr", None),
        ),
        out_specs=P(("grp", "ex"), "lyr"),
        check_vma=False,
    )
```

time: 79.3 us -> 39.7 us (0.50)
  waiting for transfers between devices: 50.5 us -> 16 us
  between operations: 13.5 us -> 0.05 us
  starting transfers between devices: 0.04 us -> 10.9 us
  matrix products: 10 us -> 0 us
  Pallas kernels: 0 us -> 6.32 us
  local copies, waits for them, and re-layouts: 2.81 us -> 5.39 us
  other arithmetic: 2.25 us -> 0.65 us
    all_gather x1 -> x0, waiting for transfers between devices: 30.7 us -> none  [local(): lax.all_gather(own_ready, 'ex', axis=1, tiled=True)]
    reduce_scatter x1 -> x0, waiting for transfers between devices: 19.7 us -> none  [local(): lax.psum_scatter(partial_scores, 'lyr', scatter_dimension=1, tiled=True)]
    ppermute x0 -> x8, waiting for transfers between devices: none -> 16 us  [flip(): return lax.ppermute(x, axis, [(i, i ^ mask) for i in range(size)])]
    ppermute x0 -> x8, starting transfers between devices: none -> 10.9 us  [flip(): return lax.ppermute(x, axis, [(i, i ^ mask) for i in range(size)])]
    dot_general x5 -> x0, matrix products: 10 us -> none  [the longest x1 4.75 us: local(): jnp.einsum('lnf,lqf->nq', train_grads, lax.all_gather(own_ready, 'ex', ax...]
    pallas_call x0 -> x2, Pallas kernels: none -> 6.32 us  [the longest x1 3.44 us: score(): pl.pallas_call(score_kernel, out_shape=[jax.ShapeDtypeStruct((rows, n), F...]
    unnamed x4 -> x10, local copies, waits for them, and re-layouts: 0.01 us -> 5.37 us
    reshape x1 -> x0, local copies, waits for them, and re-layouts: 1.48 us -> none
  transfers between devices with their start and end apart: 2 -> 8, of which waited for: 2 -> 5; matrix products, arithmetic and copies ran while one was open for 0% -> 0% of each run, Pallas kernels for 0% -> 0%
where the time goes in v1:
time: 39.7 us; the launch traced here: 39.3 us
  waiting for transfers between devices  16 us (40%)
  starting transfers between devices  10.9 us (27%)
  Pallas kernels  6.32 us (16%)
  local copies, waits for them, and re-layouts  5.39 us (14%)
  other arithmetic  0.65 us (2%)
    ppermute x8, waiting for transfers between devices, flip(): return lax.ppermute(x, axis, [(i, i ^ mask) for i in range(size)])  16 us
    ppermute x8, starting transfers between devices, flip(): return lax.ppermute(x, axis, [(i, i ^ mask) for i in range(size)])  10.9 us
    unnamed x10, local copies, waits for them, and re-layouts  5.37 us
    pallas_call x1, Pallas kernels, score(): pl.pallas_call(score_kernel, out_shape=[jax.ShapeDtypeStruct((rows, n), F...  3.44 us
    pallas_call x1, Pallas kernels, prep(): pl.pallas_call(functools.partial(prep_kernel, nq, group), out_shape=jax.S...  2.89 us
  transfers between devices with their start and end apart: 8, of which 5 were waited for; matrix products, arithmetic and copies ran while one was open for 0% of the time, Pallas kernels for 0%

profile of v1, /device:TPU:0, one launch (start us, length us, event | category | flops | bytes accessed | tf_op | source)
XLA Modules:
  0.0 39.3 jit_solution(18208977978606301504)
XLA Ops:
  0.0 0.0 copy-start.1
  0.0 0.9 %copy-done.1 = bf16[1,32,4096]{2,1,0:T(8,128)(2,1)S(1)} copy-done((bf16[1,32,4096]{2,1,0:T(8,128)(2,1)S(1)}, bf16[1,32,4096]{2,1,0:T(8,128)(2,1)}, u32[]{:S(2)}) %copy-start.1) | copy-done | bytes 262168
  1.0 0.0 copy-start.2
  1.0 0.8 %copy-done.2 = f32[1,64,64]{2,1,0:T(8,128)S(1)} copy-done((f32[1,64,64]{2,1,0:T(8,128)S(1)}, f32[1,64,64]{2,1,0:T(8,128)}, u32[]{:S(2)}) %copy-start.2) | copy-done | bytes 16408
  1.7 0.0 copy-start.3
  1.7 0.8 %copy-done.3 = f32[1,64,64]{2,1,0:T(8,128)S(1)} copy-done((f32[1,64,64]{2,1,0:T(8,128)S(1)}, f32[1,64,64]{2,1,0:T(8,128)}, u32[]{:S(2)}) %copy-start.3) | copy-done | bytes 16408
  2.5 0.0 copy-start.4
  2.5 0.7 %copy-done.4 = f32[1,4096]{1,0:T(1,128)S(1)} copy-done((f32[1,4096]{1,0:T(1,128)S(1)}, f32[1,4096]{1,0:T(1,128)}, u32[]{:S(2)}) %copy-start.4) | copy-done | bytes 16408
  3.2 2.9 %shard_map.55.own = bf16[32,4096]{1,0:T(8,128)(2,1)S(1)} custom-call(bf16[1,32,4096]{2,1,0:T(8,128)(2,1)S(1)} %copy-done.1, f32[1,64,64]{2,1,0:T(8,128)S(1)} %copy-done.2, f32[1,64,64]{2,1,0:T(8,128)S(1)} %copy-done.3, f32[1,4096]{1,0:T(1,128)S(1)} %copy-done.4), custom_call_target="tpu_custom_call" | custom-call | tf_op jit(solution)/shard_map/pallas_call | solution.py:113
  6.1 5.1 %collective-permute-start.3 = (bf16[16,4096]{1,0:T(8,128)(2,1)S(1)}, bf16[16,4096]{1,0:T(8,128)(2,1)S(1)}, u32[]{:S(2)}, u32[]{:S(2)}) collective-permute-start(bf16[16,4096]{1,0:T(8,128)(2,1)S(1)} %constant_dynamic-slice_fusion), channel_id=1, source_target_pairs={{0,12},{4,8},{8,4},{12,0},{1,13},{5,9},{9,5},{13,1},{2,14},{6,10},... | collective-permute-start | bytes 393224 | tf_op jit(solution)/shard_map/ppermute | solution.py:187
  11.2 0.0 collective-permute-start.1
  11.2 0.6 %collective-permute-start = (bf16[32,4096]{1,0:T(8,128)(2,1)S(1)}, bf16[32,4096]{1,0:T(8,128)(2,1)S(1)}, u32[]{:S(2)}, u32[]{:S(2)}) collective-permute-start(bf16[32,4096]{1,0:T(8,128)(2,1)S(1)} %shard_map.55.own), channel_id=1, source_target_pairs={{0,4},{4,0},{8,12},{12,8},{1,5},{5,1},{9,13},{13,9},{2,6},{6,2},{1... | collective-permute-start | bytes 786440 | tf_op jit(solution)/shard_map/ppermute | solution.py:187
  11.9 3.8 %collective-permute-done.3.far = bf16[16,4096]{1,0:T(8,128)(2,1)S(1)} collective-permute-done((bf16[16,4096]{1,0:T(8,128)(2,1)S(1)}, bf16[16,4096]{1,0:T(8,128)(2,1)S(1)}, u32[]{:S(2)}, u32[]{:S(2)}) %collective-permute-start.3) | collective-permute-done | bytes 131104 | tf_op jit(solution)/shard_map/ppermute | solution.py:187
  15.7 1.7 %collective-permute-start.4 = (bf16[16,4096]{1,0:T(8,128)(2,1)S(1)}, bf16[16,4096]{1,0:T(8,128)(2,1)S(1)}, u32[]{:S(2)}, u32[]{:S(2)}) collective-permute-start(bf16[16,4096]{1,0:T(8,128)(2,1)S(1)} %collective-permute-done.3.far), channel_id=1, source_target_pairs={{0,16},{16,0},{1,17},{17,1},{2,18},{18,2},{3,19},{19,3},{4,20},{20... | collective-permute-start | bytes 393224 | tf_op jit(solution)/shard_map/ppermute | solution.py:187
  17.4 5.0 %collective-permute-done.1.mid = bf16[16,4096]{1,0:T(8,128)(2,1)S(1)} collective-permute-done((bf16[16,4096]{1,0:T(8,128)(2,1)S(1)}, bf16[16,4096]{1,0:T(8,128)(2,1)S(1)}, u32[]{:S(2)}, u32[]{:S(2)}) %collective-permute-start.1) | collective-permute-done | bytes 131104 | tf_op jit(solution)/shard_map/ppermute | solution.py:187
  22.4 1.5 %collective-permute-start.2 = (bf16[16,4096]{1,0:T(8,128)(2,1)S(1)}, bf16[16,4096]{1,0:T(8,128)(2,1)S(1)}, u32[]{:S(2)}, u32[]{:S(2)}) collective-permute-start(bf16[16,4096]{1,0:T(8,128)(2,1)S(1)} %collective-permute-done.1.mid), channel_id=1, source_target_pairs={{0,16},{16,0},{1,17},{17,1},{2,18},{18,2},{3,19},{19,3},{4,20},{20... | collective-permute-start | bytes 393224 | tf_op jit(solution)/shard_map/ppermute | solution.py:187
  23.9 0.0 collective-permute-done.4.far2
  23.9 3.4 %collective-permute-done.2.mid2 = bf16[16,4096]{1,0:T(8,128)(2,1)S(1)} collective-permute-done((bf16[16,4096]{1,0:T(8,128)(2,1)S(1)}, bf16[16,4096]{1,0:T(8,128)(2,1)S(1)}, u32[]{:S(2)}, u32[]{:S(2)}) %collective-permute-start.2) | collective-permute-done | bytes 131104 | tf_op jit(solution)/shard_map/ppermute | solution.py:187
  27.4 0.0 collective-permute-done.near
  27.4 0.0 copy-start
  27.4 2.2 %copy-done = bf16[1,512,4096]{2,1,0:T(8,128)(2,1)S(1)} copy-done((bf16[1,512,4096]{2,1,0:T(8,128)(2,1)S(1)}, bf16[1,512,4096]{2,1,0:T(8,128)(2,1)}, u32[]{:S(2)}) %copy-start) | copy-done | bytes 4194328
  29.6 3.4 %shard_map.56 = (f32[32,512]{1,0:T(8,128)S(1)}, f32[32,512]{1,0:T(8,128)S(1)}, f32[32,512]{1,0:T(8,128)S(1)}, f32[32,512]{1,0:T(8,128)S(1)}) custom-call(bf16[1,512,4096]{2,1,0:T(8,128)(2,1)S(1)} %copy-done, bf16[32,4096]{1,0:T(8,128)(2,1)S(1)} %shard_map.55.own, bf16[32,4096]{1,0:T(8,128)(2,1)S(1)} %collective-permute-done.near, ...), custom_call_target="tpu_custom_call" | custom-call | tf_op jit(solution)/shard_map/pallas_call | solution.py:171
  33.0 0.1 collective-permute-start.5
  33.1 1.6 %collective-permute-start.6 = (f32[32,512]{1,0:T(8,128)S(1)}, f32[32,512]{1,0:T(8,128)S(1)}, u32[]{:S(2)}, u32[]{:S(2)}) collective-permute-start(f32[32,512]{1,0:T(8,128)S(1)} %get-tuple-element.11), channel_id=1, source_target_pairs={{0,2},{1,3},{2,0},{3,1},{4,6},{5,7},{6,4},{7,5},{8,10},{9,11},{10,... | collective-permute-start | bytes 196616 | tf_op jit(solution)/shard_map/ppermute | solution.py:187
  34.6 0.3 collective-permute-start.7
  34.9 0.0 collective-permute-done.5
  34.9 2.6 %collective-permute-done.6 = f32[32,512]{1,0:T(8,128)S(1)} collective-permute-done((f32[32,512]{1,0:T(8,128)S(1)}, f32[32,512]{1,0:T(8,128)S(1)}, u32[]{:S(2)}, u32[]{:S(2)}) %collective-permute-start.6) | collective-permute-done | bytes 65568 | tf_op jit(solution)/shard_map/ppermute | solution.py:187
  37.6 1.1 %collective-permute-done.7 = f32[32,512]{1,0:T(8,128)S(1)} collective-permute-done((f32[32,512]{1,0:T(8,128)S(1)}, f32[32,512]{1,0:T(8,128)S(1)}, u32[]{:S(2)}, u32[]{:S(2)}) %collective-permute-start.7) | collective-permute-done | bytes 65568 | tf_op jit(solution)/shard_map/ppermute | solution.py:187
  38.7 0.6 %add_bitcast_fusion = f32[512,32]{0,1:T(8,128)} fusion(f32[32,512]{1,0:T(8,128)S(1)} %collective-permute-done.7, f32[32,512]{1,0:T(8,128)S(1)} %collective-permute-done.6, f32[32,512]{1,0:T(8,128)S(1)} %get-tuple-element.9, f32[32,512]{1,0:T(8,128)S(1)} %collective-permute-done.5), kind=kLoop, calls=%fused_computation | loop fusion | flops 49152 | bytes 327680 | tf_op jit(solution)/shard_map/transpose | solution.py:206
  (1 shorter events, 0.0 us)
Async XLA Ops:
  0.0 0.9 %copy-start.1 = (bf16[1,32,4096]{2,1,0:T(8,128)(2,1)S(1)}, bf16[1,32,4096]{2,1,0:T(8,128)(2,1)}, u32[]{:S(2)}) copy-start(bf16[1,32,4096]{2,1,0:T(8,128)(2,1)} %q_hbm.1) | copy-start | bytes 786436
  1.0 0.8 %copy-start.2 = (f32[1,64,64]{2,1,0:T(8,128)S(1)}, f32[1,64,64]{2,1,0:T(8,128)}, u32[]{:S(2)}) copy-start(f32[1,64,64]{2,1,0:T(8,128)} %bo_hbm.1) | copy-start | bytes 49156
  1.7 0.8 %copy-start.3 = (f32[1,64,64]{2,1,0:T(8,128)S(1)}, f32[1,64,64]{2,1,0:T(8,128)}, u32[]{:S(2)}) copy-start(f32[1,64,64]{2,1,0:T(8,128)} %bi_hbm.1) | copy-start | bytes 49156
  2.5 0.7 %copy-start.4 = (f32[1,4096]{1,0:T(1,128)S(1)}, f32[1,4096]{1,0:T(1,128)}, u32[]{:S(2)}) copy-start(f32[1,4096]{1,0:T(1,128)} %ev_hbm.1) | copy-start | bytes 49156
  6.1 9.5 %collective-permute-start.3 = (bf16[16,4096]{1,0:T(8,128)(2,1)S(1)}, bf16[16,4096]{1,0:T(8,128)(2,1)S(1)}, u32[]{:S(2)}, u32[]{:S(2)}) collective-permute-start(bf16[16,4096]{1,0:T(8,128)(2,1)S(1)} %constant_dynamic-slice_fusion), channel_id=1, source_target_pairs={{0,12},{4,8},{8,4},{12,0},{1,13},{5,9},{9,5},{13,1},{2,14},{6,10},... | collective-permute-start | bytes 393224 | tf_op jit(solution)/shard_map/ppermute | solution.py:187
  11.2 11.2 %collective-permute-start.1 = (bf16[16,4096]{1,0:T(8,128)(2,1)S(1)}, bf16[16,4096]{1,0:T(8,128)(2,1)S(1)}, u32[]{:S(2)}, u32[]{:S(2)}) collective-permute-start(bf16[16,4096]{1,0:T(8,128)(2,1)S(1)} %constant_dynamic-slice_fusion), channel_id=1, source_target_pairs={{0,8},{4,12},{8,0},{12,4},{1,9},{5,13},{9,1},{13,5},{2,10},{6,14},... | collective-permute-start | bytes 393224 | tf_op jit(solution)/shard_map/ppermute | solution.py:187
  11.2 16.1 %collective-permute-start = (bf16[32,4096]{1,0:T(8,128)(2,1)S(1)}, bf16[32,4096]{1,0:T(8,128)(2,1)S(1)}, u32[]{:S(2)}, u32[]{:S(2)}) collective-permute-start(bf16[32,4096]{1,0:T(8,128)(2,1)S(1)} %shard_map.55.own), channel_id=1, source_target_pairs={{0,4},{4,0},{8,12},{12,8},{1,5},{5,1},{9,13},{13,9},{2,6},{6,2},{1... | collective-permute-start | bytes 786440 | tf_op jit(solution)/shard_map/ppermute | solution.py:187
  15.7 8.3 %collective-permute-start.4 = (bf16[16,4096]{1,0:T(8,128)(2,1)S(1)}, bf16[16,4096]{1,0:T(8,128)(2,1)S(1)}, u32[]{:S(2)}, u32[]{:S(2)}) collective-permute-start(bf16[16,4096]{1,0:T(8,128)(2,1)S(1)} %collective-permute-done.3.far), channel_id=1, source_target_pairs={{0,16},{16,0},{1,17},{17,1},{2,18},{18,2},{3,19},{19,3},{4,20},{20... | collective-permute-start | bytes 393224 | tf_op jit(solution)/shard_map/ppermute | solution.py:187
  22.4 5.0 %collective-permute-start.2 = (bf16[16,4096]{1,0:T(8,128)(2,1)S(1)}, bf16[16,4096]{1,0:T(8,128)(2,1)S(1)}, u32[]{:S(2)}, u32[]{:S(2)}) collective-permute-start(bf16[16,4096]{1,0:T(8,128)(2,1)S(1)} %collective-permute-done.1.mid), channel_id=1, source_target_pairs={{0,16},{16,0},{1,17},{17,1},{2,18},{18,2},{3,19},{19,3},{4,20},{20... | collective-permute-start | bytes 393224 | tf_op jit(solution)/shard_map/ppermute | solution.py:187
  27.4 2.2 %copy-start = (bf16[1,512,4096]{2,1,0:T(8,128)(2,1)S(1)}, bf16[1,512,4096]{2,1,0:T(8,128)(2,1)}, u32[]{:S(2)}) copy-start(bf16[1,512,4096]{2,1,0:T(8,128)(2,1)} %train_hbm.1) | copy-start | bytes 12582916
  33.0 1.9 %collective-permute-start.5 = (f32[32,512]{1,0:T(8,128)S(1)}, f32[32,512]{1,0:T(8,128)S(1)}, u32[]{:S(2)}, u32[]{:S(2)}) collective-permute-start(f32[32,512]{1,0:T(8,128)S(1)} %get-tuple-element.10), channel_id=1, source_target_pairs={{0,1},{1,0},{2,3},{3,2},{4,5},{5,4},{6,7},{7,6},{8,9},{9,8},{10,11... | collective-permute-start | bytes 196616 | tf_op jit(solution)/shard_map/ppermute | solution.py:187
  33.1 4.5 %collective-permute-start.6 = (f32[32,512]{1,0:T(8,128)S(1)}, f32[32,512]{1,0:T(8,128)S(1)}, u32[]{:S(2)}, u32[]{:S(2)}) collective-permute-start(f32[32,512]{1,0:T(8,128)S(1)} %get-tuple-element.11), channel_id=1, source_target_pairs={{0,2},{1,3},{2,0},{3,1},{4,6},{5,7},{6,4},{7,5},{8,10},{9,11},{10,... | collective-permute-start | bytes 196616 | tf_op jit(solution)/shard_map/ppermute | solution.py:187
  34.6 4.0 %collective-permute-start.7 = (f32[32,512]{1,0:T(8,128)S(1)}, f32[32,512]{1,0:T(8,128)S(1)}, u32[]{:S(2)}, u32[]{:S(2)}) collective-permute-start(f32[32,512]{1,0:T(8,128)S(1)} %get-tuple-element.12), channel_id=1, source_target_pairs={{0,3},{1,2},{2,1},{3,0},{4,7},{5,6},{6,5},{7,4},{8,11},{9,10},{10,... | collective-permute-start | bytes 196616 | tf_op jit(solution)/shard_map/ppermute | solution.py:187

commit v2 on v1

v2 whole, which is shorter than its diff:
```python
import functools
import math

import jax, jax.numpy as jnp
from jax import lax
from jax.experimental import pallas as pl
from jax.experimental.pallas import tpu as pltpu
from jax.sharding import PartitionSpec as P

GR = 64
GC = 64
damping = 0.1
F32, BF16 = jnp.float32, jnp.bfloat16
VM = pl.BlockSpec(memory_space=pltpu.VMEM)
HB = pl.BlockSpec(memory_space=pl.ANY)


def dot(a, b, ca=1, cb=0):
    return lax.dot_general(a, b, (((ca,), (cb,)), ((), ())), preferred_element_type=F32)
def split(x):
    h = x.astype(BF16)
    return h, (x - h.astype(F32)).astype(BF16)
def selector(rows, which, swap):
    k = lax.broadcasted_iota(jnp.int32, (rows, 64), 0)
    b = lax.broadcasted_iota(jnp.int32, (rows, 64), 1)
    kk = k % 64
    par = kk // 32
    if swap: par = 1 - par
    hit = b == 2 * (kk % 32) + par
    if which == 1: hit = hit & (k < 128)
    if which == 2: hit = hit & (k >= 128)
    return jnp.where(hit, 1.0, 0.0).astype(BF16)
def row_maps(bo):
    h, l = split(bo)
    sel = selector(64, 0, False)
    outs = []
    for cb in (1, 0):
        th, tl = dot(sel, h, 1, cb).astype(BF16), dot(sel, l, 1, cb).astype(BF16)
        parts = []
        for swap in (False, True):
            full = dot(th, selector(192, 1, swap), 1, 1) + dot(tl, selector(192, 2, swap), 1, 1)
            parts.append(full[32 * swap:32 * swap + 32])
        outs.append(jnp.concatenate(parts, 0).astype(BF16))
    return outs
def col_maps(bi):
    h, l = split(bi)
    r = lax.broadcasted_iota(jnp.int32, (128, 64), 0) % 64
    c = lax.broadcasted_iota(jnp.int32, (128, 64), 1)
    e = jnp.where(r == c, 1.0, 0.0).astype(BF16)
    i = lax.broadcasted_iota(jnp.int32, (128, 128), 0) // 64
    j = lax.broadcasted_iota(jnp.int32, (128, 128), 1) // 64
    same = i == j
    def tile(x, cb):
        t = dot(e, x, 1, cb).astype(BF16)
        return dot(t, e, 1, 1)
    def pick(t, m): return jnp.where(m, t, 0.0).astype(BF16)
    th, tl = tile(h, 0), tile(l, 0)
    diff = jnp.logical_not(same)
    first = jnp.concatenate([jnp.concatenate([pick(th, same), pick(th, diff)], 1), jnp.concatenate([pick(tl, same), pick(tl, diff)], 1)], 0)
    uh, ul = tile(h, 1), tile(l, 1)
    last = jnp.concatenate([pick(uh, same), pick(uh, same), pick(ul, same)], 0)
    return first, last
def prep_body(nq, get, put, left_in, left_out, first, last, rec, xa, xb, os, group=8):
    g = jnp.concatenate([get(t) for t in range(32)], 0)
    x = dot(jnp.concatenate([g, g], 1), first)
    xa[...] = x[:, :128]
    xb[...] = x[:, 128:]
    lane = lax.broadcasted_iota(jnp.int32, (32, 128), 1) < 64
    for q0 in range(0, nq, group):
        qs = range(q0, q0 + group)
        ww = jnp.concatenate([jnp.concatenate([r[pl.ds(q, 32, stride=nq), :] for q in qs], 1) for r in (xa, xb)], 0)
        h, l = split(ww)
        r = dot(left_in, jnp.concatenate([h, l, h], 0))
        ys, yr = [], []
        for i in range(group):
            s = slice(i * 128, i * 128 + 128)
            y = jnp.where(lane, r[:32, s], r[32:, s]) * rec
            ys.append(y); yr.append(pltpu.roll(y, 64, 1))
        yy = jnp.concatenate([jnp.concatenate(ys, 1), jnp.concatenate(yr, 1)], 0)
        h, l = split(yy)
        r = dot(left_out, jnp.concatenate([h, l, h], 0))
        z = jnp.concatenate([jnp.where(lane, r[:32, i * 128:i * 128 + 128], r[32:, i * 128:i * 128 + 128]) for i in range(group)], 0)
        h, l = split(z)
        os[pl.ds(q0 * 32, group * 32), :] = dot(jnp.concatenate([h, l, h], 1), last)
    for t in range(32):
        put(t, os[pl.ds(t, nq, stride=32), :])

def scores_of(train, ready):
    return dot(train, ready, 1, 1).T * (1.0 / math.sqrt(GR * GC))


def first_kernel(nq, q_hbm, bo_hbm, bi_hbm, ev_hbm, train_hbm, tv, lin, lout, fst, lst, rec, part, qv, bov, biv, evv, xa, xb, os, pv, sem):
    copies = [
        pltpu.make_async_copy(a, b, sem.at[i])
        for i, (a, b) in enumerate(((bo_hbm, bov), (bi_hbm, biv), (ev_hbm, evv), (q_hbm, qv), (train_hbm.at[0], tv)))
    ]
    for c in copies:
        c.start()
    for c in copies[:4]:
        c.wait()
    for t in range(32):
        rec[t:t + 1, :] = 1.0 / (evv[0:1, t * 128:t * 128 + 128] + damping)
    lin[...], lout[...] = row_maps(bov[0])
    fst[...], lst[...] = col_maps(biv[0])

    def put(t, v):
        pv[:, t * 128:t * 128 + 128] = v.astype(BF16)

    prep_body(nq, lambda t: qv[0, :, t * 128:t * 128 + 128], put, lin[...], lout[...], fst[...], lst[...], rec[...], xa, xb, os, 16)
    copies[4].wait()
    part[...] = scores_of(tv[...], pv[...])


def maps_shapes():
    return [
        jax.ShapeDtypeStruct((64, 192), BF16),
        jax.ShapeDtypeStruct((64, 192), BF16),
        jax.ShapeDtypeStruct((256, 256), BF16),
        jax.ShapeDtypeStruct((384, 128), BF16),
        jax.ShapeDtypeStruct((32, 128), F32),
    ]


def work(nq):
    return [pltpu.VMEM((32 * nq, 128), F32)] * 3 + [pltpu.VMEM((nq, GR * GC), BF16)]


def cost(nq, n):
    return pl.CostEstimate(flops=2 * n * 4096 * 2048, bytes_accessed=8 << 20, transcendentals=0)


def first(q, bo, bi, ev, train):
    nq = q.shape[1]
    n, f = train.shape[1:]
    return pl.pallas_call(
        functools.partial(first_kernel, nq),
        out_shape=[jax.ShapeDtypeStruct((n, f), BF16)] + maps_shapes() + [jax.ShapeDtypeStruct((nq, n), F32)],
        in_specs=[HB] * 5,
        out_specs=[VM] * 7,
        scratch_shapes=[
            pltpu.VMEM(q.shape, BF16),
            pltpu.VMEM(bo.shape, F32),
            pltpu.VMEM(bi.shape, F32),
            pltpu.VMEM(ev.shape, F32),
        ] + work(nq) + [pltpu.SemaphoreType.DMA((5,))],
        compiler_params=pltpu.CompilerParams(vmem_limit_bytes=20 << 20),
        cost_estimate=cost(nq, n),
    )(q, bo, bi, ev, train)


def next_kernel(counts, *refs):
    k = len(counts)
    chunks, (tv, lin, lout, fst, lst, rec), part, (xa, xb, os, pv) = refs[:k], refs[k:k + 6], refs[k + 6], refs[k + 7:]
    nq = sum(counts)

    def get(t):
        return jnp.concatenate([c[:, t * 128:t * 128 + 128] for c in chunks], 0)

    def put(t, v):
        pv[:, t * 128:t * 128 + 128] = v.astype(BF16)

    prep_body(nq, get, put, lin[...], lout[...], fst[...], lst[...], rec[...], xa, xb, os, 16)
    part[...] = scores_of(tv[...], pv[...])


def following(chunks, tv, maps):
    counts = [c.shape[0] for c in chunks]
    nq, n = sum(counts), tv.shape[0]
    return pl.pallas_call(
        functools.partial(next_kernel, counts),
        out_shape=jax.ShapeDtypeStruct((nq, n), F32),
        in_specs=[VM] * (len(chunks) + 6),
        out_specs=VM,
        scratch_shapes=work(nq),
        compiler_params=pltpu.CompilerParams(vmem_limit_bytes=20 << 20),
        cost_estimate=cost(nq, n),
    )(*chunks, tv, *maps)


def last_kernel(chunk, tv, lin, lout, fst, lst, rec, p_own, p_near, p_mid, p_rest, mine, core, across, both, xa, xb, os, pv, sv):
    half = 16 * lax.axis_index("grp")
    other = 16 - half
    rows = p_own.shape[0]
    slot = lax.axis_index("ex") ^ lax.axis_index("lyr")

    def at(m, extra, size):
        return pl.ds(pl.multiple_of((slot ^ m) * rows + extra, 16), size)

    sv[at(0, 0, rows), :] = p_own[...]
    sv[at(1, 0, rows), :] = p_near[...]
    sv[at(2, half, 16), :] = p_mid[...]
    sv[at(2, other, 16), :] = p_rest[0:16, :]
    sv[at(3, half, 16), :] = p_rest[16:32, :]

    def put(t, v):
        pv[:, t * 128:t * 128 + 128] = v.astype(BF16)

    prep_body(16, lambda t: chunk[:, t * 128:t * 128 + 128], put, lin[...], lout[...], fst[...], lst[...], rec[...], xa, xb, os, 16)
    sv[at(3, other, 16), :] = scores_of(tv[...], pv[...])
    for m, o in enumerate((mine, core, across, both)):
        o[...] = sv[m * rows:m * rows + rows, :].astype(o.dtype)


def final(chunk, tv, maps, *parts):
    rows, n = parts[0].shape
    return pl.pallas_call(
        last_kernel,
        out_shape=[jax.ShapeDtypeStruct((rows, n), d) for d in (F32, F32, SENT, SENT)],
        in_specs=[VM] * (7 + len(parts)),
        out_specs=[VM] * 4,
        scratch_shapes=work(16) + [pltpu.VMEM((4 * rows, n), F32)],
        compiler_params=pltpu.CompilerParams(vmem_limit_bytes=20 << 20),
        cost_estimate=cost(16, n),
    )(chunk, tv, *maps, *parts)


SENT = BF16


def flip(x, axis, mask, size):
    return lax.ppermute(x, axis, [(i, i ^ mask) for i in range(size)])


def plain(sizes, train, query, bo, bi, ev):
    g = query.shape[1]
    matrix = query[0].astype(F32).reshape(g, GR, GC)
    high = lax.Precision.HIGHEST
    x = jnp.einsum("ba,qbc->qac", bo[0], matrix, precision=high)
    x = jnp.einsum("qac,cd->qad", x, bi[0], precision=high)
    x = x / (ev.reshape(1, GR, GC) + damping)
    x = jnp.einsum("ab,qbc->qac", bo[0], x, precision=high)
    x = jnp.einsum("qac,dc->qad", x, bi[0], precision=high)
    ready = lax.all_gather(x.reshape(g, GR * GC).astype(BF16), "ex", axis=0, tiled=True)
    part = dot(train[0], ready, 1, 1)
    return lax.psum_scatter(part, "lyr", scatter_dimension=1, tiled=True) / math.sqrt(GR * GC)


def local(sizes, train, query, bo, bi, ev):
    if sizes != (4, 4, 2) or query.shape[1] != 32:
        return plain(sizes, train, query, bo, bi, ev)
    raw = query[0]
    start = 16 * lax.axis_index("grp")
    half = lax.dynamic_slice_in_dim(raw, start, 16, 0)
    mid = flip(half, "ex", 2, 4)
    far = flip(half, "ex", 3, 4)
    near = flip(raw, "ex", 1, 4)
    tv, *rest = first(query, bo, bi, ev, train)
    maps, p_own = rest[:5], rest[5]
    mid2 = flip(mid, "grp", 1, 2)
    far2 = flip(far, "grp", 1, 2)
    p_near = following([near], tv, maps)
    p_mid = following([mid], tv, maps)
    p_rest = following([mid2, far], tv, maps)
    mine, core, across, both = final(far2, tv, maps, p_own, p_near, p_mid, p_rest)
    total = mine + flip(core, "lyr", 1, 4)
    total = total + flip(across, "lyr", 2, 4).astype(F32) + flip(both, "lyr", 3, 4).astype(F32)
    return total.T


def solution(mesh):
    sizes = tuple(mesh.shape[a] for a in ("ex", "lyr", "grp"))
    return jax.shard_map(
        functools.partial(local, sizes),
        mesh=mesh,
        in_specs=(
            P("lyr", ("grp", "ex"), None),
            P("lyr", "ex", None),
            P("lyr", None, None),
            P("lyr", None, None),
            P("lyr", None),
        ),
        out_specs=P(("grp", "ex"), "lyr"),
        check_vma=False,
    )
```

time: 39.7 us -> 38.6 us (0.972)
  waiting for transfers between devices: 16 us -> 4.73 us
  Pallas kernels: 6.32 us -> 16.8 us
  starting transfers between devices: 10.9 us -> 9.7 us
  local copies, waits for them, and re-layouts: 5.39 us -> 6.31 us
    ppermute x8, waiting for transfers between devices: 16 us -> 4.73 us  [flip(): return lax.ppermute(x, axis, [(i, i ^ mask) for i in range(size)])]
    pallas_call x2 -> x5, Pallas kernels: 6.32 us -> 16.8 us  [the longest x3 9.64 us: following(): pl.pallas_call(functools.partial(next_kernel, counts), out_shape=jax.Shap...]
    ppermute x8, starting transfers between devices: 10.9 us -> 9.7 us  [flip(): return lax.ppermute(x, axis, [(i, i ^ mask) for i in range(size)])]
    dynamic_slice x1, local copies, waits for them, and re-layouts: 0.02 us -> 0.91 us  [local(): half = lax.dynamic_slice_in_dim(raw, start, 16, 0)]
  transfers between devices with their start and end apart: 8 -> 8, of which waited for: 5 -> 3; matrix products, arithmetic and copies ran while one was open for 0% -> 0% of each run, Pallas kernels for 0% -> 38%
where the time goes in v2:
time: 38.6 us; the launch traced here: 38.2 us
  Pallas kernels  16.8 us (44%)
  starting transfers between devices  9.7 us (25%)
  local copies, waits for them, and re-layouts  6.31 us (16%)
  waiting for transfers between devices  4.73 us (12%)
  other arithmetic  0.65 us (2%)
    ppermute x8, starting transfers between devices, flip(): return lax.ppermute(x, axis, [(i, i ^ mask) for i in range(size)])  9.7 us
    pallas_call x3, Pallas kernels, following(): pl.pallas_call(functools.partial(next_kernel, counts), out_shape=jax.Shap...  9.64 us
    unnamed x10, local copies, waits for them, and re-layouts  5.4 us
    ppermute x8, waiting for transfers between devices, flip(): return lax.ppermute(x, axis, [(i, i ^ mask) for i in range(size)])  4.73 us
    pallas_call x1, Pallas kernels, first(): pl.pallas_call(functools.partial(first_kernel, nq), out_shape=[jax.ShapeD...  4.73 us
    pallas_call x1, Pallas kernels, final(): pl.pallas_call(last_kernel, out_shape=[jax.ShapeDtypeStruct((rows, n), d)...  2.4 us
    dynamic_slice x1, local copies, waits for them, and re-layouts, local(): half = lax.dynamic_slice_in_dim(raw, start, 16, 0)  0.91 us
  transfers between devices with their start and end apart: 8, of which 3 were waited for; matrix products, arithmetic and copies ran while one was open for 0% of the time, Pallas kernels for 38%

profile of v2, /device:TPU:0, one launch (start us, length us, event | category | flops | bytes accessed | tf_op | source)
XLA Modules:
  0.0 38.2 jit_solution(2963090838580360575)
XLA Ops:
  0.0 0.9 %dynamic-slice_bitcast_fusion = bf16[16,4096]{1,0:T(8,128)(2,1)S(1)} fusion(bf16[1,32,4096]{2,1,0:T(8,128)(2,1)} %q_hbm.1, s32[]{:T(128)S(6)} %select_n.3), kind=kLoop, calls=%fused_computation | loop fusion | bytes 262148 | tf_op jit(solution)/shard_map/dynamic_slice | solution.py:243
  0.9 4.1 %collective-permute-start.3 = (bf16[16,4096]{1,0:T(8,128)(2,1)S(1)}, bf16[16,4096]{1,0:T(8,128)(2,1)S(1)}, u32[]{:S(2)}, u32[]{:S(2)}) collective-permute-start(bf16[16,4096]{1,0:T(8,128)(2,1)S(1)} %dynamic-slice_bitcast_fusion), channel_id=1, source_target_pairs={{0,8},{4,12},{8,0},{12,4},{1,9},{5,13},{9,1},{13,5},{2,10},{6,14},... | collective-permute-start | bytes 393224 | tf_op jit(solution)/shard_map/ppermute | solution.py:221
  5.0 1.3 %collective-permute-start = (bf16[16,4096]{1,0:T(8,128)(2,1)S(1)}, bf16[16,4096]{1,0:T(8,128)(2,1)S(1)}, u32[]{:S(2)}, u32[]{:S(2)}) collective-permute-start(bf16[16,4096]{1,0:T(8,128)(2,1)S(1)} %dynamic-slice_bitcast_fusion), channel_id=1, source_target_pairs={{0,12},{4,8},{8,4},{12,0},{1,13},{5,9},{9,5},{13,1},{2,14},{6,10},... | collective-permute-start | bytes 393224 | tf_op jit(solution)/shard_map/ppermute | solution.py:221
  6.4 0.2 collective-permute-start.2
  6.6 0.0 copy-start
  6.6 1.0 %copy-done = bf16[1,32,4096]{2,1,0:T(8,128)(2,1)S(1)} copy-done((bf16[1,32,4096]{2,1,0:T(8,128)(2,1)S(1)}, bf16[1,32,4096]{2,1,0:T(8,128)(2,1)}, u32[]{:S(2)}) %copy-start) | copy-done | bytes 262168
  7.6 0.0 copy-start.1
  7.6 2.2 %copy-done.1 = bf16[1,512,4096]{2,1,0:T(8,128)(2,1)S(1)} copy-done((bf16[1,512,4096]{2,1,0:T(8,128)(2,1)S(1)}, bf16[1,512,4096]{2,1,0:T(8,128)(2,1)}, u32[]{:S(2)}) %copy-start.1) | copy-done | bytes 4194328
  9.8 0.0 copy-start.2
  9.8 0.8 %copy-done.2 = f32[1,64,64]{2,1,0:T(8,128)S(1)} copy-done((f32[1,64,64]{2,1,0:T(8,128)S(1)}, f32[1,64,64]{2,1,0:T(8,128)}, u32[]{:S(2)}) %copy-start.2) | copy-done | bytes 16408
  10.5 0.0 copy-start.3
  10.5 0.8 %copy-done.3 = f32[1,64,64]{2,1,0:T(8,128)S(1)} copy-done((f32[1,64,64]{2,1,0:T(8,128)S(1)}, f32[1,64,64]{2,1,0:T(8,128)}, u32[]{:S(2)}) %copy-start.3) | copy-done | bytes 16408
  11.3 0.0 copy-start.4
  11.3 0.7 %copy-done.4 = f32[1,4096]{1,0:T(1,128)S(1)} copy-done((f32[1,4096]{1,0:T(1,128)S(1)}, f32[1,4096]{1,0:T(1,128)}, u32[]{:S(2)}) %copy-start.4) | copy-done | bytes 16408
  12.0 4.7 %shard_map.55 = (bf16[512,4096]{1,0:T(8,128)(2,1)S(1)}, bf16[64,192]{1,0:T(8,128)(2,1)S(1)}, bf16[64,192]{1,0:T(8,128)(2,1)S(1)}, bf16[256,256]{1,0:T(8,128)(2,1...) custom-call(bf16[1,32,4096]{2,1,0:T(8,128)(2,1)S(1)} %copy-done, ...), custom_call_target="tpu_custom_call" | custom-call | flops 8589934592 | bytes 8388608 | tf_op jit(solution)/shard_map/pallas_call | solution.py:135
  16.7 0.0 collective-permute-done.3.refs_0_
  16.8 1.6 %collective-permute-start.4 = (bf16[16,4096]{1,0:T(8,128)(2,1)S(1)}, bf16[16,4096]{1,0:T(8,128)(2,1)S(1)}, u32[]{:S(2)}, u32[]{:S(2)}) collective-permute-start(bf16[16,4096]{1,0:T(8,128)(2,1)S(1)} %collective-permute-done.3.refs_0_), channel_id=1, source_target_pairs={{0,16},{16,0},{1,17},{17,1},{2,18},{18,2},{3,19},{19,3},{4,20},{20... | collective-permute-start | bytes 393224 | tf_op jit(solution)/shard_map/ppermute | solution.py:221
  18.3 0.0 collective-permute-done.refs_1_
  18.3 0.5 %collective-permute-start.1 = (bf16[16,4096]{1,0:T(8,128)(2,1)S(1)}, bf16[16,4096]{1,0:T(8,128)(2,1)S(1)}, u32[]{:S(2)}, u32[]{:S(2)}) collective-permute-start(bf16[16,4096]{1,0:T(8,128)(2,1)S(1)} %collective-permute-done.refs_1_), channel_id=1, source_target_pairs={{0,16},{16,0},{1,17},{17,1},{2,18},{18,2},{3,19},{19,3},{4,20},{20... | collective-permute-start | bytes 393224 | tf_op jit(solution)/shard_map/ppermute | solution.py:221
  18.8 2.4 %shard_map.57.p_mid = f32[16,512]{1,0:T(8,128)S(1)} custom-call(bf16[16,4096]{1,0:T(8,128)(2,1)S(1)} %collective-permute-done.3.refs_0_, bf16[512,4096]{1,0:T(8,128)(2,1)S(1)} %get-tuple-element.16.refs_1_.refs_2_.tv, bf16[64,192]{1,0:T(8,128)(2,1)S(1)} %get-tuple-element.17.refs_2_.refs_3_.lin, bf16[64,192]{1,0:T(8,128)(2,1)S(1)} %get-tuple-element.18.refs_3_.refs_4_.lout, ...), custom_call_target="tpu_custom_call" | custom-call | flops 8589934592 | bytes 8388608 | tf_op jit(solution)/shard_map/pallas_call | solution.py:169
  21.2 1.7 %collective-permute-done.4.refs_0_ = bf16[16,4096]{1,0:T(8,128)(2,1)S(1)} collective-permute-done((bf16[16,4096]{1,0:T(8,128)(2,1)S(1)}, bf16[16,4096]{1,0:T(8,128)(2,1)S(1)}, u32[]{:S(2)}, u32[]{:S(2)}) %collective-permute-start.4) | collective-permute-done | bytes 131104 | tf_op jit(solution)/shard_map/ppermute | solution.py:221
  22.9 3.6 %shard_map.58.p_rest = f32[32,512]{1,0:T(8,128)S(1)} custom-call(bf16[16,4096]{1,0:T(8,128)(2,1)S(1)} %collective-permute-done.4.refs_0_, bf16[16,4096]{1,0:T(8,128)(2,1)S(1)} %collective-permute-done.refs_1_, bf16[512,4096]{1,0:T(8,128)(2,1)S(1)} %get-tuple-element.16.refs_1_.refs_2_.tv, bf16[64,192]{1,0:T(8,128)(2,1)S(1)} %get-tuple-element.17.refs_2_.refs_3_.lin, ...), custom_call_target="tpu_custom_call" | custom-call | flops 8589934592 | bytes 8388608 | tf_op jit(solution)/shard_map/pallas_call | solution.py:169
  26.5 0.0 collective-permute-done.2.refs_0_
  26.5 3.6 %shard_map.56.p_near = f32[32,512]{1,0:T(8,128)S(1)} custom-call(bf16[32,4096]{1,0:T(8,128)(2,1)S(1)} %collective-permute-done.2.refs_0_, bf16[512,4096]{1,0:T(8,128)(2,1)S(1)} %get-tuple-element.16.refs_1_.refs_2_.tv, bf16[64,192]{1,0:T(8,128)(2,1)S(1)} %get-tuple-element.17.refs_2_.refs_3_.lin, bf16[64,192]{1,0:T(8,128)(2,1)S(1)} %get-tuple-element.18.refs_3_.refs_4_.lout, ...), custom_call_target="tpu_custom_call" | custom-call | flops 8589934592 | bytes 8388608 | tf_op jit(solution)/shard_map/pallas_call | solution.py:169
  30.2 0.0 collective-permute-done.1.chunk
  30.2 2.4 %shard_map.59 = (f32[32,512]{1,0:T(8,128)S(1)}, f32[32,512]{1,0:T(8,128)S(1)}, bf16[32,512]{1,0:T(8,128)(2,1)S(1)}, bf16[32,512]{1,0:T(8,128)(2,1)S(1)}) custom-call(bf16[16,4096]{1,0:T(8,128)(2,1)S(1)} %collective-permute-done.1.chunk, bf16[512,4096]{1,0:T(8,128)(2,1)S(1)} %get-tuple-element.16.refs_1_.refs_2_.tv, ...), custom_call_target="tpu_custom_call" | custom-call | flops 8589934592 | bytes 8388608 | tf_op jit(solution)/shard_map/pallas_call | solution.py:206
  32.6 0.1 collective-permute-start.5
  32.7 1.6 %collective-permute-start.6 = (bf16[32,512]{1,0:T(8,128)(2,1)S(1)}, bf16[32,512]{1,0:T(8,128)(2,1)S(1)}, u32[]{:S(2)}, u32[]{:S(2)}) collective-permute-start(bf16[32,512]{1,0:T(8,128)(2,1)S(1)} %get-tuple-element.25), channel_id=1, source_target_pairs={{0,2},{1,3},{2,0},{3,1},{4,6},{5,7},{6,4},{7,5},{8,10},{9,11},{10,... | collective-permute-start | bytes 98312 | tf_op jit(solution)/shard_map/ppermute | solution.py:221
  34.2 0.3 collective-permute-start.7
  34.5 2.1 %collective-permute-done.6 = bf16[32,512]{1,0:T(8,128)(2,1)S(1)} collective-permute-done((bf16[32,512]{1,0:T(8,128)(2,1)S(1)}, bf16[32,512]{1,0:T(8,128)(2,1)S(1)}, u32[]{:S(2)}, u32[]{:S(2)}) %collective-permute-start.6) | collective-permute-done | bytes 32800 | tf_op jit(solution)/shard_map/ppermute | solution.py:221
  36.6 0.9 %collective-permute-done.7 = bf16[32,512]{1,0:T(8,128)(2,1)S(1)} collective-permute-done((bf16[32,512]{1,0:T(8,128)(2,1)S(1)}, bf16[32,512]{1,0:T(8,128)(2,1)S(1)}, u32[]{:S(2)}, u32[]{:S(2)}) %collective-permute-start.7) | collective-permute-done | bytes 32800 | tf_op jit(solution)/shard_map/ppermute | solution.py:221
  37.6 0.0 collective-permute-done.5
  37.6 0.6 %add_bitcast_fusion = f32[512,32]{0,1:T(8,128)} fusion(bf16[32,512]{1,0:T(8,128)(2,1)S(1)} %collective-permute-done.7, bf16[32,512]{1,0:T(8,128)(2,1)S(1)} %collective-permute-done.6, f32[32,512]{1,0:T(8,128)S(1)} %get-tuple-element.23, f32[32,512]{1,0:T(8,128)S(1)} %collective-permute-done.5), kind=kLoop, calls=%fused_computation.1 | loop fusion | flops 81920 | bytes 262144 | tf_op jit(solution)/shard_map/transpose | solution.py:257
Async XLA Ops:
  0.9 15.8 %collective-permute-start.3 = (bf16[16,4096]{1,0:T(8,128)(2,1)S(1)}, bf16[16,4096]{1,0:T(8,128)(2,1)S(1)}, u32[]{:S(2)}, u32[]{:S(2)}) collective-permute-start(bf16[16,4096]{1,0:T(8,128)(2,1)S(1)} %dynamic-slice_bitcast_fusion), channel_id=1, source_target_pairs={{0,8},{4,12},{8,0},{12,4},{1,9},{5,13},{9,1},{13,5},{2,10},{6,14},... | collective-permute-start | bytes 393224 | tf_op jit(solution)/shard_map/ppermute | solution.py:221
  5.0 13.3 %collective-permute-start = (bf16[16,4096]{1,0:T(8,128)(2,1)S(1)}, bf16[16,4096]{1,0:T(8,128)(2,1)S(1)}, u32[]{:S(2)}, u32[]{:S(2)}) collective-permute-start(bf16[16,4096]{1,0:T(8,128)(2,1)S(1)} %dynamic-slice_bitcast_fusion), channel_id=1, source_target_pairs={{0,12},{4,8},{8,4},{12,0},{1,13},{5,9},{9,5},{13,1},{2,14},{6,10},... | collective-permute-start | bytes 393224 | tf_op jit(solution)/shard_map/ppermute | solution.py:221
  6.4 20.2 %collective-permute-start.2 = (bf16[32,4096]{1,0:T(8,128)(2,1)}, bf16[32,4096]{1,0:T(8,128)(2,1)S(1)}, u32[]{:S(2)}, u32[]{:S(2)}) collective-permute-start(bf16[32,4096]{1,0:T(8,128)(2,1)} %bitcast.5), channel_id=1, source_target_pairs={{0,4},{4,0},{8,12},{12,8},{1,5},{5,1},{9,13},{13,9},{2,6},{6,2},{1... | collective-permute-start | bytes 786440 | tf_op jit(solution)/shard_map/ppermute | solution.py:221
  6.6 1.0 %copy-start = (bf16[1,32,4096]{2,1,0:T(8,128)(2,1)S(1)}, bf16[1,32,4096]{2,1,0:T(8,128)(2,1)}, u32[]{:S(2)}) copy-start(bf16[1,32,4096]{2,1,0:T(8,128)(2,1)} %q_hbm.1) | copy-start | bytes 786436
  7.6 2.2 %copy-start.1 = (bf16[1,512,4096]{2,1,0:T(8,128)(2,1)S(1)}, bf16[1,512,4096]{2,1,0:T(8,128)(2,1)}, u32[]{:S(2)}) copy-start(bf16[1,512,4096]{2,1,0:T(8,128)(2,1)} %train_hbm.1) | copy-start | bytes 12582916
  9.8 0.8 %copy-start.2 = (f32[1,64,64]{2,1,0:T(8,128)S(1)}, f32[1,64,64]{2,1,0:T(8,128)}, u32[]{:S(2)}) copy-start(f32[1,64,64]{2,1,0:T(8,128)} %bo_hbm.1) | copy-start | bytes 49156
  10.5 0.8 %copy-start.3 = (f32[1,64,64]{2,1,0:T(8,128)S(1)}, f32[1,64,64]{2,1,0:T(8,128)}, u32[]{:S(2)}) copy-start(f32[1,64,64]{2,1,0:T(8,128)} %bi_hbm.1) | copy-start | bytes 49156
  11.3 0.7 %copy-start.4 = (f32[1,4096]{1,0:T(1,128)S(1)}, f32[1,4096]{1,0:T(1,128)}, u32[]{:S(2)}) copy-start(f32[1,4096]{1,0:T(1,128)} %ev_hbm.1) | copy-start | bytes 49156
  16.8 6.1 %collective-permute-start.4 = (bf16[16,4096]{1,0:T(8,128)(2,1)S(1)}, bf16[16,4096]{1,0:T(8,128)(2,1)S(1)}, u32[]{:S(2)}, u32[]{:S(2)}) collective-permute-start(bf16[16,4096]{1,0:T(8,128)(2,1)S(1)} %collective-permute-done.3.refs_0_), channel_id=1, source_target_pairs={{0,16},{16,0},{1,17},{17,1},{2,18},{18,2},{3,19},{19,3},{4,20},{20... | collective-permute-start | bytes 393224 | tf_op jit(solution)/shard_map/ppermute | solution.py:221
  18.3 11.8 %collective-permute-start.1 = (bf16[16,4096]{1,0:T(8,128)(2,1)S(1)}, bf16[16,4096]{1,0:T(8,128)(2,1)S(1)}, u32[]{:S(2)}, u32[]{:S(2)}) collective-permute-start(bf16[16,4096]{1,0:T(8,128)(2,1)S(1)} %collective-permute-done.refs_1_), channel_id=1, source_target_pairs={{0,16},{16,0},{1,17},{17,1},{2,18},{18,2},{3,19},{19,3},{4,20},{20... | collective-permute-start | bytes 393224 | tf_op jit(solution)/shard_map/ppermute | solution.py:221
  32.6 5.0 %collective-permute-start.5 = (f32[32,512]{1,0:T(8,128)S(1)}, f32[32,512]{1,0:T(8,128)S(1)}, u32[]{:S(2)}, u32[]{:S(2)}) collective-permute-start(f32[32,512]{1,0:T(8,128)S(1)} %get-tuple-element.24), channel_id=1, source_target_pairs={{0,1},{1,0},{2,3},{3,2},{4,5},{5,4},{6,7},{7,6},{8,9},{9,8},{10,11... | collective-permute-start | bytes 196616 | tf_op jit(solution)/shard_map/ppermute | solution.py:221
  32.7 4.0 %collective-permute-start.6 = (bf16[32,512]{1,0:T(8,128)(2,1)S(1)}, bf16[32,512]{1,0:T(8,128)(2,1)S(1)}, u32[]{:S(2)}, u32[]{:S(2)}) collective-permute-start(bf16[32,512]{1,0:T(8,128)(2,1)S(1)} %get-tuple-element.25), channel_id=1, source_target_pairs={{0,2},{1,3},{2,0},{3,1},{4,6},{5,7},{6,4},{7,5},{8,10},{9,11},{10,... | collective-permute-start | bytes 98312 | tf_op jit(solution)/shard_map/ppermute | solution.py:221
  34.2 3.3 %collective-permute-start.7 = (bf16[32,512]{1,0:T(8,128)(2,1)S(1)}, bf16[32,512]{1,0:T(8,128)(2,1)S(1)}, u32[]{:S(2)}, u32[]{:S(2)}) collective-permute-start(bf16[32,512]{1,0:T(8,128)(2,1)S(1)} %get-tuple-element.26), channel_id=1, source_target_pairs={{0,3},{1,2},{2,1},{3,0},{4,7},{5,6},{6,5},{7,4},{8,11},{9,10},{10,... | collective-permute-start | bytes 98312 | tf_op jit(solution)/shard_map/ppermute | solution.py:221

commit v3 on v2

--- a/solution.py
+++ b/solution.py
@@ -12,7 +12,6 @@
 damping = 0.1
 F32, BF16 = jnp.float32, jnp.bfloat16
 VM = pl.BlockSpec(memory_space=pltpu.VMEM)
-HB = pl.BlockSpec(memory_space=pl.ANY)
 
 
 def dot(a, b, ca=1, cb=0):
@@ -89,7 +88,7 @@
     return dot(train, ready, 1, 1).T * (1.0 / math.sqrt(GR * GC))
 
 
-def first_kernel(nq, q_hbm, bo_hbm, bi_hbm, ev_hbm, train_hbm, tv, lin, lout, fst, lst, rec, part, qv, bov, biv, evv, xa, xb, os, pv, sem):
+def first_kernel(nq, q_hbm, bo_hbm, bi_hbm, ev_hbm, train_hbm, tv, lin, lout, fst, lst, rec, out, qv, bov, biv, evv, xa, xb, os, sem):
     copies = [
         pltpu.make_async_copy(a, b, sem.at[i])
         for i, (a, b) in enumerate(((bo_hbm, bov), (bi_hbm, biv), (ev_hbm, evv), (q_hbm, qv), (train_hbm.at[0], tv)))
@@ -104,11 +103,10 @@
     fst[...], lst[...] = col_maps(biv[0])
 
     def put(t, v):
-        pv[:, t * 128:t * 128 + 128] = v.astype(BF16)
+        out[:, t * 128:t * 128 + 128] = v.astype(BF16)
 
     prep_body(nq, lambda t: qv[0, :, t * 128:t * 128 + 128], put, lin[...], lout[...], fst[...], lst[...], rec[...], xa, xb, os, 16)
     copies[4].wait()
-    part[...] = scores_of(tv[...], pv[...])
 
 
 def maps_shapes():
@@ -122,20 +120,24 @@
 
 
 def work(nq):
-    return [pltpu.VMEM((32 * nq, 128), F32)] * 3 + [pltpu.VMEM((nq, GR * GC), BF16)]
-
-
-def cost(nq, n):
-    return pl.CostEstimate(flops=2 * n * 4096 * 2048, bytes_accessed=8 << 20, transcendentals=0)
-
-
-def first(q, bo, bi, ev, train):
+    return [pltpu.VMEM((32 * nq, 128), F32)] * 3
+
+
+def settings(us):
+    return dict(
+        compiler_params=pltpu.CompilerParams(vmem_limit_bytes=20 << 20),
+        cost_estimate=pl.CostEstimate(flops=int(us * 1e9), bytes_accessed=int(us * 3.6e6), transcendentals=0),
+    )
+
+
+def first(*args):
+    q, bo, bi, ev, train = args
     nq = q.shape[1]
     n, f = train.shape[1:]
     return pl.pallas_call(
         functools.partial(first_kernel, nq),
-        out_shape=[jax.ShapeDtypeStruct((n, f), BF16)] + maps_shapes() + [jax.ShapeDtypeStruct((nq, n), F32)],
-        in_specs=[HB] * 5,
+        out_shape=[jax.ShapeDtypeStruct((n, f), BF16)] + maps_shapes() + [jax.ShapeDtypeStruct((nq, f), BF16)],
+        in_specs=[pl.BlockSpec(memory_space=pltpu.HBM)] * 5,
         out_specs=[VM] * 7,
         scratch_shapes=[
             pltpu.VMEM(q.shape, BF16),
@@ -143,54 +145,73 @@
             pltpu.VMEM(bi.shape, F32),
             pltpu.VMEM(ev.shape, F32),
         ] + work(nq) + [pltpu.SemaphoreType.DMA((5,))],
-        compiler_params=pltpu.CompilerParams(vmem_limit_bytes=20 << 20),
-        cost_estimate=cost(nq, n),
-    )(q, bo, bi, ev, train)
-
-
-def next_kernel(counts, *refs):
-    k = len(counts)
-    chunks, (tv, lin, lout, fst, lst, rec), part, (xa, xb, os, pv) = refs[:k], refs[k:k + 6], refs[k + 6], refs[k + 7:]
-    nq = sum(counts)
-
-    def get(t):
-        return jnp.concatenate([c[:, t * 128:t * 128 + 128] for c in chunks], 0)
-
-    def put(t, v):
-        pv[:, t * 128:t * 128 + 128] = v.astype(BF16)
-
-    prep_body(nq, get, put, lin[...], lout[...], fst[...], lst[...], rec[...], xa, xb, os, 16)
-    part[...] = scores_of(tv[...], pv[...])
-
-
-def following(chunks, tv, maps):
-    counts = [c.shape[0] for c in chunks]
-    nq, n = sum(counts), tv.shape[0]
-    return pl.pallas_call(
-        functools.partial(next_kernel, counts),
-        out_shape=jax.ShapeDtypeStruct((nq, n), F32),
-        in_specs=[VM] * (len(chunks) + 6),
+        **settings(4),
+    )(*(pltpu.with_memory_space_constraint(x, pltpu.HBM) for x in args))
+
+
+def next_kernel(nq, chunk, lin, lout, fst, lst, rec, out, xa, xb, os):
+    def put(t, v):
+        out[:, t * 128:t * 128 + 128] = v.astype(BF16)
+
+    prep_body(nq, lambda t: chunk[:, t * 128:t * 128 + 128], put, lin[...], lout[...], fst[...], lst[...], rec[...], xa, xb, os, 16)
+
+
+def following(chunk, maps):
+    nq = chunk.shape[0]
+    return pl.pallas_call(
+        functools.partial(next_kernel, nq),
+        out_shape=jax.ShapeDtypeStruct(chunk.shape, BF16),
+        in_specs=[VM] * 6,
         out_specs=VM,
         scratch_shapes=work(nq),
-        compiler_params=pltpu.CompilerParams(vmem_limit_bytes=20 << 20),
-        cost_estimate=cost(nq, n),
-    )(*chunks, tv, *maps)
-
-
-def last_kernel(chunk, tv, lin, lout, fst, lst, rec, p_own, p_near, p_mid, p_rest, mine, core, across, both, xa, xb, os, pv, sv):
+        **settings(nq / 12),
+    )(chunk, *maps)
+
+
+def bulk_kernel(mid2, far, tv, lin, lout, fst, lst, rec, own, near, mid, part, xa, xb, os, pv):
+    rows = own.shape[0]
+    pv[0:rows, :] = own[...]
+    pv[rows:2 * rows, :] = near[...]
+    pv[2 * rows:2 * rows + 16, :] = mid[...]
+
+    def get(t):
+        s = slice(t * 128, t * 128 + 128)
+        return jnp.concatenate([mid2[:, s], far[:, s]], 0)
+
+    def put(t, v):
+        pv[2 * rows + 16:, t * 128:t * 128 + 128] = v.astype(BF16)
+
+    prep_body(32, get, put, lin[...], lout[...], fst[...], lst[...], rec[...], xa, xb, os, 16)
+    part[...] = scores_of(tv[...], pv[...])
+
+
+def bulk(mid2, far, tv, maps, own, near, mid):
+    rows, f = own.shape
+    n = tv.shape[0]
+    return pl.pallas_call(
+        bulk_kernel,
+        out_shape=jax.ShapeDtypeStruct((2 * rows + 48, n), F32),
+        in_specs=[VM] * 11,
+        out_specs=VM,
+        scratch_shapes=work(32) + [pltpu.VMEM((2 * rows + 48, f), BF16)],
+        **settings(3.5),
+    )(mid2, far, tv, *maps, own, near, mid)
+
+
+def last_kernel(chunk, tv, lin, lout, fst, lst, rec, part, mine, core, across, both, xa, xb, os, pv, sv):
     half = 16 * lax.axis_index("grp")
     other = 16 - half
-    rows = p_own.shape[0]
+    rows = mine.shape[0]
     slot = lax.axis_index("ex") ^ lax.axis_index("lyr")
 
     def at(m, extra, size):
         return pl.ds(pl.multiple_of((slot ^ m) * rows + extra, 16), size)
 
-    sv[at(0, 0, rows), :] = p_own[...]
-    sv[at(1, 0, rows), :] = p_near[...]
-    sv[at(2, half, 16), :] = p_mid[...]
-    sv[at(2, other, 16), :] = p_rest[0:16, :]
-    sv[at(3, half, 16), :] = p_rest[16:32, :]
+    sv[at(0, 0, rows), :] = part[0:rows, :]
+    sv[at(1, 0, rows), :] = part[rows:2 * rows, :]
+    sv[at(2, half, 16), :] = part[2 * rows:2 * rows + 16, :]
+    sv[at(2, other, 16), :] = part[2 * rows + 16:2 * rows + 32, :]
+    sv[at(3, half, 16), :] = part[2 * rows + 32:, :]
 
     def put(t, v):
         pv[:, t * 128:t * 128 + 128] = v.astype(BF16)
@@ -201,17 +222,16 @@
         o[...] = sv[m * rows:m * rows + rows, :].astype(o.dtype)
 
 
-def final(chunk, tv, maps, *parts):
-    rows, n = parts[0].shape
+def final(chunk, tv, maps, part, rows):
+    n, f = tv.shape
     return pl.pallas_call(
         last_kernel,
         out_shape=[jax.ShapeDtypeStruct((rows, n), d) for d in (F32, F32, SENT, SENT)],
-        in_specs=[VM] * (7 + len(parts)),
+        in_specs=[VM] * 8,
         out_specs=[VM] * 4,
-        scratch_shapes=work(16) + [pltpu.VMEM((4 * rows, n), F32)],
-        compiler_params=pltpu.CompilerParams(vmem_limit_bytes=20 << 20),
-        cost_estimate=cost(16, n),
-    )(chunk, tv, *maps, *parts)
+        scratch_shapes=work(16) + [pltpu.VMEM((16, f), BF16), pltpu.VMEM((4 * rows, n), F32)],
+        **settings(2),
+    )(chunk, tv, *maps, part)
 
 
 SENT = BF16
@@ -245,13 +265,15 @@
     far = flip(half, "ex", 3, 4)
     near = flip(raw, "ex", 1, 4)
     tv, *rest = first(query, bo, bi, ev, train)
-    maps, p_own = rest[:5], rest[5]
+    maps, own = rest[:5], rest[5]
+    near = following(near, maps)
+    mid, near = lax.optimization_barrier((mid, near))
     mid2 = flip(mid, "grp", 1, 2)
+    mid = following(mid, maps)
+    far, mid = lax.optimization_barrier((far, mid))
     far2 = flip(far, "grp", 1, 2)
-    p_near = following([near], tv, maps)
-    p_mid = following([mid], tv, maps)
-    p_rest = following([mid2, far], tv, maps)
-    mine, core, across, both = final(far2, tv, maps, p_own, p_near, p_mid, p_rest)
+    part = bulk(mid2, far, tv, maps, own, near, mid)
+    mine, core, across, both = final(far2, tv, maps, part, own.shape[0])
     total = mine + flip(core, "lyr", 1, 4)
     total = total + flip(across, "lyr", 2, 4).astype(F32) + flip(both, "lyr", 3, 4).astype(F32)
     return total.T

time: 38.6 us -> 38.6 us (level)
  waiting for transfers between devices: 4.73 us -> 14.1 us
  local copies, waits for them, and re-layouts: 6.31 us -> 0.91 us
  Pallas kernels: 16.8 us -> 13 us
    ppermute x8, waiting for transfers between devices: 4.73 us -> 14.1 us  [flip(): return lax.ppermute(x, axis, [(i, i ^ mask) for i in range(size)])]
    unnamed x10 -> x0, local copies, waits for them, and re-layouts: 5.4 us -> none
    pallas_call x3, Pallas kernels: 9.64 us -> 6.73 us  [the longest x1 3.65 us: bulk(): pl.pallas_call(bulk_kernel, out_shape=jax.ShapeDtypeStruct((2 * rows + 48...]
    pallas_call x1, Pallas kernels: 4.73 us -> 3.83 us  [first(): pl.pallas_call(functools.partial(first_kernel, nq), out_shape=[jax.ShapeD...]
  transfers between devices with their start and end apart: 8 -> 8, of which waited for: 3 -> 4; matrix products, arithmetic and copies ran while one was open for 0% -> 0% of each run, Pallas kernels for 38% -> 27%
where the time goes in v3:
time: 38.6 us; the launch traced here: 38.4 us
  waiting for transfers between devices  14.1 us (37%)
  Pallas kernels  13 us (34%)
  starting transfers between devices  9.77 us (25%)
  local copies, waits for them, and re-layouts  0.91 us (2%)
  other arithmetic  0.65 us (2%)
    ppermute x8, waiting for transfers between devices, flip(): return lax.ppermute(x, axis, [(i, i ^ mask) for i in range(size)])  14.1 us
    ppermute x8, starting transfers between devices, flip(): return lax.ppermute(x, axis, [(i, i ^ mask) for i in range(size)])  9.77 us
    pallas_call x1, Pallas kernels, first(): pl.pallas_call(functools.partial(first_kernel, nq), out_shape=[jax.ShapeD...  3.83 us
    pallas_call x1, Pallas kernels, bulk(): pl.pallas_call(bulk_kernel, out_shape=jax.ShapeDtypeStruct((2 * rows + 48...  3.65 us
    pallas_call x2, Pallas kernels, following(): pl.pallas_call(functools.partial(next_kernel, nq), out_shape=jax.ShapeDty...  3.08 us
    pallas_call x1, Pallas kernels, final(): pl.pallas_call(last_kernel, out_shape=[jax.ShapeDtypeStruct((rows, n), d)...  2.4 us
    dynamic_slice x1, local copies, waits for them, and re-layouts, local(): half = lax.dynamic_slice_in_dim(raw, start, 16, 0)  0.91 us
  transfers between devices with their start and end apart: 8, of which 4 were waited for; matrix products, arithmetic and copies ran while one was open for 0% of the time, Pallas kernels for 27%

profile of v3, /device:TPU:0, one launch (start us, length us, event | category | flops | bytes accessed | tf_op | source)
XLA Modules:
  0.0 38.4 jit_solution(436034084857546993)
XLA Ops:
  0.0 0.9 %dynamic-slice_bitcast_fusion = bf16[16,4096]{1,0:T(8,128)(2,1)S(1)} fusion(bf16[1,32,4096]{2,1,0:T(8,128)(2,1)} %q_hbm.1, s32[]{:T(128)S(6)} %select_n.3), kind=kLoop, calls=%fused_computation | loop fusion | bytes 262148 | tf_op jit(solution)/shard_map/dynamic_slice | solution.py:263
  0.9 4.1 %collective-permute-start.1 = (bf16[16,4096]{1,0:T(8,128)(2,1)S(1)}, bf16[16,4096]{1,0:T(8,128)(2,1)S(1)}, u32[]{:S(2)}, u32[]{:S(2)}) collective-permute-start(bf16[16,4096]{1,0:T(8,128)(2,1)S(1)} %dynamic-slice_bitcast_fusion), channel_id=1, source_target_pairs={{0,8},{4,12},{8,0},{12,4},{1,9},{5,13},{9,1},{13,5},{2,10},{6,14},... | collective-permute-start | bytes 393224 | tf_op jit(solution)/shard_map/ppermute | solution.py:241
  5.0 1.3 %collective-permute-start = (bf16[16,4096]{1,0:T(8,128)(2,1)S(1)}, bf16[16,4096]{1,0:T(8,128)(2,1)S(1)}, u32[]{:S(2)}, u32[]{:S(2)}) collective-permute-start(bf16[16,4096]{1,0:T(8,128)(2,1)S(1)} %dynamic-slice_bitcast_fusion), channel_id=1, source_target_pairs={{0,12},{4,8},{8,4},{12,0},{1,13},{5,9},{9,5},{13,1},{2,14},{6,10},... | collective-permute-start | bytes 393224 | tf_op jit(solution)/shard_map/ppermute | solution.py:241
  6.4 0.2 collective-permute-start.2
  6.6 3.8 %shard_map.55 = (bf16[512,4096]{1,0:T(8,128)(2,1)S(1)}, bf16[64,192]{1,0:T(8,128)(2,1)S(1)}, bf16[64,192]{1,0:T(8,128)(2,1)S(1)}, bf16[256,256]{1,0:T(8,128)(2,1...) custom-call(bf16[1,32,4096]{2,1,0:T(8,128)(2,1)} %q_hbm.1, ...), custom_call_target="tpu_custom_call" | custom-call | flops 4000000000 | bytes 14400000 | tf_op jit(solution)/shard_map/pallas_call | solution.py:137
  10.4 8.1 %collective-permute-done.2.chunk = bf16[32,4096]{1,0:T(8,128)(2,1)S(1)} collective-permute-done((bf16[32,4096]{1,0:T(8,128)(2,1)}, bf16[32,4096]{1,0:T(8,128)(2,1)S(1)}, u32[]{:S(2)}, u32[]{:S(2)}) %collective-permute-start.2) | collective-permute-done | bytes 262176 | tf_op jit(solution)/shard_map/ppermute | solution.py:241
  18.5 2.0 %shard_map.56.near = bf16[32,4096]{1,0:T(8,128)(2,1)S(1)} custom-call(bf16[32,4096]{1,0:T(8,128)(2,1)S(1)} %collective-permute-done.2.chunk, bf16[64,192]{1,0:T(8,128)(2,1)S(1)} %get-tuple-element.20.lin, bf16[64,192]{1,0:T(8,128)(2,1)S(1)} %get-tuple-element.21.lout, bf16[256,256]{1,0:T(8,128)(2,1)S(1)} %get-tuple-element.22.fst, ...), custom_call_target="tpu_custom_call" | custom-call | flops 2666666752 | bytes 9600000 | tf_op jit(solution)/shard_map/pallas_call | solution.py:161
  20.6 0.0 collective-permute-done.1.chunk
  20.6 1.6 %collective-permute-start.4 = (bf16[16,4096]{1,0:T(8,128)(2,1)S(1)}, bf16[16,4096]{1,0:T(8,128)(2,1)S(1)}, u32[]{:S(2)}, u32[]{:S(2)}) collective-permute-start(bf16[16,4096]{1,0:T(8,128)(2,1)S(1)} %collective-permute-done.1.chunk), channel_id=1, source_target_pairs={{0,16},{16,0},{1,17},{17,1},{2,18},{18,2},{3,19},{19,3},{4,20},{20... | collective-permute-start | bytes 393224 | tf_op jit(solution)/shard_map/ppermute | solution.py:241
  22.2 1.1 %shard_map.57.mid = bf16[16,4096]{1,0:T(8,128)(2,1)S(1)} custom-call(bf16[16,4096]{1,0:T(8,128)(2,1)S(1)} %collective-permute-done.1.chunk, bf16[64,192]{1,0:T(8,128)(2,1)S(1)} %get-tuple-element.20.lin, bf16[64,192]{1,0:T(8,128)(2,1)S(1)} %get-tuple-element.21.lout, bf16[256,256]{1,0:T(8,128)(2,1)S(1)} %get-tuple-element.22.fst, ...), custom_call_target="tpu_custom_call" | custom-call | flops 1333333376 | bytes 4800000 | tf_op jit(solution)/shard_map/pallas_call | solution.py:161
  23.3 0.0 collective-permute-done.far
  23.3 0.5 %collective-permute-start.3 = (bf16[16,4096]{1,0:T(8,128)(2,1)S(1)}, bf16[16,4096]{1,0:T(8,128)(2,1)S(1)}, u32[]{:S(2)}, u32[]{:S(2)}) collective-permute-start(bf16[16,4096]{1,0:T(8,128)(2,1)S(1)} %collective-permute-done.far), channel_id=1, source_target_pairs={{0,16},{16,0},{1,17},{17,1},{2,18},{18,2},{3,19},{19,3},{4,20},{20... | collective-permute-start | bytes 393224 | tf_op jit(solution)/shard_map/ppermute | solution.py:241
  23.8 2.9 %collective-permute-done.4.mid2 = bf16[16,4096]{1,0:T(8,128)(2,1)S(1)} collective-permute-done((bf16[16,4096]{1,0:T(8,128)(2,1)S(1)}, bf16[16,4096]{1,0:T(8,128)(2,1)S(1)}, u32[]{:S(2)}, u32[]{:S(2)}) %collective-permute-start.4) | collective-permute-done | bytes 131104 | tf_op jit(solution)/shard_map/ppermute | solution.py:241
  26.7 3.7 %shard_map.58.part = f32[112,512]{1,0:T(8,128)S(1)} custom-call(bf16[16,4096]{1,0:T(8,128)(2,1)S(1)} %collective-permute-done.4.mid2, bf16[16,4096]{1,0:T(8,128)(2,1)S(1)} %collective-permute-done.far, bf16[512,4096]{1,0:T(8,128)(2,1)S(1)} %get-tuple-element.27.tv, bf16[64,192]{1,0:T(8,128)(2,1)S(1)} %get-tuple-element.20.lin, ...), custom_call_target="tpu_custom_call" | custom-call | flops 3500000000 | bytes 12600000 | tf_op jit(solution)/shard_map/pallas_call | solution.py:191
  30.4 0.0 collective-permute-done.3.chunk
  30.4 2.4 %shard_map.59 = (f32[32,512]{1,0:T(8,128)S(1)}, f32[32,512]{1,0:T(8,128)S(1)}, bf16[32,512]{1,0:T(8,128)(2,1)S(1)}, bf16[32,512]{1,0:T(8,128)(2,1)S(1)}) custom-call(bf16[16,4096]{1,0:T(8,128)(2,1)S(1)} %collective-permute-done.3.chunk, bf16[512,4096]{1,0:T(8,128)(2,1)S(1)} %get-tuple-element.27.tv, bf16[64,192]{1,0:T(8,128)(2,1)S(1)} %get-tuple-element.20.lin, ...), custom_call_target="tpu_custom_call" | custom-call | flops 2000000000 | bytes 7200000 | tf_op jit(solution)/shard_map/pallas_call | solution.py:227
  32.8 0.1 collective-permute-start.5
  32.9 1.6 %collective-permute-start.6 = (bf16[32,512]{1,0:T(8,128)(2,1)S(1)}, bf16[32,512]{1,0:T(8,128)(2,1)S(1)}, u32[]{:S(2)}, u32[]{:S(2)}) collective-permute-start(bf16[32,512]{1,0:T(8,128)(2,1)S(1)} %get-tuple-element.33), channel_id=1, source_target_pairs={{0,2},{1,3},{2,0},{3,1},{4,6},{5,7},{6,4},{7,5},{8,10},{9,11},{10,... | collective-permute-start | bytes 98312 | tf_op jit(solution)/shard_map/ppermute | solution.py:241
  34.4 0.3 collective-permute-start.7
  34.7 2.1 %collective-permute-done.6 = bf16[32,512]{1,0:T(8,128)(2,1)S(1)} collective-permute-done((bf16[32,512]{1,0:T(8,128)(2,1)S(1)}, bf16[32,512]{1,0:T(8,128)(2,1)S(1)}, u32[]{:S(2)}, u32[]{:S(2)}) %collective-permute-start.6) | collective-permute-done | bytes 32800 | tf_op jit(solution)/shard_map/ppermute | solution.py:241
  36.8 0.9 %collective-permute-done.7 = bf16[32,512]{1,0:T(8,128)(2,1)S(1)} collective-permute-done((bf16[32,512]{1,0:T(8,128)(2,1)S(1)}, bf16[32,512]{1,0:T(8,128)(2,1)S(1)}, u32[]{:S(2)}, u32[]{:S(2)}) %collective-permute-start.7) | collective-permute-done | bytes 32800 | tf_op jit(solution)/shard_map/ppermute | solution.py:241
  37.8 0.0 collective-permute-done.5
  37.8 0.6 %add_bitcast_fusion = f32[512,32]{0,1:T(8,128)} fusion(bf16[32,512]{1,0:T(8,128)(2,1)S(1)} %collective-permute-done.7, bf16[32,512]{1,0:T(8,128)(2,1)S(1)} %collective-permute-done.6, f32[32,512]{1,0:T(8,128)S(1)} %get-tuple-element.31, f32[32,512]{1,0:T(8,128)S(1)} %collective-permute-done.5), kind=kLoop, calls=%fused_computation.1 | loop fusion | flops 81920 | bytes 262144 | tf_op jit(solution)/shard_map/transpose | solution.py:279
Async XLA Ops:
  0.9 19.7 %collective-permute-start.1 = (bf16[16,4096]{1,0:T(8,128)(2,1)S(1)}, bf16[16,4096]{1,0:T(8,128)(2,1)S(1)}, u32[]{:S(2)}, u32[]{:S(2)}) collective-permute-start(bf16[16,4096]{1,0:T(8,128)(2,1)S(1)} %dynamic-slice_bitcast_fusion), channel_id=1, source_target_pairs={{0,8},{4,12},{8,0},{12,4},{1,9},{5,13},{9,1},{13,5},{2,10},{6,14},... | collective-permute-start | bytes 393224 | tf_op jit(solution)/shard_map/ppermute | solution.py:241
  5.0 18.3 %collective-permute-start = (bf16[16,4096]{1,0:T(8,128)(2,1)S(1)}, bf16[16,4096]{1,0:T(8,128)(2,1)S(1)}, u32[]{:S(2)}, u32[]{:S(2)}) collective-permute-start(bf16[16,4096]{1,0:T(8,128)(2,1)S(1)} %dynamic-slice_bitcast_fusion), channel_id=1, source_target_pairs={{0,12},{4,8},{8,4},{12,0},{1,13},{5,9},{9,5},{13,1},{2,14},{6,10},... | collective-permute-start | bytes 393224 | tf_op jit(solution)/shard_map/ppermute | solution.py:241
  6.4 12.2 %collective-permute-start.2 = (bf16[32,4096]{1,0:T(8,128)(2,1)}, bf16[32,4096]{1,0:T(8,128)(2,1)S(1)}, u32[]{:S(2)}, u32[]{:S(2)}) collective-permute-start(bf16[32,4096]{1,0:T(8,128)(2,1)} %bitcast.5), channel_id=1, source_target_pairs={{0,4},{4,0},{8,12},{12,8},{1,5},{5,1},{9,13},{13,9},{2,6},{6,2},{1... | collective-permute-start | bytes 786440 | tf_op jit(solution)/shard_map/ppermute | solution.py:241
  20.6 6.1 %collective-permute-start.4 = (bf16[16,4096]{1,0:T(8,128)(2,1)S(1)}, bf16[16,4096]{1,0:T(8,128)(2,1)S(1)}, u32[]{:S(2)}, u32[]{:S(2)}) collective-permute-start(bf16[16,4096]{1,0:T(8,128)(2,1)S(1)} %collective-permute-done.1.chunk), channel_id=1, source_target_pairs={{0,16},{16,0},{1,17},{17,1},{2,18},{18,2},{3,19},{19,3},{4,20},{20... | collective-permute-start | bytes 393224 | tf_op jit(solution)/shard_map/ppermute | solution.py:241
  23.3 7.1 %collective-permute-start.3 = (bf16[16,4096]{1,0:T(8,128)(2,1)S(1)}, bf16[16,4096]{1,0:T(8,128)(2,1)S(1)}, u32[]{:S(2)}, u32[]{:S(2)}) collective-permute-start(bf16[16,4096]{1,0:T(8,128)(2,1)S(1)} %collective-permute-done.far), channel_id=1, source_target_pairs={{0,16},{16,0},{1,17},{17,1},{2,18},{18,2},{3,19},{19,3},{4,20},{20... | collective-permute-start | bytes 393224 | tf_op jit(solution)/shard_map/ppermute | solution.py:241
  32.8 5.0 %collective-permute-start.5 = (f32[32,512]{1,0:T(8,128)S(1)}, f32[32,512]{1,0:T(8,128)S(1)}, u32[]{:S(2)}, u32[]{:S(2)}) collective-permute-start(f32[32,512]{1,0:T(8,128)S(1)} %get-tuple-element.32), channel_id=1, source_target_pairs={{0,1},{1,0},{2,3},{3,2},{4,5},{5,4},{6,7},{7,6},{8,9},{9,8},{10,11... | collective-permute-start | bytes 196616 | tf_op jit(solution)/shard_map/ppermute | solution.py:241
  32.9 4.0 %collective-permute-start.6 = (bf16[32,512]{1,0:T(8,128)(2,1)S(1)}, bf16[32,512]{1,0:T(8,128)(2,1)S(1)}, u32[]{:S(2)}, u32[]{:S(2)}) collective-permute-start(bf16[32,512]{1,0:T(8,128)(2,1)S(1)} %get-tuple-element.33), channel_id=1, source_target_pairs={{0,2},{1,3},{2,0},{3,1},{4,6},{5,7},{6,4},{7,5},{8,10},{9,11},{10,... | collective-permute-start | bytes 98312 | tf_op jit(solution)/shard_map/ppermute | solution.py:241
  34.4 3.3 %collective-permute-start.7 = (bf16[32,512]{1,0:T(8,128)(2,1)S(1)}, bf16[32,512]{1,0:T(8,128)(2,1)S(1)}, u32[]{:S(2)}, u32[]{:S(2)}) collective-permute-start(bf16[32,512]{1,0:T(8,128)(2,1)S(1)} %get-tuple-element.34), channel_id=1, source_target_pairs={{0,3},{1,2},{2,1},{3,0},{4,7},{5,6},{6,5},{7,4},{8,11},{9,10},{10,... | collective-permute-start | bytes 98312 | tf_op jit(solution)/shard_map/ppermute | solution.py:241

commit v4 on v3

--- a/solution.py
+++ b/solution.py
@@ -88,7 +88,7 @@
     return dot(train, ready, 1, 1).T * (1.0 / math.sqrt(GR * GC))
 
 
-def first_kernel(nq, q_hbm, bo_hbm, bi_hbm, ev_hbm, train_hbm, tv, lin, lout, fst, lst, rec, out, qv, bov, biv, evv, xa, xb, os, sem):
+def first_kernel(nq, q_hbm, bo_hbm, bi_hbm, ev_hbm, train_hbm, tv, lin, lout, fst, lst, rec, out_a, out_b, qv, bov, biv, evv, xa, xb, os, sem):
     copies = [
         pltpu.make_async_copy(a, b, sem.at[i])
         for i, (a, b) in enumerate(((bo_hbm, bov), (bi_hbm, biv), (ev_hbm, evv), (q_hbm, qv), (train_hbm.at[0], tv)))
@@ -103,7 +103,9 @@
     fst[...], lst[...] = col_maps(biv[0])
 
     def put(t, v):
-        out[:, t * 128:t * 128 + 128] = v.astype(BF16)
+        v = v.astype(BF16)
+        out_a[:, t * 128:t * 128 + 128] = v[:16]
+        out_b[:, t * 128:t * 128 + 128] = v[16:]
 
     prep_body(nq, lambda t: qv[0, :, t * 128:t * 128 + 128], put, lin[...], lout[...], fst[...], lst[...], rec[...], xa, xb, os, 16)
     copies[4].wait()
@@ -136,9 +138,9 @@
     n, f = train.shape[1:]
     return pl.pallas_call(
         functools.partial(first_kernel, nq),
-        out_shape=[jax.ShapeDtypeStruct((n, f), BF16)] + maps_shapes() + [jax.ShapeDtypeStruct((nq, f), BF16)],
+        out_shape=[jax.ShapeDtypeStruct((n, f), BF16)] + maps_shapes() + [jax.ShapeDtypeStruct((16, f), BF16)] * 2,
         in_specs=[pl.BlockSpec(memory_space=pltpu.HBM)] * 5,
-        out_specs=[VM] * 7,
+        out_specs=[VM] * 8,
         scratch_shapes=[
             pltpu.VMEM(q.shape, BF16),
             pltpu.VMEM(bo.shape, F32),
@@ -168,37 +170,27 @@
     )(chunk, *maps)
 
 
-def bulk_kernel(mid2, far, tv, lin, lout, fst, lst, rec, own, near, mid, part, xa, xb, os, pv):
-    rows = own.shape[0]
-    pv[0:rows, :] = own[...]
-    pv[rows:2 * rows, :] = near[...]
-    pv[2 * rows:2 * rows + 16, :] = mid[...]
-
-    def get(t):
-        s = slice(t * 128, t * 128 + 128)
-        return jnp.concatenate([mid2[:, s], far[:, s]], 0)
-
-    def put(t, v):
-        pv[2 * rows + 16:, t * 128:t * 128 + 128] = v.astype(BF16)
-
-    prep_body(32, get, put, lin[...], lout[...], fst[...], lst[...], rec[...], xa, xb, os, 16)
+def bulk_kernel(*refs):
+    *pieces, tv, part, pv = refs
+    for i, p in enumerate(pieces):
+        pv[i * 16:i * 16 + 16, :] = p[...]
     part[...] = scores_of(tv[...], pv[...])
 
 
-def bulk(mid2, far, tv, maps, own, near, mid):
-    rows, f = own.shape
-    n = tv.shape[0]
+def bulk(tv, *pieces):
+    n, f = tv.shape
+    rows = 16 * len(pieces)
     return pl.pallas_call(
         bulk_kernel,
-        out_shape=jax.ShapeDtypeStruct((2 * rows + 48, n), F32),
-        in_specs=[VM] * 11,
+        out_shape=jax.ShapeDtypeStruct((rows, n), F32),
+        in_specs=[VM] * (len(pieces) + 1),
         out_specs=VM,
-        scratch_shapes=work(32) + [pltpu.VMEM((2 * rows + 48, f), BF16)],
-        **settings(3.5),
-    )(mid2, far, tv, *maps, own, near, mid)
-
-
-def last_kernel(chunk, tv, lin, lout, fst, lst, rec, part, mine, core, across, both, xa, xb, os, pv, sv):
+        scratch_shapes=[pltpu.VMEM((rows, f), BF16)],
+        **settings(1.5),
+    )(*pieces, tv)
+
+
+def last_kernel(far2, tv, part, mine, core, across, both, sv):
     half = 16 * lax.axis_index("grp")
     other = 16 - half
     rows = mine.shape[0]
@@ -212,26 +204,21 @@
     sv[at(2, half, 16), :] = part[2 * rows:2 * rows + 16, :]
     sv[at(2, other, 16), :] = part[2 * rows + 16:2 * rows + 32, :]
     sv[at(3, half, 16), :] = part[2 * rows + 32:, :]
-
-    def put(t, v):
-        pv[:, t * 128:t * 128 + 128] = v.astype(BF16)
-
-    prep_body(16, lambda t: chunk[:, t * 128:t * 128 + 128], put, lin[...], lout[...], fst[...], lst[...], rec[...], xa, xb, os, 16)
-    sv[at(3, other, 16), :] = scores_of(tv[...], pv[...])
+    sv[at(3, other, 16), :] = scores_of(tv[...], far2[...])
     for m, o in enumerate((mine, core, across, both)):
         o[...] = sv[m * rows:m * rows + rows, :].astype(o.dtype)
 
 
-def final(chunk, tv, maps, part, rows):
+def final(far2, tv, part, rows):
     n, f = tv.shape
     return pl.pallas_call(
         last_kernel,
         out_shape=[jax.ShapeDtypeStruct((rows, n), d) for d in (F32, F32, SENT, SENT)],
-        in_specs=[VM] * 8,
+        in_specs=[VM] * 3,
         out_specs=[VM] * 4,
-        scratch_shapes=work(16) + [pltpu.VMEM((16, f), BF16), pltpu.VMEM((4 * rows, n), F32)],
-        **settings(2),
-    )(chunk, tv, *maps, part)
+        scratch_shapes=[pltpu.VMEM((4 * rows, n), F32)],
+        **settings(1.3),
+    )(far2, tv, part)
 
 
 SENT = BF16
@@ -258,22 +245,20 @@
 def local(sizes, train, query, bo, bi, ev):
     if sizes != (4, 4, 2) or query.shape[1] != 32:
         return plain(sizes, train, query, bo, bi, ev)
-    raw = query[0]
     start = 16 * lax.axis_index("grp")
-    half = lax.dynamic_slice_in_dim(raw, start, 16, 0)
+    half = lax.dynamic_slice_in_dim(query[0], start, 16, 0)
     mid = flip(half, "ex", 2, 4)
-    far = flip(half, "ex", 3, 4)
-    near = flip(raw, "ex", 1, 4)
     tv, *rest = first(query, bo, bi, ev, train)
-    maps, own = rest[:5], rest[5]
-    near = following(near, maps)
-    mid, near = lax.optimization_barrier((mid, near))
+    maps, own_a, own_b = rest[:5], rest[5], rest[6]
+    near_a = flip(own_a, "ex", 1, 4)
+    mid = following(mid, maps)
+    far = flip(mid, "ex", 1, 4)
     mid2 = flip(mid, "grp", 1, 2)
-    mid = following(mid, maps)
-    far, mid = lax.optimization_barrier((far, mid))
+    own_b, mid = lax.optimization_barrier((own_b, mid))
+    near_b = flip(own_b, "ex", 1, 4)
     far2 = flip(far, "grp", 1, 2)
-    part = bulk(mid2, far, tv, maps, own, near, mid)
-    mine, core, across, both = final(far2, tv, maps, part, own.shape[0])
+    part = bulk(tv, own_a, own_b, near_a, near_b, mid, mid2, far)
+    mine, core, across, both = final(far2, tv, part, query.shape[1])
     total = mine + flip(core, "lyr", 1, 4)
     total = total + flip(across, "lyr", 2, 4).astype(F32) + flip(both, "lyr", 3, 4).astype(F32)
     return total.T

time: 38.6 us -> 30.4 us (0.79)
  waiting for transfers between devices: 14.1 us -> 8.52 us
  Pallas kernels: 13 us -> 7.43 us
  starting transfers between devices: 9.77 us -> 12.7 us
    ppermute x8 -> x9, waiting for transfers between devices: 14.1 us -> 8.52 us  [flip(): return lax.ppermute(x, axis, [(i, i ^ mask) for i in range(size)])]
    ppermute x8 -> x9, starting transfers between devices: 9.77 us -> 12.7 us  [flip(): return lax.ppermute(x, axis, [(i, i ^ mask) for i in range(size)])]
    pallas_call x1, Pallas kernels: 3.65 us -> 1.3 us  [bulk(): pl.pallas_call(bulk_kernel, out_shape=jax.ShapeDtypeStruct((rows, n), F32...]
    pallas_call x2 -> x1, Pallas kernels: 3.08 us -> 1.05 us  [following(): pl.pallas_call(functools.partial(next_kernel, nq), out_shape=jax.ShapeDty...]
    pallas_call x1, Pallas kernels: 2.4 us -> 1.28 us  [final(): pl.pallas_call(last_kernel, out_shape=[jax.ShapeDtypeStruct((rows, n), d)...]
  transfers between devices with their start and end apart: 8 -> 9, of which waited for: 4 -> 6; matrix products, arithmetic and copies ran while one was open for 0% -> 0% of each run, Pallas kernels for 27% -> 20%
where the time goes in v4:
time: 30.4 us; the launch traced here: 30.3 us
  starting transfers between devices  12.7 us (42%)
  waiting for transfers between devices  8.52 us (28%)
  Pallas kernels  7.43 us (24%)
  local copies, waits for them, and re-layouts  0.91 us (3%)
  other arithmetic  0.65 us (2%)
    ppermute x9, starting transfers between devices, flip(): return lax.ppermute(x, axis, [(i, i ^ mask) for i in range(size)])  12.7 us
    ppermute x9, waiting for transfers between devices, flip(): return lax.ppermute(x, axis, [(i, i ^ mask) for i in range(size)])  8.52 us
    pallas_call x1, Pallas kernels, first(): pl.pallas_call(functools.partial(first_kernel, nq), out_shape=[jax.ShapeD...  3.8 us
    pallas_call x1, Pallas kernels, bulk(): pl.pallas_call(bulk_kernel, out_shape=jax.ShapeDtypeStruct((rows, n), F32...  1.3 us
    pallas_call x1, Pallas kernels, final(): pl.pallas_call(last_kernel, out_shape=[jax.ShapeDtypeStruct((rows, n), d)...  1.28 us
    pallas_call x1, Pallas kernels, following(): pl.pallas_call(functools.partial(next_kernel, nq), out_shape=jax.ShapeDty...  1.05 us
    dynamic_slice x1, local copies, waits for them, and re-layouts, local(): half = lax.dynamic_slice_in_dim(query[0], start, 16, 0)  0.91 us
    transpose x1, other arithmetic, local(): return total.T  0.65 us
  transfers between devices with their start and end apart: 9, of which 6 were waited for; matrix products, arithmetic and copies ran while one was open for 0% of the time, Pallas kernels for 20%

profile of v4, /device:TPU:0, one launch (start us, length us, event | category | flops | bytes accessed | tf_op | source)
XLA Modules:
  0.0 30.3 jit_solution(2695058252856595746)
XLA Ops:
  0.0 0.9 %dynamic-slice_bitcast_fusion = bf16[16,4096]{1,0:T(8,128)(2,1)S(1)} fusion(bf16[1,32,4096]{2,1,0:T(8,128)(2,1)} %q_hbm.1, s32[]{:T(128)S(6)} %select_n.3), kind=kLoop, calls=%fused_computation | loop fusion | bytes 262148 | tf_op jit(solution)/shard_map/dynamic_slice | solution.py:249
  0.9 4.1 %collective-permute-start = (bf16[16,4096]{1,0:T(8,128)(2,1)S(1)}, bf16[16,4096]{1,0:T(8,128)(2,1)S(1)}, u32[]{:S(2)}, u32[]{:S(2)}) collective-permute-start(bf16[16,4096]{1,0:T(8,128)(2,1)S(1)} %dynamic-slice_bitcast_fusion), channel_id=1, source_target_pairs={{0,8},{4,12},{8,0},{12,4},{1,9},{5,13},{9,1},{13,5},{2,10},{6,14},... | collective-permute-start | bytes 393224 | tf_op jit(solution)/shard_map/ppermute | solution.py:228
  5.0 3.8 %shard_map.55 = (bf16[512,4096]{1,0:T(8,128)(2,1)S(1)}, bf16[64,192]{1,0:T(8,128)(2,1)S(1)}, bf16[64,192]{1,0:T(8,128)(2,1)S(1)}, bf16[256,256]{1,0:T(8,128)(2,1...) custom-call(bf16[1,32,4096]{2,1,0:T(8,128)(2,1)} %q_hbm.1, ...), custom_call_target="tpu_custom_call" | custom-call | flops 4000000000 | bytes 14400000 | tf_op jit(solution)/shard_map/pallas_call | solution.py:139
  8.8 1.6 %collective-permute-start.3 = (bf16[16,4096]{1,0:T(8,128)(2,1)S(1)}, bf16[16,4096]{1,0:T(8,128)(2,1)S(1)}, u32[]{:S(2)}, u32[]{:S(2)}) collective-permute-start(bf16[16,4096]{1,0:T(8,128)(2,1)S(1)} %get-tuple-element.25.refs_0_), channel_id=1, source_target_pairs={{0,4},{4,0},{8,12},{12,8},{1,5},{5,1},{9,13},{13,9},{2,6},{6,2},{1... | collective-permute-start | bytes 393224 | tf_op jit(solution)/shard_map/ppermute | solution.py:228
  10.5 0.9 %collective-permute-done.chunk = bf16[16,4096]{1,0:T(8,128)(2,1)S(1)} collective-permute-done((bf16[16,4096]{1,0:T(8,128)(2,1)S(1)}, bf16[16,4096]{1,0:T(8,128)(2,1)S(1)}, u32[]{:S(2)}, u32[]{:S(2)}) %collective-permute-start) | collective-permute-done | bytes 131104 | tf_op jit(solution)/shard_map/ppermute | solution.py:228
  11.4 1.1 %shard_map.56.refs_4_ = bf16[16,4096]{1,0:T(8,128)(2,1)S(1)} custom-call(bf16[16,4096]{1,0:T(8,128)(2,1)S(1)} %collective-permute-done.chunk, bf16[64,192]{1,0:T(8,128)(2,1)S(1)} %get-tuple-element.19.lin, bf16[64,192]{1,0:T(8,128)(2,1)S(1)} %get-tuple-element.20.lout, bf16[256,256]{1,0:T(8,128)(2,1)S(1)} %get-tuple-element.21.fst, ...), custom_call_target="tpu_custom_call" | custom-call | flops 1333333376 | bytes 4800000 | tf_op jit(solution)/shard_map/pallas_call | solution.py:163
  12.4 0.8 %collective-permute-start.1 = (bf16[16,4096]{1,0:T(8,128)(2,1)S(1)}, bf16[16,4096]{1,0:T(8,128)(2,1)S(1)}, u32[]{:S(2)}, u32[]{:S(2)}) collective-permute-start(bf16[16,4096]{1,0:T(8,128)(2,1)S(1)} %shard_map.56.refs_4_), channel_id=1, source_target_pairs={{0,4},{4,0},{8,12},{12,8},{1,5},{5,1},{9,13},{13,9},{2,6},{6,2},{1... | collective-permute-start | bytes 393224 | tf_op jit(solution)/shard_map/ppermute | solution.py:228
  13.2 1.3 %collective-permute-start.4 = (bf16[16,4096]{1,0:T(8,128)(2,1)S(1)}, bf16[16,4096]{1,0:T(8,128)(2,1)S(1)}, u32[]{:S(2)}, u32[]{:S(2)}) collective-permute-start(bf16[16,4096]{1,0:T(8,128)(2,1)S(1)} %get-tuple-element.27.refs_1_), channel_id=1, source_target_pairs={{0,4},{4,0},{8,12},{12,8},{1,5},{5,1},{9,13},{13,9},{2,6},{6,2},{1... | collective-permute-start | bytes 393224 | tf_op jit(solution)/shard_map/ppermute | solution.py:228
  14.5 1.6 %collective-permute-start.5 = (bf16[16,4096]{1,0:T(8,128)(2,1)S(1)}, bf16[16,4096]{1,0:T(8,128)(2,1)S(1)}, u32[]{:S(2)}, u32[]{:S(2)}) collective-permute-start(bf16[16,4096]{1,0:T(8,128)(2,1)S(1)} %shard_map.56.refs_4_), channel_id=1, source_target_pairs={{0,16},{16,0},{1,17},{17,1},{2,18},{18,2},{3,19},{19,3},{4,20},{20... | collective-permute-start | bytes 393224 | tf_op jit(solution)/shard_map/ppermute | solution.py:228
  16.1 2.5 %collective-permute-done.1.refs_6_ = bf16[16,4096]{1,0:T(8,128)(2,1)S(1)} collective-permute-done((bf16[16,4096]{1,0:T(8,128)(2,1)S(1)}, bf16[16,4096]{1,0:T(8,128)(2,1)S(1)}, u32[]{:S(2)}, u32[]{:S(2)}) %collective-permute-start.1) | collective-permute-done | bytes 131104 | tf_op jit(solution)/shard_map/ppermute | solution.py:228
  18.5 1.4 %collective-permute-start.2 = (bf16[16,4096]{1,0:T(8,128)(2,1)S(1)}, bf16[16,4096]{1,0:T(8,128)(2,1)S(1)}, u32[]{:S(2)}, u32[]{:S(2)}) collective-permute-start(bf16[16,4096]{1,0:T(8,128)(2,1)S(1)} %collective-permute-done.1.refs_6_), channel_id=1, source_target_pairs={{0,16},{16,0},{1,17},{17,1},{2,18},{18,2},{3,19},{19,3},{4,20},{20... | collective-permute-start | bytes 393224 | tf_op jit(solution)/shard_map/ppermute | solution.py:228
  19.9 0.0 collective-permute-done.3.refs_2_
  19.9 0.0 collective-permute-done.4.refs_3_
  19.9 0.9 %collective-permute-done.5.refs_5_ = bf16[16,4096]{1,0:T(8,128)(2,1)S(1)} collective-permute-done((bf16[16,4096]{1,0:T(8,128)(2,1)S(1)}, bf16[16,4096]{1,0:T(8,128)(2,1)S(1)}, u32[]{:S(2)}, u32[]{:S(2)}) %collective-permute-start.5) | collective-permute-done | bytes 131104 | tf_op jit(solution)/shard_map/ppermute | solution.py:228
  20.8 1.3 %shard_map.57.part = f32[112,512]{1,0:T(8,128)S(1)} custom-call(bf16[16,4096]{1,0:T(8,128)(2,1)S(1)} %get-tuple-element.25.refs_0_, bf16[16,4096]{1,0:T(8,128)(2,1)S(1)} %get-tuple-element.27.refs_1_, bf16[16,4096]{1,0:T(8,128)(2,1)S(1)} %collective-permute-done.3.refs_2_, bf16[16,4096]{1,0:T(8,128)(2,1)S(1)} %collective-permute-done.4.refs_3_, ...), custom_call_target="tpu_custom_call" | custom-call | flops 1500000000 | bytes 5400000 | tf_op jit(solution)/shard_map/pallas_call | solution.py:183
  22.1 1.4 %collective-permute-done.2.far2 = bf16[16,4096]{1,0:T(8,128)(2,1)S(1)} collective-permute-done((bf16[16,4096]{1,0:T(8,128)(2,1)S(1)}, bf16[16,4096]{1,0:T(8,128)(2,1)S(1)}, u32[]{:S(2)}, u32[]{:S(2)}) %collective-permute-start.2) | collective-permute-done | bytes 131104 | tf_op jit(solution)/shard_map/ppermute | solution.py:228
  23.5 1.3 %shard_map.58 = (f32[32,512]{1,0:T(8,128)S(1)}, f32[32,512]{1,0:T(8,128)S(1)}, bf16[32,512]{1,0:T(8,128)(2,1)S(1)}, bf16[32,512]{1,0:T(8,128)(2,1)S(1)}) custom-call(bf16[16,4096]{1,0:T(8,128)(2,1)S(1)} %collective-permute-done.2.far2, bf16[512,4096]{1,0:T(8,128)(2,1)S(1)} %get-tuple-element.24.refs_7_.tv, f32[112,512]{1,0:T(8,128)S(1)} %shard_map.57.part), custom_call_target="tpu_custom_call" | custom-call | flops 1300000000 | bytes 4680000 | tf_op jit(solution)/shard_map/pallas_call | solution.py:214
  24.8 0.1 collective-permute-start.6
  24.9 1.4 %collective-permute-start.7 = (bf16[32,512]{1,0:T(8,128)(2,1)S(1)}, bf16[32,512]{1,0:T(8,128)(2,1)S(1)}, u32[]{:S(2)}, u32[]{:S(2)}) collective-permute-start(bf16[32,512]{1,0:T(8,128)(2,1)S(1)} %get-tuple-element.31), channel_id=1, source_target_pairs={{0,2},{1,3},{2,0},{3,1},{4,6},{5,7},{6,4},{7,5},{8,10},{9,11},{10,... | collective-permute-start | bytes 98312 | tf_op jit(solution)/shard_map/ppermute | solution.py:228
  26.3 0.4 %collective-permute-start.8 = (bf16[32,512]{1,0:T(8,128)(2,1)S(1)}, bf16[32,512]{1,0:T(8,128)(2,1)S(1)}, u32[]{:S(2)}, u32[]{:S(2)}) collective-permute-start(bf16[32,512]{1,0:T(8,128)(2,1)S(1)} %get-tuple-element.32), channel_id=1, source_target_pairs={{0,3},{1,2},{2,1},{3,0},{4,7},{5,6},{6,5},{7,4},{8,11},{9,10},{10,... | collective-permute-start | bytes 98312 | tf_op jit(solution)/shard_map/ppermute | solution.py:228
  26.7 2.1 %collective-permute-done.7 = bf16[32,512]{1,0:T(8,128)(2,1)S(1)} collective-permute-done((bf16[32,512]{1,0:T(8,128)(2,1)S(1)}, bf16[32,512]{1,0:T(8,128)(2,1)S(1)}, u32[]{:S(2)}, u32[]{:S(2)}) %collective-permute-start.7) | collective-permute-done | bytes 32800 | tf_op jit(solution)/shard_map/ppermute | solution.py:228
  28.9 0.8 %collective-permute-done.8 = bf16[32,512]{1,0:T(8,128)(2,1)S(1)} collective-permute-done((bf16[32,512]{1,0:T(8,128)(2,1)S(1)}, bf16[32,512]{1,0:T(8,128)(2,1)S(1)}, u32[]{:S(2)}, u32[]{:S(2)}) %collective-permute-start.8) | collective-permute-done | bytes 32800 | tf_op jit(solution)/shard_map/ppermute | solution.py:228
  29.6 0.0 collective-permute-done.6
  29.6 0.6 %add_bitcast_fusion = f32[512,32]{0,1:T(8,128)} fusion(bf16[32,512]{1,0:T(8,128)(2,1)S(1)} %collective-permute-done.8, bf16[32,512]{1,0:T(8,128)(2,1)S(1)} %collective-permute-done.7, f32[32,512]{1,0:T(8,128)S(1)} %get-tuple-element.29, f32[32,512]{1,0:T(8,128)S(1)} %collective-permute-done.6), kind=kLoop, calls=%fused_computation.1 | loop fusion | flops 81920 | bytes 262144 | tf_op jit(solution)/shard_map/transpose | solution.py:264
Async XLA Ops:
  0.9 10.4 %collective-permute-start = (bf16[16,4096]{1,0:T(8,128)(2,1)S(1)}, bf16[16,4096]{1,0:T(8,128)(2,1)S(1)}, u32[]{:S(2)}, u32[]{:S(2)}) collective-permute-start(bf16[16,4096]{1,0:T(8,128)(2,1)S(1)} %dynamic-slice_bitcast_fusion), channel_id=1, source_target_pairs={{0,8},{4,12},{8,0},{12,4},{1,9},{5,13},{9,1},{13,5},{2,10},{6,14},... | collective-permute-start | bytes 393224 | tf_op jit(solution)/shard_map/ppermute | solution.py:228
  8.8 11.1 %collective-permute-start.3 = (bf16[16,4096]{1,0:T(8,128)(2,1)S(1)}, bf16[16,4096]{1,0:T(8,128)(2,1)S(1)}, u32[]{:S(2)}, u32[]{:S(2)}) collective-permute-start(bf16[16,4096]{1,0:T(8,128)(2,1)S(1)} %get-tuple-element.25.refs_0_), channel_id=1, source_target_pairs={{0,4},{4,0},{8,12},{12,8},{1,5},{5,1},{9,13},{13,9},{2,6},{6,2},{1... | collective-permute-start | bytes 393224 | tf_op jit(solution)/shard_map/ppermute | solution.py:228
  12.4 6.1 %collective-permute-start.1 = (bf16[16,4096]{1,0:T(8,128)(2,1)S(1)}, bf16[16,4096]{1,0:T(8,128)(2,1)S(1)}, u32[]{:S(2)}, u32[]{:S(2)}) collective-permute-start(bf16[16,4096]{1,0:T(8,128)(2,1)S(1)} %shard_map.56.refs_4_), channel_id=1, source_target_pairs={{0,4},{4,0},{8,12},{12,8},{1,5},{5,1},{9,13},{13,9},{2,6},{6,2},{1... | collective-permute-start | bytes 393224 | tf_op jit(solution)/shard_map/ppermute | solution.py:228
  13.2 6.7 %collective-permute-start.4 = (bf16[16,4096]{1,0:T(8,128)(2,1)S(1)}, bf16[16,4096]{1,0:T(8,128)(2,1)S(1)}, u32[]{:S(2)}, u32[]{:S(2)}) collective-permute-start(bf16[16,4096]{1,0:T(8,128)(2,1)S(1)} %get-tuple-element.27.refs_1_), channel_id=1, source_target_pairs={{0,4},{4,0},{8,12},{12,8},{1,5},{5,1},{9,13},{13,9},{2,6},{6,2},{1... | collective-permute-start | bytes 393224 | tf_op jit(solution)/shard_map/ppermute | solution.py:228
  14.5 6.3 %collective-permute-start.5 = (bf16[16,4096]{1,0:T(8,128)(2,1)S(1)}, bf16[16,4096]{1,0:T(8,128)(2,1)S(1)}, u32[]{:S(2)}, u32[]{:S(2)}) collective-permute-start(bf16[16,4096]{1,0:T(8,128)(2,1)S(1)} %shard_map.56.refs_4_), channel_id=1, source_target_pairs={{0,16},{16,0},{1,17},{17,1},{2,18},{18,2},{3,19},{19,3},{4,20},{20... | collective-permute-start | bytes 393224 | tf_op jit(solution)/shard_map/ppermute | solution.py:228
  18.5 5.0 %collective-permute-start.2 = (bf16[16,4096]{1,0:T(8,128)(2,1)S(1)}, bf16[16,4096]{1,0:T(8,128)(2,1)S(1)}, u32[]{:S(2)}, u32[]{:S(2)}) collective-permute-start(bf16[16,4096]{1,0:T(8,128)(2,1)S(1)} %collective-permute-done.1.refs_6_), channel_id=1, source_target_pairs={{0,16},{16,0},{1,17},{17,1},{2,18},{18,2},{3,19},{19,3},{4,20},{20... | collective-permute-start | bytes 393224 | tf_op jit(solution)/shard_map/ppermute | solution.py:228
  24.8 4.8 %collective-permute-start.6 = (f32[32,512]{1,0:T(8,128)S(1)}, f32[32,512]{1,0:T(8,128)S(1)}, u32[]{:S(2)}, u32[]{:S(2)}) collective-permute-start(f32[32,512]{1,0:T(8,128)S(1)} %get-tuple-element.30), channel_id=1, source_target_pairs={{0,1},{1,0},{2,3},{3,2},{4,5},{5,4},{6,7},{7,6},{8,9},{9,8},{10,11... | collective-permute-start | bytes 196616 | tf_op jit(solution)/shard_map/ppermute | solution.py:228
  24.9 4.0 %collective-permute-start.7 = (bf16[32,512]{1,0:T(8,128)(2,1)S(1)}, bf16[32,512]{1,0:T(8,128)(2,1)S(1)}, u32[]{:S(2)}, u32[]{:S(2)}) collective-permute-start(bf16[32,512]{1,0:T(8,128)(2,1)S(1)} %get-tuple-element.31), channel_id=1, source_target_pairs={{0,2},{1,3},{2,0},{3,1},{4,6},{5,7},{6,4},{7,5},{8,10},{9,11},{10,... | collective-permute-start | bytes 98312 | tf_op jit(solution)/shard_map/ppermute | solution.py:228
  26.3 3.3 %collective-permute-start.8 = (bf16[32,512]{1,0:T(8,128)(2,1)S(1)}, bf16[32,512]{1,0:T(8,128)(2,1)S(1)}, u32[]{:S(2)}, u32[]{:S(2)}) collective-permute-start(bf16[32,512]{1,0:T(8,128)(2,1)S(1)} %get-tuple-element.32), channel_id=1, source_target_pairs={{0,3},{1,2},{2,1},{3,0},{4,7},{5,6},{6,5},{7,4},{8,11},{9,10},{10,... | collective-permute-start | bytes 98312 | tf_op jit(solution)/shard_map/ppermute | solution.py:228

commit v5 on v4

--- a/solution.py
+++ b/solution.py
@@ -88,7 +88,7 @@
     return dot(train, ready, 1, 1).T * (1.0 / math.sqrt(GR * GC))
 
 
-def first_kernel(nq, q_hbm, bo_hbm, bi_hbm, ev_hbm, train_hbm, tv, lin, lout, fst, lst, rec, out_a, out_b, qv, bov, biv, evv, xa, xb, os, sem):
+def first_kernel(nq, q_hbm, bo_hbm, bi_hbm, ev_hbm, train_hbm, tv, out, lin, lout, fst, lst, rec, qv, bov, biv, evv, xa, xb, os, sem):
     copies = [
         pltpu.make_async_copy(a, b, sem.at[i])
         for i, (a, b) in enumerate(((bo_hbm, bov), (bi_hbm, biv), (ev_hbm, evv), (q_hbm, qv), (train_hbm.at[0], tv)))
@@ -103,9 +103,7 @@
     fst[...], lst[...] = col_maps(biv[0])
 
     def put(t, v):
-        v = v.astype(BF16)
-        out_a[:, t * 128:t * 128 + 128] = v[:16]
-        out_b[:, t * 128:t * 128 + 128] = v[16:]
+        out[:, t * 128:t * 128 + 128] = v.astype(BF16)
 
     prep_body(nq, lambda t: qv[0, :, t * 128:t * 128 + 128], put, lin[...], lout[...], fst[...], lst[...], rec[...], xa, xb, os, 16)
     copies[4].wait()
@@ -135,18 +133,15 @@
 def first(*args):
     q, bo, bi, ev, train = args
     nq = q.shape[1]
-    n, f = train.shape[1:]
     return pl.pallas_call(
         functools.partial(first_kernel, nq),
-        out_shape=[jax.ShapeDtypeStruct((n, f), BF16)] + maps_shapes() + [jax.ShapeDtypeStruct((16, f), BF16)] * 2,
+        out_shape=[jax.ShapeDtypeStruct(x.shape[1:], BF16) for x in (train, q)] + maps_shapes(),
         in_specs=[pl.BlockSpec(memory_space=pltpu.HBM)] * 5,
-        out_specs=[VM] * 8,
-        scratch_shapes=[
-            pltpu.VMEM(q.shape, BF16),
-            pltpu.VMEM(bo.shape, F32),
-            pltpu.VMEM(bi.shape, F32),
-            pltpu.VMEM(ev.shape, F32),
-        ] + work(nq) + [pltpu.SemaphoreType.DMA((5,))],
+        out_specs=[VM] * 7,
+        scratch_shapes=[pltpu.VMEM(q.shape, BF16)]
+        + [pltpu.VMEM(x.shape, F32) for x in (bo, bi, ev)]
+        + work(nq)
+        + [pltpu.SemaphoreType.DMA((5,))],
         **settings(4),
     )(*(pltpu.with_memory_space_constraint(x, pltpu.HBM) for x in args))
 
@@ -170,27 +165,32 @@
     )(chunk, *maps)
 
 
-def bulk_kernel(*refs):
-    *pieces, tv, part, pv = refs
-    for i, p in enumerate(pieces):
-        pv[i * 16:i * 16 + 16, :] = p[...]
+def bulk_kernel(own, near, mid, tv, lin, lout, fst, lst, rec, part, xa, xb, os, pv):
+    rows = own.shape[0]
+    pv[0:rows, :] = own[...]
+    pv[2 * rows:, :] = mid[...]
+
+    def put(t, v):
+        pv[rows:2 * rows, t * 128:t * 128 + 128] = v.astype(BF16)
+
+    prep_body(rows, lambda t: near[:, t * 128:t * 128 + 128], put, lin[...], lout[...], fst[...], lst[...], rec[...], xa, xb, os, 16)
     part[...] = scores_of(tv[...], pv[...])
 
 
-def bulk(tv, *pieces):
-    n, f = tv.shape
-    rows = 16 * len(pieces)
+def bulk(own, near, mid, tv, maps):
+    rows, f = own.shape
+    n = tv.shape[0]
     return pl.pallas_call(
         bulk_kernel,
-        out_shape=jax.ShapeDtypeStruct((rows, n), F32),
-        in_specs=[VM] * (len(pieces) + 1),
+        out_shape=jax.ShapeDtypeStruct((2 * rows + 16, n), F32),
+        in_specs=[VM] * 9,
         out_specs=VM,
-        scratch_shapes=[pltpu.VMEM((rows, f), BF16)],
-        **settings(1.5),
-    )(*pieces, tv)
-
-
-def last_kernel(far2, tv, part, mine, core, across, both, sv):
+        scratch_shapes=work(rows) + [pltpu.VMEM((2 * rows + 16, f), BF16)],
+        **settings(3.5),
+    )(own, near, mid, tv, *maps)
+
+
+def last_kernel(mid2, far, far2, tv, part, mine, core, across, both, pv, sv):
     half = 16 * lax.axis_index("grp")
     other = 16 - half
     rows = mine.shape[0]
@@ -201,24 +201,27 @@
 
     sv[at(0, 0, rows), :] = part[0:rows, :]
     sv[at(1, 0, rows), :] = part[rows:2 * rows, :]
-    sv[at(2, half, 16), :] = part[2 * rows:2 * rows + 16, :]
-    sv[at(2, other, 16), :] = part[2 * rows + 16:2 * rows + 32, :]
-    sv[at(3, half, 16), :] = part[2 * rows + 32:, :]
-    sv[at(3, other, 16), :] = scores_of(tv[...], far2[...])
+    sv[at(3, half, 16), :] = part[2 * rows:, :]
+    for i, p in enumerate((mid2, far, far2)):
+        pv[i * 16:i * 16 + 16, :] = p[...]
+    late = scores_of(tv[...], pv[...])
+    sv[at(3, other, 16), :] = late[0:16]
+    sv[at(2, half, 16), :] = late[16:32]
+    sv[at(2, other, 16), :] = late[32:48]
     for m, o in enumerate((mine, core, across, both)):
         o[...] = sv[m * rows:m * rows + rows, :].astype(o.dtype)
 
 
-def final(far2, tv, part, rows):
+def final(mid2, far, far2, tv, part, rows):
     n, f = tv.shape
     return pl.pallas_call(
         last_kernel,
         out_shape=[jax.ShapeDtypeStruct((rows, n), d) for d in (F32, F32, SENT, SENT)],
-        in_specs=[VM] * 3,
+        in_specs=[VM] * 5,
         out_specs=[VM] * 4,
-        scratch_shapes=[pltpu.VMEM((4 * rows, n), F32)],
+        scratch_shapes=[pltpu.VMEM((48, f), BF16), pltpu.VMEM((4 * rows, n), F32)],
         **settings(1.3),
-    )(far2, tv, part)
+    )(mid2, far, far2, tv, part)
 
 
 SENT = BF16
@@ -247,18 +250,15 @@
         return plain(sizes, train, query, bo, bi, ev)
     start = 16 * lax.axis_index("grp")
     half = lax.dynamic_slice_in_dim(query[0], start, 16, 0)
-    mid = flip(half, "ex", 2, 4)
-    tv, *rest = first(query, bo, bi, ev, train)
-    maps, own_a, own_b = rest[:5], rest[5], rest[6]
-    near_a = flip(own_a, "ex", 1, 4)
+    mid = flip(half, "ex", 3, 4)
+    near = flip(query[0], "ex", 1, 4)
+    tv, own, *maps = first(query, bo, bi, ev, train)
     mid = following(mid, maps)
+    mid2 = flip(mid, "grp", 1, 2)
     far = flip(mid, "ex", 1, 4)
-    mid2 = flip(mid, "grp", 1, 2)
-    own_b, mid = lax.optimization_barrier((own_b, mid))
-    near_b = flip(own_b, "ex", 1, 4)
-    far2 = flip(far, "grp", 1, 2)
-    part = bulk(tv, own_a, own_b, near_a, near_b, mid, mid2, far)
-    mine, core, across, both = final(far2, tv, part, query.shape[1])
+    far2 = lax.ppermute(mid, ("grp", "ex"), [(g * 4 + z, (1 - g) * 4 + (z ^ 1)) for g in range(2) for z in range(4)])
+    part = bulk(own, near, mid, tv, maps)
+    mine, core, across, both = final(mid2, far, far2, tv, part, query.shape[1])
     total = mine + flip(core, "lyr", 1, 4)
     total = total + flip(across, "lyr", 2, 4).astype(F32) + flip(both, "lyr", 3, 4).astype(F32)
     return total.T

time: 30.4 us -> 28.3 us (0.931)
  waiting for transfers between devices: 8.52 us -> 6.09 us
  Pallas kernels: 7.43 us -> 9.83 us
  starting transfers between devices: 12.7 us -> 10.6 us
    ppermute x9 -> x7, starting transfers between devices: 12.7 us -> 7.94 us  [flip(): return lax.ppermute(x, axis, [(i, i ^ mask) for i in range(size)])]
    ppermute x9 -> x7, waiting for transfers between devices: 8.52 us -> 5.84 us  [flip(): return lax.ppermute(x, axis, [(i, i ^ mask) for i in range(size)])]
    ppermute x0 -> x1, starting transfers between devices: none -> 2.67 us  [local(): lax.ppermute(mid, ('grp', 'ex'), [(g * 4 + z, (1 - g) * 4 + (z ^ 1)) for...]
    pallas_call x1, Pallas kernels: 1.3 us -> 3.65 us  [bulk(): pl.pallas_call(bulk_kernel, out_shape=jax.ShapeDtypeStruct((2 * rows + 16...]
  transfers between devices with their start and end apart: 9 -> 8, of which waited for: 6 -> 7; matrix products, arithmetic and copies ran while one was open for 0% -> 0% of each run, Pallas kernels for 20% -> 30%
where the time goes in v5:
time: 28.3 us; the launch traced here: 28.1 us
  starting transfers between devices  10.6 us (37%)
  Pallas kernels  9.83 us (35%)
  waiting for transfers between devices  6.09 us (22%)
  local copies, waits for them, and re-layouts  0.91 us (3%)
  other arithmetic  0.65 us (2%)
    ppermute x7, starting transfers between devices, flip(): return lax.ppermute(x, axis, [(i, i ^ mask) for i in range(size)])  7.94 us
    ppermute x7, waiting for transfers between devices, flip(): return lax.ppermute(x, axis, [(i, i ^ mask) for i in range(size)])  5.84 us
    pallas_call x1, Pallas kernels, first(): pl.pallas_call(functools.partial(first_kernel, nq), out_shape=[jax.ShapeD...  3.83 us
    pallas_call x1, Pallas kernels, bulk(): pl.pallas_call(bulk_kernel, out_shape=jax.ShapeDtypeStruct((2 * rows + 16...  3.65 us
    ppermute x1, starting transfers between devices, local(): lax.ppermute(mid, ('grp', 'ex'), [(g * 4 + z, (1 - g) * 4 + (z ^ 1)) for...  2.67 us
    pallas_call x1, Pallas kernels, final(): pl.pallas_call(last_kernel, out_shape=[jax.ShapeDtypeStruct((rows, n), d)...  1.29 us
    pallas_call x1, Pallas kernels, following(): pl.pallas_call(functools.partial(next_kernel, nq), out_shape=jax.ShapeDty...  1.06 us
    dynamic_slice x1, local copies, waits for them, and re-layouts, local(): half = lax.dynamic_slice_in_dim(query[0], start, 16, 0)  0.91 us
  transfers between devices with their start and end apart: 8, of which 7 were waited for; matrix products, arithmetic and copies ran while one was open for 0% of the time, Pallas kernels for 30%

profile of v5, /device:TPU:0, one launch (start us, length us, event | category | flops | bytes accessed | tf_op | source)
XLA Modules:
  0.0 28.1 jit_solution(13917815988905382849)
XLA Ops:
  0.0 0.9 %dynamic-slice_bitcast_fusion = bf16[16,4096]{1,0:T(8,128)(2,1)S(1)} fusion(bf16[1,32,4096]{2,1,0:T(8,128)(2,1)} %q_hbm.1, s32[]{:T(128)S(6)} %select_n.3), kind=kLoop, calls=%fused_computation | loop fusion | bytes 262148 | tf_op jit(solution)/shard_map/dynamic_slice | solution.py:252
  0.9 5.1 %collective-permute-start = (bf16[16,4096]{1,0:T(8,128)(2,1)S(1)}, bf16[16,4096]{1,0:T(8,128)(2,1)S(1)}, u32[]{:S(2)}, u32[]{:S(2)}) collective-permute-start(bf16[16,4096]{1,0:T(8,128)(2,1)S(1)} %dynamic-slice_bitcast_fusion), channel_id=1, source_target_pairs={{0,12},{4,8},{8,4},{12,0},{1,13},{5,9},{9,5},{13,1},{2,14},{6,10},... | collective-permute-start | bytes 393224 | tf_op jit(solution)/shard_map/ppermute | solution.py:231
  6.0 0.0 collective-permute-start.4
  6.0 3.8 %shard_map.55 = (bf16[512,4096]{1,0:T(8,128)(2,1)S(1)}, bf16[32,4096]{1,0:T(8,128)(2,1)S(1)}, bf16[64,192]{1,0:T(8,128)(2,1)S(1)}, bf16[64,192]{1,0:T(8,128)(2,1...) custom-call(bf16[1,32,4096]{2,1,0:T(8,128)(2,1)} %q_hbm.1, ...), custom_call_target="tpu_custom_call" | custom-call | flops 4000000000 | bytes 14400000 | tf_op jit(solution)/shard_map/pallas_call | solution.py:136
  9.9 0.5 %collective-permute-done.chunk = bf16[16,4096]{1,0:T(8,128)(2,1)S(1)} collective-permute-done((bf16[16,4096]{1,0:T(8,128)(2,1)S(1)}, bf16[16,4096]{1,0:T(8,128)(2,1)S(1)}, u32[]{:S(2)}, u32[]{:S(2)}) %collective-permute-start) | collective-permute-done | bytes 131104 | tf_op jit(solution)/shard_map/ppermute | solution.py:231
  10.4 1.1 %shard_map.56.mid = bf16[16,4096]{1,0:T(8,128)(2,1)S(1)} custom-call(bf16[16,4096]{1,0:T(8,128)(2,1)S(1)} %collective-permute-done.chunk, bf16[64,192]{1,0:T(8,128)(2,1)S(1)} %get-tuple-element.16.lin, bf16[64,192]{1,0:T(8,128)(2,1)S(1)} %get-tuple-element.17.lout, bf16[256,256]{1,0:T(8,128)(2,1)S(1)} %get-tuple-element.18.fst, ...), custom_call_target="tpu_custom_call" | custom-call | flops 1333333376 | bytes 4800000 | tf_op jit(solution)/shard_map/pallas_call | solution.py:158
  11.5 2.7 %collective-permute-start.3 = (bf16[16,4096]{1,0:T(8,128)(2,1)S(1)}, bf16[16,4096]{1,0:T(8,128)(2,1)S(1)}, u32[]{:S(2)}, u32[]{:S(2)}) collective-permute-start(bf16[16,4096]{1,0:T(8,128)(2,1)S(1)} %shard_map.56.mid), channel_id=1, source_target_pairs={{0,20},{4,16},{8,28},{12,24},{16,4},{20,0},{24,12},{28,8},{1,21},{... | collective-permute-start | bytes 393224 | tf_op jit(solution)/shard_map/ppermute | solution.py:259
  14.1 0.6 %collective-permute-start.2 = (bf16[16,4096]{1,0:T(8,128)(2,1)S(1)}, bf16[16,4096]{1,0:T(8,128)(2,1)S(1)}, u32[]{:S(2)}, u32[]{:S(2)}) collective-permute-start(bf16[16,4096]{1,0:T(8,128)(2,1)S(1)} %shard_map.56.mid), channel_id=1, source_target_pairs={{0,4},{4,0},{8,12},{12,8},{1,5},{5,1},{9,13},{13,9},{2,6},{6,2},{1... | collective-permute-start | bytes 393224 | tf_op jit(solution)/shard_map/ppermute | solution.py:231
  14.7 0.3 %collective-permute-start.1 = (bf16[16,4096]{1,0:T(8,128)(2,1)S(1)}, bf16[16,4096]{1,0:T(8,128)(2,1)S(1)}, u32[]{:S(2)}, u32[]{:S(2)}) collective-permute-start(bf16[16,4096]{1,0:T(8,128)(2,1)S(1)} %shard_map.56.mid), channel_id=1, source_target_pairs={{0,16},{16,0},{1,17},{17,1},{2,18},{18,2},{3,19},{19,3},{4,20},{20... | collective-permute-start | bytes 393224 | tf_op jit(solution)/shard_map/ppermute | solution.py:231
  15.0 0.8 %collective-permute-done.4.near = bf16[32,4096]{1,0:T(8,128)(2,1)S(1)} collective-permute-done((bf16[32,4096]{1,0:T(8,128)(2,1)}, bf16[32,4096]{1,0:T(8,128)(2,1)S(1)}, u32[]{:S(2)}, u32[]{:S(2)}) %collective-permute-start.4) | collective-permute-done | bytes 262176 | tf_op jit(solution)/shard_map/ppermute | solution.py:231
  15.8 3.7 %shard_map.57.part = f32[80,512]{1,0:T(8,128)S(1)} custom-call(bf16[32,4096]{1,0:T(8,128)(2,1)S(1)} %get-tuple-element.22.own, bf16[32,4096]{1,0:T(8,128)(2,1)S(1)} %collective-permute-done.4.near, bf16[16,4096]{1,0:T(8,128)(2,1)S(1)} %shard_map.56.mid, bf16[512,4096]{1,0:T(8,128)(2,1)S(1)} %get-tuple-element.21.tv, ...), custom_call_target="tpu_custom_call" | custom-call | flops 3500000000 | bytes 12600000 | tf_op jit(solution)/shard_map/pallas_call | solution.py:183
  19.4 0.3 collective-permute-done.3.far2
  19.7 1.2 %collective-permute-done.2.far = bf16[16,4096]{1,0:T(8,128)(2,1)S(1)} collective-permute-done((bf16[16,4096]{1,0:T(8,128)(2,1)S(1)}, bf16[16,4096]{1,0:T(8,128)(2,1)S(1)}, u32[]{:S(2)}, u32[]{:S(2)}) %collective-permute-start.2) | collective-permute-done | bytes 131104 | tf_op jit(solution)/shard_map/ppermute | solution.py:231
  20.9 0.3 %collective-permute-done.1.mid2 = bf16[16,4096]{1,0:T(8,128)(2,1)S(1)} collective-permute-done((bf16[16,4096]{1,0:T(8,128)(2,1)S(1)}, bf16[16,4096]{1,0:T(8,128)(2,1)S(1)}, u32[]{:S(2)}, u32[]{:S(2)}) %collective-permute-start.1) | collective-permute-done | bytes 131104 | tf_op jit(solution)/shard_map/ppermute | solution.py:231
  21.2 1.3 %shard_map.58 = (f32[32,512]{1,0:T(8,128)S(1)}, f32[32,512]{1,0:T(8,128)S(1)}, bf16[32,512]{1,0:T(8,128)(2,1)S(1)}, bf16[32,512]{1,0:T(8,128)(2,1)S(1)}) custom-call(bf16[16,4096]{1,0:T(8,128)(2,1)S(1)} %collective-permute-done.1.mid2, bf16[16,4096]{1,0:T(8,128)(2,1)S(1)} %collective-permute-done.2.far, bf16[16,4096]{1,0:T(8,128)(2,1)S(1)} %collective-permute-done.3.far2, ...), custom_call_target="tpu_custom_call" | custom-call | flops 1300000000 | bytes 4680000 | tf_op jit(solution)/shard_map/pallas_call | solution.py:217
  22.5 0.1 collective-permute-start.5
  22.6 1.6 %collective-permute-start.6 = (bf16[32,512]{1,0:T(8,128)(2,1)S(1)}, bf16[32,512]{1,0:T(8,128)(2,1)S(1)}, u32[]{:S(2)}, u32[]{:S(2)}) collective-permute-start(bf16[32,512]{1,0:T(8,128)(2,1)S(1)} %get-tuple-element.25), channel_id=1, source_target_pairs={{0,2},{1,3},{2,0},{3,1},{4,6},{5,7},{6,4},{7,5},{8,10},{9,11},{10,... | collective-permute-start | bytes 98312 | tf_op jit(solution)/shard_map/ppermute | solution.py:231
  24.1 0.3 %collective-permute-start.7 = (bf16[32,512]{1,0:T(8,128)(2,1)S(1)}, bf16[32,512]{1,0:T(8,128)(2,1)S(1)}, u32[]{:S(2)}, u32[]{:S(2)}) collective-permute-start(bf16[32,512]{1,0:T(8,128)(2,1)S(1)} %get-tuple-element.26), channel_id=1, source_target_pairs={{0,3},{1,2},{2,1},{3,0},{4,7},{5,6},{6,5},{7,4},{8,11},{9,10},{10,... | collective-permute-start | bytes 98312 | tf_op jit(solution)/shard_map/ppermute | solution.py:231
  24.4 2.1 %collective-permute-done.6 = bf16[32,512]{1,0:T(8,128)(2,1)S(1)} collective-permute-done((bf16[32,512]{1,0:T(8,128)(2,1)S(1)}, bf16[32,512]{1,0:T(8,128)(2,1)S(1)}, u32[]{:S(2)}, u32[]{:S(2)}) %collective-permute-start.6) | collective-permute-done | bytes 32800 | tf_op jit(solution)/shard_map/ppermute | solution.py:231
  26.6 0.9 %collective-permute-done.7 = bf16[32,512]{1,0:T(8,128)(2,1)S(1)} collective-permute-done((bf16[32,512]{1,0:T(8,128)(2,1)S(1)}, bf16[32,512]{1,0:T(8,128)(2,1)S(1)}, u32[]{:S(2)}, u32[]{:S(2)}) %collective-permute-start.7) | collective-permute-done | bytes 32800 | tf_op jit(solution)/shard_map/ppermute | solution.py:231
  27.5 0.0 collective-permute-done.5
  27.5 0.6 %add_bitcast_fusion = f32[512,32]{0,1:T(8,128)} fusion(bf16[32,512]{1,0:T(8,128)(2,1)S(1)} %collective-permute-done.7, bf16[32,512]{1,0:T(8,128)(2,1)S(1)} %collective-permute-done.6, f32[32,512]{1,0:T(8,128)S(1)} %get-tuple-element.23, f32[32,512]{1,0:T(8,128)S(1)} %collective-permute-done.5), kind=kLoop, calls=%fused_computation.1 | loop fusion | flops 81920 | bytes 262144 | tf_op jit(solution)/shard_map/transpose | solution.py:264
Async XLA Ops:
  0.9 9.5 %collective-permute-start = (bf16[16,4096]{1,0:T(8,128)(2,1)S(1)}, bf16[16,4096]{1,0:T(8,128)(2,1)S(1)}, u32[]{:S(2)}, u32[]{:S(2)}) collective-permute-start(bf16[16,4096]{1,0:T(8,128)(2,1)S(1)} %dynamic-slice_bitcast_fusion), channel_id=1, source_target_pairs={{0,12},{4,8},{8,4},{12,0},{1,13},{5,9},{9,5},{13,1},{2,14},{6,10},... | collective-permute-start | bytes 393224 | tf_op jit(solution)/shard_map/ppermute | solution.py:231
  6.0 9.7 %collective-permute-start.4 = (bf16[32,4096]{1,0:T(8,128)(2,1)}, bf16[32,4096]{1,0:T(8,128)(2,1)S(1)}, u32[]{:S(2)}, u32[]{:S(2)}) collective-permute-start(bf16[32,4096]{1,0:T(8,128)(2,1)} %bitcast.5), channel_id=1, source_target_pairs={{0,4},{4,0},{8,12},{12,8},{1,5},{5,1},{9,13},{13,9},{2,6},{6,2},{1... | collective-permute-start | bytes 786440 | tf_op jit(solution)/shard_map/ppermute | solution.py:231
  11.5 8.2 %collective-permute-start.3 = (bf16[16,4096]{1,0:T(8,128)(2,1)S(1)}, bf16[16,4096]{1,0:T(8,128)(2,1)S(1)}, u32[]{:S(2)}, u32[]{:S(2)}) collective-permute-start(bf16[16,4096]{1,0:T(8,128)(2,1)S(1)} %shard_map.56.mid), channel_id=1, source_target_pairs={{0,20},{4,16},{8,28},{12,24},{16,4},{20,0},{24,12},{28,8},{1,21},{... | collective-permute-start | bytes 393224 | tf_op jit(solution)/shard_map/ppermute | solution.py:259
  14.1 6.8 %collective-permute-start.2 = (bf16[16,4096]{1,0:T(8,128)(2,1)S(1)}, bf16[16,4096]{1,0:T(8,128)(2,1)S(1)}, u32[]{:S(2)}, u32[]{:S(2)}) collective-permute-start(bf16[16,4096]{1,0:T(8,128)(2,1)S(1)} %shard_map.56.mid), channel_id=1, source_target_pairs={{0,4},{4,0},{8,12},{12,8},{1,5},{5,1},{9,13},{13,9},{2,6},{6,2},{1... | collective-permute-start | bytes 393224 | tf_op jit(solution)/shard_map/ppermute | solution.py:231
  14.7 6.5 %collective-permute-start.1 = (bf16[16,4096]{1,0:T(8,128)(2,1)S(1)}, bf16[16,4096]{1,0:T(8,128)(2,1)S(1)}, u32[]{:S(2)}, u32[]{:S(2)}) collective-permute-start(bf16[16,4096]{1,0:T(8,128)(2,1)S(1)} %shard_map.56.mid), channel_id=1, source_target_pairs={{0,16},{16,0},{1,17},{17,1},{2,18},{18,2},{3,19},{19,3},{4,20},{20... | collective-permute-start | bytes 393224 | tf_op jit(solution)/shard_map/ppermute | solution.py:231
  22.5 5.0 %collective-permute-start.5 = (f32[32,512]{1,0:T(8,128)S(1)}, f32[32,512]{1,0:T(8,128)S(1)}, u32[]{:S(2)}, u32[]{:S(2)}) collective-permute-start(f32[32,512]{1,0:T(8,128)S(1)} %get-tuple-element.24), channel_id=1, source_target_pairs={{0,1},{1,0},{2,3},{3,2},{4,5},{5,4},{6,7},{7,6},{8,9},{9,8},{10,11... | collective-permute-start | bytes 196616 | tf_op jit(solution)/shard_map/ppermute | solution.py:231
  22.6 4.0 %collective-permute-start.6 = (bf16[32,512]{1,0:T(8,128)(2,1)S(1)}, bf16[32,512]{1,0:T(8,128)(2,1)S(1)}, u32[]{:S(2)}, u32[]{:S(2)}) collective-permute-start(bf16[32,512]{1,0:T(8,128)(2,1)S(1)} %get-tuple-element.25), channel_id=1, source_target_pairs={{0,2},{1,3},{2,0},{3,1},{4,6},{5,7},{6,4},{7,5},{8,10},{9,11},{10,... | collective-permute-start | bytes 98312 | tf_op jit(solution)/shard_map/ppermute | solution.py:231
  24.1 3.3 %collective-permute-start.7 = (bf16[32,512]{1,0:T(8,128)(2,1)S(1)}, bf16[32,512]{1,0:T(8,128)(2,1)S(1)}, u32[]{:S(2)}, u32[]{:S(2)}) collective-permute-start(bf16[32,512]{1,0:T(8,128)(2,1)S(1)} %get-tuple-element.26), channel_id=1, source_target_pairs={{0,3},{1,2},{2,1},{3,0},{4,7},{5,6},{6,5},{7,4},{8,11},{9,10},{10,... | collective-permute-start | bytes 98312 | tf_op jit(solution)/shard_map/ppermute | solution.py:231

commit v6 on v5

--- a/solution.py
+++ b/solution.py
@@ -59,15 +59,14 @@
     uh, ul = tile(h, 1), tile(l, 1)
     last = jnp.concatenate([pick(uh, same), pick(uh, same), pick(ul, same)], 0)
     return first, last
-def prep_body(nq, get, put, left_in, left_out, first, last, rec, xa, xb, os, group=8):
+def prep_body(nq, get, put, left_in, left_out, first, last, rec, group=16):
     g = jnp.concatenate([get(t) for t in range(32)], 0)
     x = dot(jnp.concatenate([g, g], 1), first)
-    xa[...] = x[:, :128]
-    xb[...] = x[:, 128:]
+    both = [jnp.swapaxes(v.reshape(32, nq, 128), 0, 1) for v in (x[:, :128], x[:, 128:])]
     lane = lax.broadcasted_iota(jnp.int32, (32, 128), 1) < 64
     for q0 in range(0, nq, group):
         qs = range(q0, q0 + group)
-        ww = jnp.concatenate([jnp.concatenate([r[pl.ds(q, 32, stride=nq), :] for q in qs], 1) for r in (xa, xb)], 0)
+        ww = jnp.concatenate([jnp.concatenate([r[q] for q in qs], 1) for r in both], 0)
         h, l = split(ww)
         r = dot(left_in, jnp.concatenate([h, l, h], 0))
         ys, yr = [], []
@@ -80,15 +79,16 @@
         r = dot(left_out, jnp.concatenate([h, l, h], 0))
         z = jnp.concatenate([jnp.where(lane, r[:32, i * 128:i * 128 + 128], r[32:, i * 128:i * 128 + 128]) for i in range(group)], 0)
         h, l = split(z)
-        os[pl.ds(q0 * 32, group * 32), :] = dot(jnp.concatenate([h, l, h], 1), last)
-    for t in range(32):
-        put(t, os[pl.ds(t, nq, stride=32), :])
+        o = dot(jnp.concatenate([h, l, h], 1), last)
+        o = jnp.swapaxes(o.reshape(group, 32, 128), 0, 1)
+        for t in range(32):
+            put(t, o[t], q0)
 
 def scores_of(train, ready):
     return dot(train, ready, 1, 1).T * (1.0 / math.sqrt(GR * GC))
 
 
-def first_kernel(nq, q_hbm, bo_hbm, bi_hbm, ev_hbm, train_hbm, tv, out, lin, lout, fst, lst, rec, qv, bov, biv, evv, xa, xb, os, sem):
+def first_kernel(nq, q_hbm, bo_hbm, bi_hbm, ev_hbm, train_hbm, tv, out, lin, lout, fst, lst, rec, qv, bov, biv, evv, sem):
     copies = [
         pltpu.make_async_copy(a, b, sem.at[i])
         for i, (a, b) in enumerate(((bo_hbm, bov), (bi_hbm, biv), (ev_hbm, evv), (q_hbm, qv), (train_hbm.at[0], tv)))
@@ -102,10 +102,10 @@
     lin[...], lout[...] = row_maps(bov[0])
     fst[...], lst[...] = col_maps(biv[0])
 
-    def put(t, v):
-        out[:, t * 128:t * 128 + 128] = v.astype(BF16)
-
-    prep_body(nq, lambda t: qv[0, :, t * 128:t * 128 + 128], put, lin[...], lout[...], fst[...], lst[...], rec[...], xa, xb, os, 16)
+    def put(t, v, at):
+        out[at:at + v.shape[0], t * 128:t * 128 + 128] = v.astype(BF16)
+
+    prep_body(nq, lambda t: qv[0, :, t * 128:t * 128 + 128], put, lin[...], lout[...], fst[...], lst[...], rec[...], 16)
     copies[4].wait()
 
 
@@ -119,10 +119,6 @@
     ]
 
 
-def work(nq):
-    return [pltpu.VMEM((32 * nq, 128), F32)] * 3
-
-
 def settings(us):
     return dict(
         compiler_params=pltpu.CompilerParams(vmem_limit_bytes=20 << 20),
@@ -140,17 +136,16 @@
         out_specs=[VM] * 7,
         scratch_shapes=[pltpu.VMEM(q.shape, BF16)]
         + [pltpu.VMEM(x.shape, F32) for x in (bo, bi, ev)]
-        + work(nq)
         + [pltpu.SemaphoreType.DMA((5,))],
         **settings(4),
     )(*(pltpu.with_memory_space_constraint(x, pltpu.HBM) for x in args))
 
 
-def next_kernel(nq, chunk, lin, lout, fst, lst, rec, out, xa, xb, os):
-    def put(t, v):
-        out[:, t * 128:t * 128 + 128] = v.astype(BF16)
-
-    prep_body(nq, lambda t: chunk[:, t * 128:t * 128 + 128], put, lin[...], lout[...], fst[...], lst[...], rec[...], xa, xb, os, 16)
+def next_kernel(nq, chunk, lin, lout, fst, lst, rec, out):
+    def put(t, v, at):
+        out[at:at + v.shape[0], t * 128:t * 128 + 128] = v.astype(BF16)
+
+    prep_body(nq, lambda t: chunk[:, t * 128:t * 128 + 128], put, lin[...], lout[...], fst[...], lst[...], rec[...], 16)
 
 
 def following(chunk, maps):
@@ -160,20 +155,20 @@
         out_shape=jax.ShapeDtypeStruct(chunk.shape, BF16),
         in_specs=[VM] * 6,
         out_specs=VM,
-        scratch_shapes=work(nq),
         **settings(nq / 12),
     )(chunk, *maps)
 
 
-def bulk_kernel(own, near, mid, tv, lin, lout, fst, lst, rec, part, xa, xb, os, pv):
+def bulk_kernel(own, near, mid, tv, lin, lout, fst, lst, rec, part, pv):
     rows = own.shape[0]
     pv[0:rows, :] = own[...]
     pv[2 * rows:, :] = mid[...]
 
-    def put(t, v):
-        pv[rows:2 * rows, t * 128:t * 128 + 128] = v.astype(BF16)
-
-    prep_body(rows, lambda t: near[:, t * 128:t * 128 + 128], put, lin[...], lout[...], fst[...], lst[...], rec[...], xa, xb, os, 16)
+    def put(t, v, at):
+        at += rows
+        pv[at:at + v.shape[0], t * 128:t * 128 + 128] = v.astype(BF16)
+
+    prep_body(rows, lambda t: near[:, t * 128:t * 128 + 128], put, lin[...], lout[...], fst[...], lst[...], rec[...], 16)
     part[...] = scores_of(tv[...], pv[...])
 
 
@@ -185,7 +180,7 @@
         out_shape=jax.ShapeDtypeStruct((2 * rows + 16, n), F32),
         in_specs=[VM] * 9,
         out_specs=VM,
-        scratch_shapes=work(rows) + [pltpu.VMEM((2 * rows + 16, f), BF16)],
+        scratch_shapes=[pltpu.VMEM((2 * rows + 16, f), BF16)],
         **settings(3.5),
     )(own, near, mid, tv, *maps)
 

time: 28.3 us -> 28.1 us (level)
  Pallas kernels: 9.83 us -> 8.89 us
  waiting for transfers between devices: 6.09 us -> 6.88 us
    ppermute x1, waiting for transfers between devices: 0.25 us -> 0.68 us  [local(): lax.ppermute(mid, ('grp', 'ex'), [(g * 4 + z, (1 - g) * 4 + (z ^ 1)) for...]
    pallas_call x1, Pallas kernels: 3.65 us -> 3.23 us  [bulk(): pl.pallas_call(bulk_kernel, out_shape=jax.ShapeDtypeStruct((2 * rows + 16...]
    pallas_call x1, Pallas kernels: 3.83 us -> 3.41 us  [first(): pl.pallas_call(functools.partial(first_kernel, nq), out_shape=[jax.ShapeD...]
    ppermute x7, waiting for transfers between devices: 5.84 us -> 6.19 us  [flip(): return lax.ppermute(x, axis, [(i, i ^ mask) for i in range(size)])]
  transfers between devices with their start and end apart: 8 -> 8, of which waited for: 7 -> 7; matrix products, arithmetic and copies ran while one was open for 0% -> 0% of each run, Pallas kernels for 30% -> 27%
where the time goes in v6:
time: 28.1 us; the launch traced here: 28 us
  starting transfers between devices  10.6 us (38%)
  Pallas kernels  8.89 us (32%)
  waiting for transfers between devices  6.88 us (24%)
  local copies, waits for them, and re-layouts  0.91 us (3%)
  other arithmetic  0.65 us (2%)
    ppermute x7, starting transfers between devices, flip(): return lax.ppermute(x, axis, [(i, i ^ mask) for i in range(size)])  7.93 us
    ppermute x7, waiting for transfers between devices, flip(): return lax.ppermute(x, axis, [(i, i ^ mask) for i in range(size)])  6.19 us
    pallas_call x1, Pallas kernels, first(): pl.pallas_call(functools.partial(first_kernel, nq), out_shape=[jax.ShapeD...  3.41 us
    pallas_call x1, Pallas kernels, bulk(): pl.pallas_call(bulk_kernel, out_shape=jax.ShapeDtypeStruct((2 * rows + 16...  3.23 us
    ppermute x1, starting transfers between devices, local(): lax.ppermute(mid, ('grp', 'ex'), [(g * 4 + z, (1 - g) * 4 + (z ^ 1)) for...  2.67 us
    pallas_call x1, Pallas kernels, final(): pl.pallas_call(last_kernel, out_shape=[jax.ShapeDtypeStruct((rows, n), d)...  1.29 us
    pallas_call x1, Pallas kernels, following(): pl.pallas_call(functools.partial(next_kernel, nq), out_shape=jax.ShapeDty...  0.97 us
    dynamic_slice x1, local copies, waits for them, and re-layouts, local(): half = lax.dynamic_slice_in_dim(query[0], start, 16, 0)  0.91 us
  transfers between devices with their start and end apart: 8, of which 7 were waited for; matrix products, arithmetic and copies ran while one was open for 0% of the time, Pallas kernels for 27%

profile of v6, /device:TPU:0, one launch (start us, length us, event | category | flops | bytes accessed | tf_op | source)
XLA Modules:
  0.0 28.0 jit_solution(12150029045812589711)
XLA Ops:
  0.0 0.9 %dynamic-slice_bitcast_fusion = bf16[16,4096]{1,0:T(8,128)(2,1)S(1)} fusion(bf16[1,32,4096]{2,1,0:T(8,128)(2,1)} %q_hbm.1, s32[]{:T(128)S(6)} %select_n.3), kind=kLoop, calls=%fused_computation | loop fusion | bytes 262148 | tf_op jit(solution)/shard_map/dynamic_slice | solution.py:247
  0.9 5.1 %collective-permute-start = (bf16[16,4096]{1,0:T(8,128)(2,1)S(1)}, bf16[16,4096]{1,0:T(8,128)(2,1)S(1)}, u32[]{:S(2)}, u32[]{:S(2)}) collective-permute-start(bf16[16,4096]{1,0:T(8,128)(2,1)S(1)} %dynamic-slice_bitcast_fusion), channel_id=1, source_target_pairs={{0,12},{4,8},{8,4},{12,0},{1,13},{5,9},{9,5},{13,1},{2,14},{6,10},... | collective-permute-start | bytes 393224 | tf_op jit(solution)/shard_map/ppermute | solution.py:226
  6.0 0.0 collective-permute-start.4
  6.0 3.4 %shard_map.55 = (bf16[512,4096]{1,0:T(8,128)(2,1)S(1)}, bf16[32,4096]{1,0:T(8,128)(2,1)S(1)}, bf16[64,192]{1,0:T(8,128)(2,1)S(1)}, bf16[64,192]{1,0:T(8,128)(2,1...) custom-call(bf16[1,32,4096]{2,1,0:T(8,128)(2,1)} %q_hbm.1, ...), custom_call_target="tpu_custom_call" | custom-call | flops 4000000000 | bytes 14400000 | tf_op jit(solution)/shard_map/pallas_call | solution.py:132
  9.5 0.9 %collective-permute-done.chunk = bf16[16,4096]{1,0:T(8,128)(2,1)S(1)} collective-permute-done((bf16[16,4096]{1,0:T(8,128)(2,1)S(1)}, bf16[16,4096]{1,0:T(8,128)(2,1)S(1)}, u32[]{:S(2)}, u32[]{:S(2)}) %collective-permute-start) | collective-permute-done | bytes 131104 | tf_op jit(solution)/shard_map/ppermute | solution.py:226
  10.4 1.0 %shard_map.56.mid = bf16[16,4096]{1,0:T(8,128)(2,1)S(1)} custom-call(bf16[16,4096]{1,0:T(8,128)(2,1)S(1)} %collective-permute-done.chunk, bf16[64,192]{1,0:T(8,128)(2,1)S(1)} %get-tuple-element.16.lin, bf16[64,192]{1,0:T(8,128)(2,1)S(1)} %get-tuple-element.17.lout, bf16[256,256]{1,0:T(8,128)(2,1)S(1)} %get-tuple-element.18.fst, ...), custom_call_target="tpu_custom_call" | custom-call | flops 1333333376 | bytes 4800000 | tf_op jit(solution)/shard_map/pallas_call | solution.py:153
  11.4 2.7 %collective-permute-start.3 = (bf16[16,4096]{1,0:T(8,128)(2,1)S(1)}, bf16[16,4096]{1,0:T(8,128)(2,1)S(1)}, u32[]{:S(2)}, u32[]{:S(2)}) collective-permute-start(bf16[16,4096]{1,0:T(8,128)(2,1)S(1)} %shard_map.56.mid), channel_id=1, source_target_pairs={{0,20},{4,16},{8,28},{12,24},{16,4},{20,0},{24,12},{28,8},{1,21},{... | collective-permute-start | bytes 393224 | tf_op jit(solution)/shard_map/ppermute | solution.py:254
  14.0 0.6 %collective-permute-start.2 = (bf16[16,4096]{1,0:T(8,128)(2,1)S(1)}, bf16[16,4096]{1,0:T(8,128)(2,1)S(1)}, u32[]{:S(2)}, u32[]{:S(2)}) collective-permute-start(bf16[16,4096]{1,0:T(8,128)(2,1)S(1)} %shard_map.56.mid), channel_id=1, source_target_pairs={{0,4},{4,0},{8,12},{12,8},{1,5},{5,1},{9,13},{13,9},{2,6},{6,2},{1... | collective-permute-start | bytes 393224 | tf_op jit(solution)/shard_map/ppermute | solution.py:226
  14.6 0.3 %collective-permute-start.1 = (bf16[16,4096]{1,0:T(8,128)(2,1)S(1)}, bf16[16,4096]{1,0:T(8,128)(2,1)S(1)}, u32[]{:S(2)}, u32[]{:S(2)}) collective-permute-start(bf16[16,4096]{1,0:T(8,128)(2,1)S(1)} %shard_map.56.mid), channel_id=1, source_target_pairs={{0,16},{16,0},{1,17},{17,1},{2,18},{18,2},{3,19},{19,3},{4,20},{20... | collective-permute-start | bytes 393224 | tf_op jit(solution)/shard_map/ppermute | solution.py:226
  14.9 0.8 %collective-permute-done.4.near = bf16[32,4096]{1,0:T(8,128)(2,1)S(1)} collective-permute-done((bf16[32,4096]{1,0:T(8,128)(2,1)}, bf16[32,4096]{1,0:T(8,128)(2,1)S(1)}, u32[]{:S(2)}, u32[]{:S(2)}) %collective-permute-start.4) | collective-permute-done | bytes 262176 | tf_op jit(solution)/shard_map/ppermute | solution.py:226
  15.8 3.2 %shard_map.57.part = f32[80,512]{1,0:T(8,128)S(1)} custom-call(bf16[32,4096]{1,0:T(8,128)(2,1)S(1)} %get-tuple-element.22.own, bf16[32,4096]{1,0:T(8,128)(2,1)S(1)} %collective-permute-done.4.near, bf16[16,4096]{1,0:T(8,128)(2,1)S(1)} %shard_map.56.mid, bf16[512,4096]{1,0:T(8,128)(2,1)S(1)} %get-tuple-element.21.tv, ...), custom_call_target="tpu_custom_call" | custom-call | flops 3500000000 | bytes 12600000 | tf_op jit(solution)/shard_map/pallas_call | solution.py:178
  19.0 0.7 %collective-permute-done.3.far2 = bf16[16,4096]{1,0:T(8,128)(2,1)S(1)} collective-permute-done((bf16[16,4096]{1,0:T(8,128)(2,1)S(1)}, bf16[16,4096]{1,0:T(8,128)(2,1)S(1)}, u32[]{:S(2)}, u32[]{:S(2)}) %collective-permute-start.3) | collective-permute-done | bytes 131104 | tf_op jit(solution)/shard_map/ppermute | solution.py:254
  19.7 1.2 %collective-permute-done.2.far = bf16[16,4096]{1,0:T(8,128)(2,1)S(1)} collective-permute-done((bf16[16,4096]{1,0:T(8,128)(2,1)S(1)}, bf16[16,4096]{1,0:T(8,128)(2,1)S(1)}, u32[]{:S(2)}, u32[]{:S(2)}) %collective-permute-start.2) | collective-permute-done | bytes 131104 | tf_op jit(solution)/shard_map/ppermute | solution.py:226
  20.9 0.1 collective-permute-done.1.mid2
  21.0 1.3 %shard_map.58 = (f32[32,512]{1,0:T(8,128)S(1)}, f32[32,512]{1,0:T(8,128)S(1)}, bf16[32,512]{1,0:T(8,128)(2,1)S(1)}, bf16[32,512]{1,0:T(8,128)(2,1)S(1)}) custom-call(bf16[16,4096]{1,0:T(8,128)(2,1)S(1)} %collective-permute-done.1.mid2, bf16[16,4096]{1,0:T(8,128)(2,1)S(1)} %collective-permute-done.2.far, bf16[16,4096]{1,0:T(8,128)(2,1)S(1)} %collective-permute-done.3.far2, ...), custom_call_target="tpu_custom_call" | custom-call | flops 1300000000 | bytes 4680000 | tf_op jit(solution)/shard_map/pallas_call | solution.py:212
  22.3 0.1 collective-permute-start.5
  22.4 1.6 %collective-permute-start.6 = (bf16[32,512]{1,0:T(8,128)(2,1)S(1)}, bf16[32,512]{1,0:T(8,128)(2,1)S(1)}, u32[]{:S(2)}, u32[]{:S(2)}) collective-permute-start(bf16[32,512]{1,0:T(8,128)(2,1)S(1)} %get-tuple-element.25), channel_id=1, source_target_pairs={{0,2},{1,3},{2,0},{3,1},{4,6},{5,7},{6,4},{7,5},{8,10},{9,11},{10,... | collective-permute-start | bytes 98312 | tf_op jit(solution)/shard_map/ppermute | solution.py:226
  24.0 0.3 %collective-permute-start.7 = (bf16[32,512]{1,0:T(8,128)(2,1)S(1)}, bf16[32,512]{1,0:T(8,128)(2,1)S(1)}, u32[]{:S(2)}, u32[]{:S(2)}) collective-permute-start(bf16[32,512]{1,0:T(8,128)(2,1)S(1)} %get-tuple-element.26), channel_id=1, source_target_pairs={{0,3},{1,2},{2,1},{3,0},{4,7},{5,6},{6,5},{7,4},{8,11},{9,10},{10,... | collective-permute-start | bytes 98312 | tf_op jit(solution)/shard_map/ppermute | solution.py:226
  24.3 2.1 %collective-permute-done.6 = bf16[32,512]{1,0:T(8,128)(2,1)S(1)} collective-permute-done((bf16[32,512]{1,0:T(8,128)(2,1)S(1)}, bf16[32,512]{1,0:T(8,128)(2,1)S(1)}, u32[]{:S(2)}, u32[]{:S(2)}) %collective-permute-start.6) | collective-permute-done | bytes 32800 | tf_op jit(solution)/shard_map/ppermute | solution.py:226
  26.4 0.9 %collective-permute-done.7 = bf16[32,512]{1,0:T(8,128)(2,1)S(1)} collective-permute-done((bf16[32,512]{1,0:T(8,128)(2,1)S(1)}, bf16[32,512]{1,0:T(8,128)(2,1)S(1)}, u32[]{:S(2)}, u32[]{:S(2)}) %collective-permute-start.7) | collective-permute-done | bytes 32800 | tf_op jit(solution)/shard_map/ppermute | solution.py:226
  27.3 0.0 collective-permute-done.5
  27.3 0.6 %add_bitcast_fusion = f32[512,32]{0,1:T(8,128)} fusion(bf16[32,512]{1,0:T(8,128)(2,1)S(1)} %collective-permute-done.7, bf16[32,512]{1,0:T(8,128)(2,1)S(1)} %collective-permute-done.6, f32[32,512]{1,0:T(8,128)S(1)} %get-tuple-element.23, f32[32,512]{1,0:T(8,128)S(1)} %collective-permute-done.5), kind=kLoop, calls=%fused_computation.1 | loop fusion | flops 81920 | bytes 262144 | tf_op jit(solution)/shard_map/transpose | solution.py:259
Async XLA Ops:
  0.9 9.5 %collective-permute-start = (bf16[16,4096]{1,0:T(8,128)(2,1)S(1)}, bf16[16,4096]{1,0:T(8,128)(2,1)S(1)}, u32[]{:S(2)}, u32[]{:S(2)}) collective-permute-start(bf16[16,4096]{1,0:T(8,128)(2,1)S(1)} %dynamic-slice_bitcast_fusion), channel_id=1, source_target_pairs={{0,12},{4,8},{8,4},{12,0},{1,13},{5,9},{9,5},{13,1},{2,14},{6,10},... | collective-permute-start | bytes 393224 | tf_op jit(solution)/shard_map/ppermute | solution.py:226
  6.0 9.7 %collective-permute-start.4 = (bf16[32,4096]{1,0:T(8,128)(2,1)}, bf16[32,4096]{1,0:T(8,128)(2,1)S(1)}, u32[]{:S(2)}, u32[]{:S(2)}) collective-permute-start(bf16[32,4096]{1,0:T(8,128)(2,1)} %bitcast.5), channel_id=1, source_target_pairs={{0,4},{4,0},{8,12},{12,8},{1,5},{5,1},{9,13},{13,9},{2,6},{6,2},{1... | collective-permute-start | bytes 786440 | tf_op jit(solution)/shard_map/ppermute | solution.py:226
  11.4 8.3 %collective-permute-start.3 = (bf16[16,4096]{1,0:T(8,128)(2,1)S(1)}, bf16[16,4096]{1,0:T(8,128)(2,1)S(1)}, u32[]{:S(2)}, u32[]{:S(2)}) collective-permute-start(bf16[16,4096]{1,0:T(8,128)(2,1)S(1)} %shard_map.56.mid), channel_id=1, source_target_pairs={{0,20},{4,16},{8,28},{12,24},{16,4},{20,0},{24,12},{28,8},{1,21},{... | collective-permute-start | bytes 393224 | tf_op jit(solution)/shard_map/ppermute | solution.py:254
  14.0 6.9 %collective-permute-start.2 = (bf16[16,4096]{1,0:T(8,128)(2,1)S(1)}, bf16[16,4096]{1,0:T(8,128)(2,1)S(1)}, u32[]{:S(2)}, u32[]{:S(2)}) collective-permute-start(bf16[16,4096]{1,0:T(8,128)(2,1)S(1)} %shard_map.56.mid), channel_id=1, source_target_pairs={{0,4},{4,0},{8,12},{12,8},{1,5},{5,1},{9,13},{13,9},{2,6},{6,2},{1... | collective-permute-start | bytes 393224 | tf_op jit(solution)/shard_map/ppermute | solution.py:226
  14.6 6.4 %collective-permute-start.1 = (bf16[16,4096]{1,0:T(8,128)(2,1)S(1)}, bf16[16,4096]{1,0:T(8,128)(2,1)S(1)}, u32[]{:S(2)}, u32[]{:S(2)}) collective-permute-start(bf16[16,4096]{1,0:T(8,128)(2,1)S(1)} %shard_map.56.mid), channel_id=1, source_target_pairs={{0,16},{16,0},{1,17},{17,1},{2,18},{18,2},{3,19},{19,3},{4,20},{20... | collective-permute-start | bytes 393224 | tf_op jit(solution)/shard_map/ppermute | solution.py:226
  22.3 5.0 %collective-permute-start.5 = (f32[32,512]{1,0:T(8,128)S(1)}, f32[32,512]{1,0:T(8,128)S(1)}, u32[]{:S(2)}, u32[]{:S(2)}) collective-permute-start(f32[32,512]{1,0:T(8,128)S(1)} %get-tuple-element.24), channel_id=1, source_target_pairs={{0,1},{1,0},{2,3},{3,2},{4,5},{5,4},{6,7},{7,6},{8,9},{9,8},{10,11... | collective-permute-start | bytes 196616 | tf_op jit(solution)/shard_map/ppermute | solution.py:226
  22.4 4.0 %collective-permute-start.6 = (bf16[32,512]{1,0:T(8,128)(2,1)S(1)}, bf16[32,512]{1,0:T(8,128)(2,1)S(1)}, u32[]{:S(2)}, u32[]{:S(2)}) collective-permute-start(bf16[32,512]{1,0:T(8,128)(2,1)S(1)} %get-tuple-element.25), channel_id=1, source_target_pairs={{0,2},{1,3},{2,0},{3,1},{4,6},{5,7},{6,4},{7,5},{8,10},{9,11},{10,... | collective-permute-start | bytes 98312 | tf_op jit(solution)/shard_map/ppermute | solution.py:226
  24.0 3.3 %collective-permute-start.7 = (bf16[32,512]{1,0:T(8,128)(2,1)S(1)}, bf16[32,512]{1,0:T(8,128)(2,1)S(1)}, u32[]{:S(2)}, u32[]{:S(2)}) collective-permute-start(bf16[32,512]{1,0:T(8,128)(2,1)S(1)} %get-tuple-element.26), channel_id=1, source_target_pairs={{0,3},{1,2},{2,1},{3,0},{4,7},{5,6},{6,5},{7,4},{8,11},{9,10},{10,... | collective-permute-start | bytes 98312 | tf_op jit(solution)/shard_map/ppermute | solution.py:226

commit v7 on v6

--- a/solution.py
+++ b/solution.py
@@ -169,7 +169,16 @@
         pv[at:at + v.shape[0], t * 128:t * 128 + 128] = v.astype(BF16)
 
     prep_body(rows, lambda t: near[:, t * 128:t * 128 + 128], put, lin[...], lout[...], fst[...], lst[...], rec[...], 16)
-    part[...] = scores_of(tv[...], pv[...])
+    half = 16 * lax.axis_index("grp")
+    slot = lax.axis_index("ex") ^ lax.axis_index("lyr")
+
+    def at(m, extra, size):
+        return pl.ds(pl.multiple_of((slot ^ m) * rows + extra, 16), size)
+
+    early = scores_of(tv[...], pv[...])
+    part[at(0, 0, rows), :] = early[0:rows]
+    part[at(1, 0, rows), :] = early[rows:2 * rows]
+    part[at(3, half, 16), :] = early[2 * rows:]
 
 
 def bulk(own, near, mid, tv, maps):
@@ -177,7 +186,7 @@
     n = tv.shape[0]
     return pl.pallas_call(
         bulk_kernel,
-        out_shape=jax.ShapeDtypeStruct((2 * rows + 16, n), F32),
+        out_shape=jax.ShapeDtypeStruct((4 * rows, n), F32),
         in_specs=[VM] * 9,
         out_specs=VM,
         scratch_shapes=[pltpu.VMEM((2 * rows + 16, f), BF16)],
@@ -185,7 +194,7 @@
     )(own, near, mid, tv, *maps)
 
 
-def last_kernel(mid2, far, far2, tv, part, mine, core, across, both, pv, sv):
+def last_kernel(mid2, far, far2, tv, part, mine, core, across, both, sv):
     half = 16 * lax.axis_index("grp")
     other = 16 - half
     rows = mine.shape[0]
@@ -194,12 +203,8 @@
     def at(m, extra, size):
         return pl.ds(pl.multiple_of((slot ^ m) * rows + extra, 16), size)
 
-    sv[at(0, 0, rows), :] = part[0:rows, :]
-    sv[at(1, 0, rows), :] = part[rows:2 * rows, :]
-    sv[at(3, half, 16), :] = part[2 * rows:, :]
-    for i, p in enumerate((mid2, far, far2)):
-        pv[i * 16:i * 16 + 16, :] = p[...]
-    late = scores_of(tv[...], pv[...])
+    late = scores_of(tv[...], jnp.concatenate([p[...] for p in (mid2, far, far2)], 0))
+    sv[...] = part[...]
     sv[at(3, other, 16), :] = late[0:16]
     sv[at(2, half, 16), :] = late[16:32]
     sv[at(2, other, 16), :] = late[32:48]
@@ -214,7 +219,7 @@
         out_shape=[jax.ShapeDtypeStruct((rows, n), d) for d in (F32, F32, SENT, SENT)],
         in_specs=[VM] * 5,
         out_specs=[VM] * 4,
-        scratch_shapes=[pltpu.VMEM((48, f), BF16), pltpu.VMEM((4 * rows, n), F32)],
+        scratch_shapes=[pltpu.VMEM((4 * rows, n), F32)],
         **settings(1.3),
     )(mid2, far, far2, tv, part)
 

time: 28.1 us -> 28.1 us (level)
  no operation moved by 1% of the time
where the time goes in v7:
time: 28.1 us; the launch traced here: 28 us
  starting transfers between devices  10.6 us (38%)
  Pallas kernels  8.89 us (32%)
  waiting for transfers between devices  6.87 us (24%)
  local copies, waits for them, and re-layouts  0.91 us (3%)
  other arithmetic  0.65 us (2%)
    ppermute x7, starting transfers between devices, flip(): return lax.ppermute(x, axis, [(i, i ^ mask) for i in range(size)])  7.93 us
    ppermute x7, waiting for transfers between devices, flip(): return lax.ppermute(x, axis, [(i, i ^ mask) for i in range(size)])  6.19 us
    pallas_call x1, Pallas kernels, first(): pl.pallas_call(functools.partial(first_kernel, nq), out_shape=[jax.ShapeD...  3.41 us
    pallas_call x1, Pallas kernels, bulk(): pl.pallas_call(bulk_kernel, out_shape=jax.ShapeDtypeStruct((4 * rows, n),...  3.23 us
    ppermute x1, starting transfers between devices, local(): lax.ppermute(mid, ('grp', 'ex'), [(g * 4 + z, (1 - g) * 4 + (z ^ 1)) for...  2.67 us
    pallas_call x1, Pallas kernels, final(): pl.pallas_call(last_kernel, out_shape=[jax.ShapeDtypeStruct((rows, n), d)...  1.29 us
    pallas_call x1, Pallas kernels, following(): pl.pallas_call(functools.partial(next_kernel, nq), out_shape=jax.ShapeDty...  0.97 us
    dynamic_slice x1, local copies, waits for them, and re-layouts, local(): half = lax.dynamic_slice_in_dim(query[0], start, 16, 0)  0.91 us
  transfers between devices with their start and end apart: 8, of which 7 were waited for; matrix products, arithmetic and copies ran while one was open for 0% of the time, Pallas kernels for 27%

profile of v7, /device:TPU:0, one launch (start us, length us, event | category | flops | bytes accessed | tf_op | source)
XLA Modules:
  0.0 28.0 jit_solution(10827161475846568259)
XLA Ops:
  0.0 0.9 %dynamic-slice_bitcast_fusion = bf16[16,4096]{1,0:T(8,128)(2,1)S(1)} fusion(bf16[1,32,4096]{2,1,0:T(8,128)(2,1)} %q_hbm.1, s32[]{:T(128)S(6)} %select_n.3), kind=kLoop, calls=%fused_computation | loop fusion | bytes 262148 | tf_op jit(solution)/shard_map/dynamic_slice | solution.py:252
  0.9 5.1 %collective-permute-start = (bf16[16,4096]{1,0:T(8,128)(2,1)S(1)}, bf16[16,4096]{1,0:T(8,128)(2,1)S(1)}, u32[]{:S(2)}, u32[]{:S(2)}) collective-permute-start(bf16[16,4096]{1,0:T(8,128)(2,1)S(1)} %dynamic-slice_bitcast_fusion), channel_id=1, source_target_pairs={{0,12},{4,8},{8,4},{12,0},{1,13},{5,9},{9,5},{13,1},{2,14},{6,10},... | collective-permute-start | bytes 393224 | tf_op jit(solution)/shard_map/ppermute | solution.py:231
  6.0 0.0 collective-permute-start.4
  6.0 3.4 %shard_map.55 = (bf16[512,4096]{1,0:T(8,128)(2,1)S(1)}, bf16[32,4096]{1,0:T(8,128)(2,1)S(1)}, bf16[64,192]{1,0:T(8,128)(2,1)S(1)}, bf16[64,192]{1,0:T(8,128)(2,1...) custom-call(bf16[1,32,4096]{2,1,0:T(8,128)(2,1)} %q_hbm.1, ...), custom_call_target="tpu_custom_call" | custom-call | flops 4000000000 | bytes 14400000 | tf_op jit(solution)/shard_map/pallas_call | solution.py:132
  9.5 0.9 %collective-permute-done.chunk = bf16[16,4096]{1,0:T(8,128)(2,1)S(1)} collective-permute-done((bf16[16,4096]{1,0:T(8,128)(2,1)S(1)}, bf16[16,4096]{1,0:T(8,128)(2,1)S(1)}, u32[]{:S(2)}, u32[]{:S(2)}) %collective-permute-start) | collective-permute-done | bytes 131104 | tf_op jit(solution)/shard_map/ppermute | solution.py:231
  10.4 1.0 %shard_map.56.mid = bf16[16,4096]{1,0:T(8,128)(2,1)S(1)} custom-call(bf16[16,4096]{1,0:T(8,128)(2,1)S(1)} %collective-permute-done.chunk, bf16[64,192]{1,0:T(8,128)(2,1)S(1)} %get-tuple-element.16.lin, bf16[64,192]{1,0:T(8,128)(2,1)S(1)} %get-tuple-element.17.lout, bf16[256,256]{1,0:T(8,128)(2,1)S(1)} %get-tuple-element.18.fst, ...), custom_call_target="tpu_custom_call" | custom-call | flops 1333333376 | bytes 4800000 | tf_op jit(solution)/shard_map/pallas_call | solution.py:153
  11.4 2.7 %collective-permute-start.3 = (bf16[16,4096]{1,0:T(8,128)(2,1)S(1)}, bf16[16,4096]{1,0:T(8,128)(2,1)S(1)}, u32[]{:S(2)}, u32[]{:S(2)}) collective-permute-start(bf16[16,4096]{1,0:T(8,128)(2,1)S(1)} %shard_map.56.mid), channel_id=1, source_target_pairs={{0,20},{4,16},{8,28},{12,24},{16,4},{20,0},{24,12},{28,8},{1,21},{... | collective-permute-start | bytes 393224 | tf_op jit(solution)/shard_map/ppermute | solution.py:259
  14.0 0.6 %collective-permute-start.2 = (bf16[16,4096]{1,0:T(8,128)(2,1)S(1)}, bf16[16,4096]{1,0:T(8,128)(2,1)S(1)}, u32[]{:S(2)}, u32[]{:S(2)}) collective-permute-start(bf16[16,4096]{1,0:T(8,128)(2,1)S(1)} %shard_map.56.mid), channel_id=1, source_target_pairs={{0,4},{4,0},{8,12},{12,8},{1,5},{5,1},{9,13},{13,9},{2,6},{6,2},{1... | collective-permute-start | bytes 393224 | tf_op jit(solution)/shard_map/ppermute | solution.py:231
  14.6 0.3 %collective-permute-start.1 = (bf16[16,4096]{1,0:T(8,128)(2,1)S(1)}, bf16[16,4096]{1,0:T(8,128)(2,1)S(1)}, u32[]{:S(2)}, u32[]{:S(2)}) collective-permute-start(bf16[16,4096]{1,0:T(8,128)(2,1)S(1)} %shard_map.56.mid), channel_id=1, source_target_pairs={{0,16},{16,0},{1,17},{17,1},{2,18},{18,2},{3,19},{19,3},{4,20},{20... | collective-permute-start | bytes 393224 | tf_op jit(solution)/shard_map/ppermute | solution.py:231
  14.9 0.8 %collective-permute-done.4.near = bf16[32,4096]{1,0:T(8,128)(2,1)S(1)} collective-permute-done((bf16[32,4096]{1,0:T(8,128)(2,1)}, bf16[32,4096]{1,0:T(8,128)(2,1)S(1)}, u32[]{:S(2)}, u32[]{:S(2)}) %collective-permute-start.4) | collective-permute-done | bytes 262176 | tf_op jit(solution)/shard_map/ppermute | solution.py:231
  15.8 3.2 %shard_map.57.part = f32[128,512]{1,0:T(8,128)S(1)} custom-call(bf16[32,4096]{1,0:T(8,128)(2,1)S(1)} %get-tuple-element.22.own, bf16[32,4096]{1,0:T(8,128)(2,1)S(1)} %collective-permute-done.4.near, bf16[16,4096]{1,0:T(8,128)(2,1)S(1)} %shard_map.56.mid, bf16[512,4096]{1,0:T(8,128)(2,1)S(1)} %get-tuple-element.21.tv, ...), custom_call_target="tpu_custom_call" | custom-call | flops 3500000000 | bytes 12600000 | tf_op jit(solution)/shard_map/pallas_call | solution.py:187
  19.0 0.7 %collective-permute-done.3.far2 = bf16[16,4096]{1,0:T(8,128)(2,1)S(1)} collective-permute-done((bf16[16,4096]{1,0:T(8,128)(2,1)S(1)}, bf16[16,4096]{1,0:T(8,128)(2,1)S(1)}, u32[]{:S(2)}, u32[]{:S(2)}) %collective-permute-start.3) | collective-permute-done | bytes 131104 | tf_op jit(solution)/shard_map/ppermute | solution.py:259
  19.7 1.2 %collective-permute-done.2.far = bf16[16,4096]{1,0:T(8,128)(2,1)S(1)} collective-permute-done((bf16[16,4096]{1,0:T(8,128)(2,1)S(1)}, bf16[16,4096]{1,0:T(8,128)(2,1)S(1)}, u32[]{:S(2)}, u32[]{:S(2)}) %collective-permute-start.2) | collective-permute-done | bytes 131104 | tf_op jit(solution)/shard_map/ppermute | solution.py:231
  20.9 0.1 collective-permute-done.1.mid2
  21.0 1.3 %shard_map.58 = (f32[32,512]{1,0:T(8,128)S(1)}, f32[32,512]{1,0:T(8,128)S(1)}, bf16[32,512]{1,0:T(8,128)(2,1)S(1)}, bf16[32,512]{1,0:T(8,128)(2,1)S(1)}) custom-call(bf16[16,4096]{1,0:T(8,128)(2,1)S(1)} %collective-permute-done.1.mid2, bf16[16,4096]{1,0:T(8,128)(2,1)S(1)} %collective-permute-done.2.far, bf16[16,4096]{1,0:T(8,128)(2,1)S(1)} %collective-permute-done.3.far2, ...), custom_call_target="tpu_custom_call" | custom-call | flops 1300000000 | bytes 4680000 | tf_op jit(solution)/shard_map/pallas_call | solution.py:217
  22.3 0.1 collective-permute-start.5
  22.4 1.6 %collective-permute-start.6 = (bf16[32,512]{1,0:T(8,128)(2,1)S(1)}, bf16[32,512]{1,0:T(8,128)(2,1)S(1)}, u32[]{:S(2)}, u32[]{:S(2)}) collective-permute-start(bf16[32,512]{1,0:T(8,128)(2,1)S(1)} %get-tuple-element.25), channel_id=1, source_target_pairs={{0,2},{1,3},{2,0},{3,1},{4,6},{5,7},{6,4},{7,5},{8,10},{9,11},{10,... | collective-permute-start | bytes 98312 | tf_op jit(solution)/shard_map/ppermute | solution.py:231
  24.0 0.3 %collective-permute-start.7 = (bf16[32,512]{1,0:T(8,128)(2,1)S(1)}, bf16[32,512]{1,0:T(8,128)(2,1)S(1)}, u32[]{:S(2)}, u32[]{:S(2)}) collective-permute-start(bf16[32,512]{1,0:T(8,128)(2,1)S(1)} %get-tuple-element.26), channel_id=1, source_target_pairs={{0,3},{1,2},{2,1},{3,0},{4,7},{5,6},{6,5},{7,4},{8,11},{9,10},{10,... | collective-permute-start | bytes 98312 | tf_op jit(solution)/shard_map/ppermute | solution.py:231
  24.3 2.1 %collective-permute-done.6 = bf16[32,512]{1,0:T(8,128)(2,1)S(1)} collective-permute-done((bf16[32,512]{1,0:T(8,128)(2,1)S(1)}, bf16[32,512]{1,0:T(8,128)(2,1)S(1)}, u32[]{:S(2)}, u32[]{:S(2)}) %collective-permute-start.6) | collective-permute-done | bytes 32800 | tf_op jit(solution)/shard_map/ppermute | solution.py:231
  26.4 0.9 %collective-permute-done.7 = bf16[32,512]{1,0:T(8,128)(2,1)S(1)} collective-permute-done((bf16[32,512]{1,0:T(8,128)(2,1)S(1)}, bf16[32,512]{1,0:T(8,128)(2,1)S(1)}, u32[]{:S(2)}, u32[]{:S(2)}) %collective-permute-start.7) | collective-permute-done | bytes 32800 | tf_op jit(solution)/shard_map/ppermute | solution.py:231
  27.3 0.0 collective-permute-done.5
  27.3 0.6 %add_bitcast_fusion = f32[512,32]{0,1:T(8,128)} fusion(bf16[32,512]{1,0:T(8,128)(2,1)S(1)} %collective-permute-done.7, bf16[32,512]{1,0:T(8,128)(2,1)S(1)} %collective-permute-done.6, f32[32,512]{1,0:T(8,128)S(1)} %get-tuple-element.23, f32[32,512]{1,0:T(8,128)S(1)} %collective-permute-done.5), kind=kLoop, calls=%fused_computation.1 | loop fusion | flops 81920 | bytes 262144 | tf_op jit(solution)/shard_map/transpose | solution.py:264
Async XLA Ops:
  0.9 9.5 %collective-permute-start = (bf16[16,4096]{1,0:T(8,128)(2,1)S(1)}, bf16[16,4096]{1,0:T(8,128)(2,1)S(1)}, u32[]{:S(2)}, u32[]{:S(2)}) collective-permute-start(bf16[16,4096]{1,0:T(8,128)(2,1)S(1)} %dynamic-slice_bitcast_fusion), channel_id=1, source_target_pairs={{0,12},{4,8},{8,4},{12,0},{1,13},{5,9},{9,5},{13,1},{2,14},{6,10},... | collective-permute-start | bytes 393224 | tf_op jit(solution)/shard_map/ppermute | solution.py:231
  6.0 9.7 %collective-permute-start.4 = (bf16[32,4096]{1,0:T(8,128)(2,1)}, bf16[32,4096]{1,0:T(8,128)(2,1)S(1)}, u32[]{:S(2)}, u32[]{:S(2)}) collective-permute-start(bf16[32,4096]{1,0:T(8,128)(2,1)} %bitcast.5), channel_id=1, source_target_pairs={{0,4},{4,0},{8,12},{12,8},{1,5},{5,1},{9,13},{13,9},{2,6},{6,2},{1... | collective-permute-start | bytes 786440 | tf_op jit(solution)/shard_map/ppermute | solution.py:231
  11.4 8.3 %collective-permute-start.3 = (bf16[16,4096]{1,0:T(8,128)(2,1)S(1)}, bf16[16,4096]{1,0:T(8,128)(2,1)S(1)}, u32[]{:S(2)}, u32[]{:S(2)}) collective-permute-start(bf16[16,4096]{1,0:T(8,128)(2,1)S(1)} %shard_map.56.mid), channel_id=1, source_target_pairs={{0,20},{4,16},{8,28},{12,24},{16,4},{20,0},{24,12},{28,8},{1,21},{... | collective-permute-start | bytes 393224 | tf_op jit(solution)/shard_map/ppermute | solution.py:259
  14.0 6.9 %collective-permute-start.2 = (bf16[16,4096]{1,0:T(8,128)(2,1)S(1)}, bf16[16,4096]{1,0:T(8,128)(2,1)S(1)}, u32[]{:S(2)}, u32[]{:S(2)}) collective-permute-start(bf16[16,4096]{1,0:T(8,128)(2,1)S(1)} %shard_map.56.mid), channel_id=1, source_target_pairs={{0,4},{4,0},{8,12},{12,8},{1,5},{5,1},{9,13},{13,9},{2,6},{6,2},{1... | collective-permute-start | bytes 393224 | tf_op jit(solution)/shard_map/ppermute | solution.py:231
  14.6 6.4 %collective-permute-start.1 = (bf16[16,4096]{1,0:T(8,128)(2,1)S(1)}, bf16[16,4096]{1,0:T(8,128)(2,1)S(1)}, u32[]{:S(2)}, u32[]{:S(2)}) collective-permute-start(bf16[16,4096]{1,0:T(8,128)(2,1)S(1)} %shard_map.56.mid), channel_id=1, source_target_pairs={{0,16},{16,0},{1,17},{17,1},{2,18},{18,2},{3,19},{19,3},{4,20},{20... | collective-permute-start | bytes 393224 | tf_op jit(solution)/shard_map/ppermute | solution.py:231
  22.3 5.0 %collective-permute-start.5 = (f32[32,512]{1,0:T(8,128)S(1)}, f32[32,512]{1,0:T(8,128)S(1)}, u32[]{:S(2)}, u32[]{:S(2)}) collective-permute-start(f32[32,512]{1,0:T(8,128)S(1)} %get-tuple-element.24), channel_id=1, source_target_pairs={{0,1},{1,0},{2,3},{3,2},{4,5},{5,4},{6,7},{7,6},{8,9},{9,8},{10,11... | collective-permute-start | bytes 196616 | tf_op jit(solution)/shard_map/ppermute | solution.py:231
  22.4 4.0 %collective-permute-start.6 = (bf16[32,512]{1,0:T(8,128)(2,1)S(1)}, bf16[32,512]{1,0:T(8,128)(2,1)S(1)}, u32[]{:S(2)}, u32[]{:S(2)}) collective-permute-start(bf16[32,512]{1,0:T(8,128)(2,1)S(1)} %get-tuple-element.25), channel_id=1, source_target_pairs={{0,2},{1,3},{2,0},{3,1},{4,6},{5,7},{6,4},{7,5},{8,10},{9,11},{10,... | collective-permute-start | bytes 98312 | tf_op jit(solution)/shard_map/ppermute | solution.py:231
  24.0 3.3 %collective-permute-start.7 = (bf16[32,512]{1,0:T(8,128)(2,1)S(1)}, bf16[32,512]{1,0:T(8,128)(2,1)S(1)}, u32[]{:S(2)}, u32[]{:S(2)}) collective-permute-start(bf16[32,512]{1,0:T(8,128)(2,1)S(1)} %get-tuple-element.26), channel_id=1, source_target_pairs={{0,3},{1,2},{2,1},{3,0},{4,7},{5,6},{6,5},{7,4},{8,11},{9,10},{10,... | collective-permute-start | bytes 98312 | tf_op jit(solution)/shard_map/ppermute | solution.py:231
